TPU v7x, 256 devices: a whole 4x4x8 slice. The times are simulated.
256 devices in a mesh: leaf: 32 (over z_lo, x, core), seq: 8 (over z_hi, y).
Axes of the slice: x: 4, y: 4, z: 8 (z_hi: 2, z_lo: 4; z = z_hi * 4 + z_lo), core: 2. Of those that a mesh axis runs over, the one named last changes fastest.
Arguments:
- latents: bfloat16 [32, 16, 128, 1024], P('leaf', 'seq'), may hold values from -6 to 6
- keyframes: bfloat16 [32, 128, 1024], P('leaf', 'seq'), may hold values from -6 to 6
- key_index: int32 [32, 2], P('leaf'), may hold values from 0 to 31
- timesteps: int32 [2], replicated, may hold values from 0 to 999
- mod_weight: bfloat16 [256, 2048], replicated, may hold values from -0.375 to 0.375
- norm_gain: float32 [1024], replicated, may hold values from 0.5 to 1.5
- qkv_weight: bfloat16 [1024, 3072], replicated, may hold values from -0.1875 to 0.1875
- query_gain: float32 [64], replicated, may hold values from 1 to 2
- key_gain: float32 [64], replicated, may hold values from 1 to 2
- out_weight: bfloat16 [1024, 1024], replicated, may hold values from -0.75 to 0.75
Outputs:
- denoised: bfloat16 [32, 16, 128, 1024], P('leaf', 'seq')
All inputs are finite; a program needn't handle non-finite values.
Results may differ from a plain program's by a relative error of at most 0.009.
Values may be sent and summed in bfloat16 or wider, within the bound.
No kernel may reach another device: no remote copies, remote signals or barrier semaphores. Data moves between devices by JAX's collectives and lax.ppermute only.
A program may use at most 128 MiB of HBM per device.

v0:
```python
import math

import jax
import jax.numpy as jnp
from jax import lax
from jax.sharding import PartitionSpec as P

HEADS = 16
HEAD = 64
TEMB = 256
TSTEPS = 1000


def head_norm(values, gain):
    return values * lax.rsqrt(jnp.mean(values * values, axis=-1, keepdims=True) + 1e-06) * gain


def body(
    latents,
    keyframes,
    key_index,
    timesteps,
    mod_weight,
    norm_gain,
    qkv_weight,
    query_gain,
    key_gain,
    out_weight,
):
    seq_count = lax.axis_size("seq")
    seq_place = lax.axis_index("seq")
    frame_rows = latents.shape[1]
    frame_tokens = latents.shape[2]
    width = latents.shape[3]
    row_count = frame_rows * frame_tokens
    all_frames = frame_rows * seq_count
    halfway = TEMB // 2
    freqs = jnp.exp(-math.log(10000.0) * jnp.arange(halfway, dtype=jnp.float32) / halfway)
    angles = timesteps[1].astype(jnp.float32) * freqs
    embed = jnp.concatenate([jnp.sin(angles), jnp.cos(angles)]).astype(jnp.bfloat16)
    modulation = jnp.dot(embed[None, :], mod_weight, preferred_element_type=jnp.float32)[0]
    scale = modulation[:width]
    shift = modulation[width:]
    key_weight = 1.0 - timesteps[0].astype(jnp.float32) / (2.0 * TSTEPS)
    chosen_pair = key_index[0]
    piece = lax.all_gather(keyframes, "leaf", axis=0, tiled=True)
    offsets = jnp.arange(piece.shape[0], dtype=jnp.int32)
    select = (chosen_pair[:, None] == offsets[None, :]).astype(jnp.float32)
    chosen = jnp.einsum("kn,ntd->ktd", select, piece.astype(jnp.float32))
    both_keys = lax.all_gather(chosen.astype(jnp.bfloat16), "seq", axis=1, tiled=True).astype(
        jnp.float32
    )
    frame_ids = seq_place * frame_rows + jnp.arange(frame_rows, dtype=jnp.int32)
    ramp = frame_ids.astype(jnp.float32) / max(all_frames - 1, 1)
    blend = (1.0 - ramp)[:, None, None] * both_keys[0][None] + ramp[:, None, None] * both_keys[1][
        None
    ]
    resid = (latents[0].astype(jnp.float32) + key_weight * blend).reshape(row_count, width)
    mean = jnp.mean(resid, axis=-1, keepdims=True)
    var = jnp.mean((resid - mean) ** 2, axis=-1, keepdims=True)
    normed = ((resid - mean) * lax.rsqrt(var + 1e-06) * norm_gain * (1.0 + scale) + shift).astype(
        jnp.bfloat16
    )
    qkv = jnp.dot(normed, qkv_weight, preferred_element_type=jnp.float32).reshape(
        row_count, 3, HEADS, HEAD
    )
    queries = head_norm(qkv[:, 0], query_gain).astype(jnp.bfloat16)
    keys_local = head_norm(qkv[:, 1], key_gain).astype(jnp.bfloat16)
    values = qkv[:, 2].astype(jnp.bfloat16)
    factor = HEAD ** (-0.5)
    key_piece = lax.all_gather(keys_local, "seq", axis=0, tiled=True)
    value_piece = lax.all_gather(values, "seq", axis=0, tiled=True)
    scores = (
        jnp.einsum("qhd,khd->hqk", queries, key_piece, preferred_element_type=jnp.float32) * factor
    )
    weights = jnp.exp(scores)
    summed = jnp.sum(weights, axis=-1).T
    mixed = jnp.einsum(
        "hqk,khd->qhd",
        weights.astype(jnp.bfloat16),
        value_piece,
        preferred_element_type=jnp.float32,
    )
    mixed, summed = (mixed, summed)
    attended = (mixed / summed[:, :, None]).astype(jnp.bfloat16)
    flat = attended.reshape(row_count, width)
    output = resid + jnp.dot(flat, out_weight, preferred_element_type=jnp.float32)
    return output.astype(jnp.bfloat16).reshape(1, frame_rows, frame_tokens, width)


def solution(mesh):
    in_specs = (
        P("leaf", "seq", None, None),
        P("leaf", "seq", None),
        P("leaf", None),
        P(),
        P(),
        P(),
        P(),
        P(),
        P(),
        P(),
    )
    out_specs = P("leaf", "seq", None, None)
    return jax.shard_map(body, mesh=mesh, in_specs=in_specs, out_specs=out_specs, check_vma=False)
```

profile of v0, /device:TPU:2, one launch (start us, length us, event | category | flops | bytes accessed | tf_op | source)
XLA Modules:
  0.0 372.0 jit_solution(4931087563981557008)
XLA Ops:
  6.5 0.0 copy-start
  6.5 0.0 all-gather.5.cloned.1.call-start
  6.5 0.7 all-gather.5.cloned.1.call-update
  7.3 0.0 all-gather.7.cloned.1.call-start
  7.3 1.3 fusion.30
  9.9 0.1 cosine_convert_fusion
  10.0 0.0 copy-start.4
  10.0 0.0 copy-start.7
  10.0 8.7 %copy.16 = bf16[1024,3072]{0,1:T(8,128)(2,1)} copy(bf16[1024,3072]{1,0:T(8,128)(2,1)} %param.16) | data formatting | bytes 12582912 | tf_op args[6]
  18.8 0.0 copy-done.4
  18.8 0.2 fusion.31
  19.0 51.7 %all-gather.5.cloned.1.call-done = bf16[32,16,1024]{2,1,0:T(8,128)(2,1)} async-done(((bf16[1,16,1024]{2,1,0:T(8,128)(2,1)}), bf16[32,16,1024]{2,1,0:T(8,128)(2,1)}) %all-gather.5.cloned.1.call-update) | async-done | bytes 1048592 | tf_op jit(solution)/shard_map/all_gather | solution.py:46
  70.7 0.0 copy-done.7
  70.7 2.4 convolution_convert_fusion
  73.2 0.0 copy-start.5
  73.2 44.9 %all_gather.13 = bf16[2,128,1024]{2,0,1:T(2,128)(2,1)S(1)} all-gather(bf16[2,16,1024]{2,0,1:T(2,128)(2,1)S(1)} %convolution_convert_fusion), channel_id=1, replica_groups=mesh['leaf'=32,'seq'=8] {'seq'}, dimensions={1}, use_global_device_ids=true | all-gather | bytes 589824 | tf_op jit(solution)/shard_map/all_gather | solution.py:50
  118.1 0.7 fusion.29
  118.8 0.0 copy-start.2
  118.8 0.2 copy_bitcast_fusion
  119.1 1.6 fusion.28
  120.6 0.3 multiply_reduce_fusion.2
  120.9 0.0 copy-done.5
  120.9 0.3 add_convert_fusion
  121.2 0.6 copy-done.2
  121.8 0.0 copy-start.8
  121.8 1.8 fusion.32
  123.6 0.0 copy-start.1
  123.6 0.0 copy-start.6
  123.6 0.2 multiply_reduce_fusion.1
  123.9 1.4 copy-done.1
  125.3 0.0 copy-done.8
  125.3 1.1 multiply_convert_fusion
  126.3 0.0 all-gather.7.cloned.1.call-update
  126.3 0.2 all-gather.9.cloned.1.call-start
  126.6 2.1 slice.58
  128.7 0.0 all-gather.9.cloned.1.call-update
  128.7 0.1 broadcast_bitcast_fusion
  128.8 2.3 fusion.14
  131.0 106.4 %all-gather.7.cloned.1.call-done = bf16[2048,16,64]{0,2,1:T(8,128)(2,1)} async-done(((bf16[256,16,64]{0,2,1:T(8,128)(2,1)}), bf16[2048,16,64]{0,2,1:T(8,128)(2,1)}) %all-gather.7.cloned.1.call-update) | async-done | bytes 4194320 | tf_op jit(solution)/shard_map/all_gather | solution.py:71
  237.5 0.0 copy-done.6
  237.5 16.2 %fusion = (f32[16,256]{1,0:T(8,128)S(1)}, f32[16,256,2048]{2,1,0:T(8,128)}) fusion(bf16[2048,16,64]{0,2,1:T(8,128)(2,1)} %all-gather.7.cloned.1.call-done, f32[256,3,16,64]{0,3,2,1:T(8,128)} %copy-done.1, f32[64]{0:T(128)S(1)} %copy-done.6, f32[256,16]{0,1:T(8,128)S(1)} %add_rsqrt_fusion.1), kind=kOutput, calls=%fused_computation.1 | convolution fusion | flops 1091301376 | bytes 38830336 | tf_op jit(solution)/shard_map/qhd,khd->hqk/dot_general | solution.py:74
  253.7 93.5 %all-gather.9.cloned.1.call-done = bf16[2048,1,16,64]{0,3,2,1:T(8,128)(2,1)} async-done(((bf16[256,1,16,64]{0,3,2,1:T(8,128)(2,1)}), bf16[2048,1,16,64]{0,3,2,1:T(8,128)(2,1)}) %all-gather.9.cloned.1.call-update) | async-done | bytes 4194320 | tf_op jit(solution)/shard_map/all_gather | solution.py:72
  347.2 0.0 copy-start.3
  347.2 15.7 %divide_convert_fusion = bf16[256,16,64]{0,2,1:T(8,128)(2,1)} fusion(f32[16,256,2048]{2,1,0:T(8,128)} %get-tuple-element.16, bf16[2048,1,16,64]{0,3,2,1:T(8,128)(2,1)} %all-gather.9.cloned.1.call-done, f32[256,16]{0,1:T(8,128)S(1)} %bitcast.76), kind=kOutput, calls=%fused_computation.19 | convolution fusion | flops 1091043328 | bytes 38289408 | tf_op jit(solution)/shard_map/hqk,khd->qhd/dot_general | solution.py:78
  362.9 0.0 copy-done
  362.9 0.0 copy-done.3
  362.9 2.6 fusion.11
  (9 shorter events, 0.1 us)
Async XLA Ops:
  6.5 356.4 %copy-start = (bf16[1024,1024]{1,0:T(8,128)(2,1)S(1)}, bf16[1024,1024]{1,0:T(8,128)(2,1)}, u32[]{:S(2)}) copy-start(bf16[1024,1024]{1,0:T(8,128)(2,1)} %param.19) | copy-start | bytes 6291460
  6.5 64.2 %all-gather.5.cloned.1.call-start = ((), (), s32[]{:S(2)}) async-start(), calls=%async_computation | async-start | bytes 1081344 | tf_op jit(solution)/shard_map/all_gather | solution.py:46
  7.3 230.2 %all-gather.7.cloned.1.call-start = ((), (), s32[]{:S(2)}) async-start(), calls=%async_computation.1 | async-start | bytes 4718592 | tf_op jit(solution)/shard_map/all_gather | solution.py:71
  10.0 8.8 %copy-start.4 = (bf16[256,2048]{1,0:T(8,128)(2,1)S(1)}, bf16[256,2048]{1,0:T(8,128)(2,1)}, u32[]{:S(2)}) copy-start(bf16[256,2048]{1,0:T(8,128)(2,1)} %param.14) | copy-start | bytes 3145732
  10.0 60.7 %copy-start.7 = (s32[1,2]{1,0:T(1,128)S(1)}, s32[1,2]{1,0:T(1,128)}, u32[]{:S(2)}) copy-start(s32[1,2]{1,0:T(1,128)} %param.12) | copy-start | bytes 28
  73.2 47.7 %copy-start.5 = (f32[1024]{0:T(1024)S(1)}, f32[1024]{0:T(1024)}, u32[]{:S(2)}) copy-start(f32[1024]{0:T(1024)} %param.15) | copy-start | bytes 12292
  118.8 2.9 copy-start.2
  121.8 3.5 copy-start.8
  123.6 1.6 copy-start.1
  123.6 113.8 %copy-start.6 = (f32[64]{0:T(128)S(1)}, f32[64]{0:T(128)}, u32[]{:S(2)}) copy-start(f32[64]{0:T(128)} %param.17) | copy-start | bytes 772
  126.3 220.9 %all-gather.9.cloned.1.call-start = ((), (), s32[]{:S(2)}) async-start(), calls=%async_computation.2 | async-start | bytes 4718592 | tf_op jit(solution)/shard_map/all_gather | solution.py:72
  347.2 15.7 %copy-start.3 = (f32[256,1024]{1,0:T(8,128)S(1)}, f32[256,1024]{1,0:T(8,128)}, u32[]{:S(2)}) copy-start(f32[256,1024]{1,0:T(8,128)} %fusion.14) | copy-start | bytes 3145732
Sparse Core Ops, SparseCore 0:
  9.2 61.4 all-gather.4
  126.5 110.9 all-gather.6
  240.0 107.1 all-gather.8
where the time goes:
time: 373 us; the launch traced here: 372 us
  waiting for transfers between devices  252 us (68%)
  blocking collectives  44.9 us (12%)
  matrix products  39 us (10%)
  local copies, waits for them, and re-layouts  15.1 us (4%)
  between operations  14.5 us (4%)
  other arithmetic  5.8 us (2%)
    all_gather x1, waiting for transfers between devices, body(): key_piece = lax.all_gather(keys_local, 'seq', axis=0, tiled=True)  106 us
    all_gather x1, waiting for transfers between devices, body(): value_piece = lax.all_gather(values, 'seq', axis=0, tiled=True)  93.5 us
    all_gather x1, waiting for transfers between devices, body(): piece = lax.all_gather(keyframes, 'leaf', axis=0, tiled=True)  51.7 us
    all_gather x1, blocking collectives, body(): lax.all_gather(chosen.astype(jnp.bfloat16), 'seq', axis=1, tiled=True)  44.9 us
    dot_general x1, matrix products, body(): jnp.einsum('qhd,khd->hqk', queries, key_piece, preferred_element_type=jnp...  16.2 us
    dot_general x1, matrix products, body(): jnp.einsum('hqk,khd->qhd', weights.astype(jnp.bfloat16), value_piece, pre...  15.7 us
    unnamed x20, local copies, waits for them, and re-layouts  10.9 us
  transfers between devices with their start and end apart: 3, of which 3 were waited for; matrix products, arithmetic and copies ran while one was open for 8% of the time, Pallas kernels for 0%

commit v1 on v0

v1 whole, which is shorter than its diff:
```python
import functools
import math

import jax
import jax.numpy as jnp
from jax import lax
from jax.experimental import pallas as pl
from jax.experimental.pallas import tpu as pltpu
from jax.sharding import PartitionSpec as P

HEADS = 16
HEAD = 64
TEMB = 256
TSTEPS = 1000
D = 1024
FRAMES = 16
TOKF = 128
AXES = ("leaf", "seq")
ZL, X, CORE, ZH, Y = 4, 4, 2, 2, 4
ROWS = 256
PIECE = 16
PAIRS = HEADS // 2
F32 = jnp.float32
BF16 = jnp.bfloat16
QSCALE = HEAD ** (-0.5) * math.log2(math.e)


def moves(zl=0, x=0, core=0, zh=0, y=0):
    pairs = []
    for i in range(ZL * X * CORE * ZH * Y):
        rest, iy = divmod(i, Y)
        rest, izh = divmod(rest, ZH)
        rest, ic = divmod(rest, CORE)
        izl, ix = divmod(rest, X)
        izl, ix, ic = (izl + zl) % ZL, (ix + x) % X, (ic + core) % CORE
        izh, iy = (izh + zh) % ZH, (iy + y) % Y
        pairs.append((i, (((izl * X + ix) * CORE + ic) * ZH + izh) * Y + iy))
    return pairs


def send(value, **step):
    return lax.ppermute(value, AXES, moves(**step))


def dot(a, b):
    return jnp.dot(a, b, preferred_element_type=F32)


def dot_t(a, b):
    return lax.dot_general(a, b, (((1,), (1,)), ((), ())), preferred_element_type=F32)


def blend_tables(kw, piece_refs, base_ref, first_s, diff_s):
    for i, piece in enumerate(piece_refs):
        for z in range(ZH):
            base = pl.multiple_of(base_ref[i * ZH + z], PIECE)
            first = piece[z, 0].astype(F32) * kw
            last = piece[z, 1].astype(F32) * kw
            first_s[pl.ds(base, PIECE), :] = first
            diff_s[pl.ds(base, PIECE), :] = last - first


def norm_chunk(lat_ref, ramps, first_s, diff_s, gain_ref, shift_ref, x_s):
    step = 32

    def rows(i, carry):
        r = pl.multiple_of(i * step, step)
        tok = pl.multiple_of(lax.rem(i, TOKF // step) * step, step)
        ramp = jnp.where(i < TOKF // step, ramps[0], ramps[1])
        resid = lat_ref[pl.ds(r, step), :].astype(F32) + (
            first_s[pl.ds(tok, step), :] + ramp * diff_s[pl.ds(tok, step), :]
        )
        mean = jnp.mean(resid, axis=-1, keepdims=True)
        cent = resid - mean
        var = jnp.mean(cent * cent, axis=-1, keepdims=True)
        normed = cent * lax.rsqrt(var + 1e-06) * gain_ref[...] + shift_ref[...]
        x_s[pl.ds(r, step), :] = normed.astype(BF16)
        return carry

    lax.fori_loop(0, ROWS // step, rows, 0, unroll=2)


def head_norm_t(block, gain):
    heads = block.reshape(block.shape[0] // HEAD, HEAD, block.shape[1])
    mean = jnp.mean(heads * heads, axis=1, keepdims=True)
    return (heads * lax.rsqrt(mean + 1e-06) * gain[None]).reshape(block.shape)


def keys_values(j, x_s, wk_ref, wv_ref, kgain_ref, kt_s, v_s):
    def block(i, carry):
        f = pl.multiple_of(i * 256, 256)
        kt = dot_t(wk_ref[pl.ds(f, 256), :], x_s[...])
        kt_s[pl.ds(f, 256), j * ROWS : (j + 1) * ROWS] = head_norm_t(kt, kgain_ref[...]).astype(BF16)
        v = dot(x_s[...], wv_ref[:, pl.ds(f, 256)])
        v_s[j * ROWS : (j + 1) * ROWS, pl.ds(f, 256)] = v.astype(BF16)
        return carry

    lax.fori_loop(0, D // 256, block, 0)


def attend(q_ref, kt_s, v_s, acc_in, acc_out):
    lane_q = lax.broadcasted_iota(jnp.int32, (ROWS, 128), 1) < HEAD
    nkeys = kt_s.shape[1]
    lane_v = lax.broadcasted_iota(jnp.int32, (nkeys, 128), 1) < HEAD

    def pair(p, carry):
        f = pl.multiple_of(p * 128, 128)
        qp = q_ref[:, pl.ds(f, 128)]
        vp = v_s[:, pl.ds(f, 128)]
        one = jnp.ones((), BF16)
        zero = jnp.zeros((), BF16)
        for odd in range(2):
            keep = lane_q if odd == 0 else jnp.logical_not(lane_q)
            qh = jnp.where(keep, qp, zero)
            keepv = lane_v if odd == 0 else jnp.logical_not(lane_v)
            vh = jnp.where(keepv, vp, one)
            total = None
            for b in range(nkeys // 256):
                s = dot(qh, kt_s[pl.ds(f, 128), b * 256 : (b + 1) * 256])
                w = jnp.exp2(s).astype(BF16)
                o = dot(w, vh[b * 256 : (b + 1) * 256])
                total = o if total is None else total + o
            if acc_in is not None:
                total = total + acc_in[2 * p + odd]
            acc_out[2 * p + odd] = total
        return carry

    lax.fori_loop(0, PAIRS, pair, 0)


def first_kernel(
    fl_ref, base_ref, l0, l1, l2, l3, p0, p1, p2, p3, gain_ref, shift_ref, wq_ref, wk_ref, wv_ref,
    qgain_ref, kgain_ref, acc_ref, q_ref, first_s, diff_s, x_s, kt_s, v_s,
):
    blend_tables(fl_ref[0], (p0, p1, p2, p3), base_ref, first_s, diff_s)
    for j, lat in enumerate((l0, l1, l2, l3)):
        ramps = (fl_ref[1 + 2 * j], fl_ref[2 + 2 * j])
        norm_chunk(lat, ramps, first_s, diff_s, gain_ref, shift_ref, x_s)
        if j == 0:
            def block(i, carry):
                f = pl.multiple_of(i * 256, 256)
                qt = dot_t(wq_ref[pl.ds(f, 256), :], x_s[...])
                q = head_norm_t(qt, qgain_ref[...])
                q_ref[:, pl.ds(f, 256)] = q.T.astype(BF16)
                return carry

            lax.fori_loop(0, D // 256, block, 0)
        keys_values(j, x_s, wk_ref, wv_ref, kgain_ref, kt_s, v_s)
    attend(q_ref, kt_s, v_s, None, acc_ref)


def second_kernel(
    fl_ref, base_ref, own, l0, l1, l2, l3, p0, p1, p2, p3, gain_ref, shift_ref, wk_ref, wv_ref,
    kgain_ref, wo_ref, q_ref, acc_ref, out_ref, first_s, diff_s, x_s, kt_s, v_s, acc_s,
):
    blend_tables(fl_ref[0], (p0, p1, p2, p3), base_ref, first_s, diff_s)
    for j, lat in enumerate((l0, l1, l2, l3)):
        ramps = (fl_ref[1 + 2 * j], fl_ref[2 + 2 * j])
        norm_chunk(lat, ramps, first_s, diff_s, gain_ref, shift_ref, x_s)
        keys_values(j, x_s, wk_ref, wv_ref, kgain_ref, kt_s, v_s)
    attend(q_ref, kt_s, v_s, acc_ref, acc_s)

    lane = lax.broadcasted_iota(jnp.int32, (ROWS, 128), 1) < HEAD
    for p in range(PAIRS):
        even = acc_s[2 * p]
        odd = acc_s[2 * p + 1]
        num = jnp.where(lane, even, odd)
        den = pltpu.roll(jnp.where(lane, odd, even), HEAD, 1)
        x_s[:, p * 128 : (p + 1) * 128] = (num / den).astype(BF16)

    def block(i, carry):
        f = pl.multiple_of(i * 256, 256)
        o = dot(x_s[...], wo_ref[:, pl.ds(f, 256)])
        for k in range(2):
            r = slice(k * TOKF, (k + 1) * TOKF)
            resid = own[r, pl.ds(f, 256)].astype(F32) + (
                first_s[:, pl.ds(f, 256)] + fl_ref[9 + k] * diff_s[:, pl.ds(f, 256)]
            )
            out_ref[r, pl.ds(f, 256)] = (resid + o[r]).astype(BF16)
        return carry

    lax.fori_loop(0, D // 256, block, 0)


VMEM = pl.BlockSpec(memory_space=pltpu.VMEM)
SMEM = pl.BlockSpec(memory_space=pltpu.SMEM)


def scratch():
    return [
        pltpu.VMEM((TOKF, D), F32),
        pltpu.VMEM((TOKF, D), F32),
        pltpu.VMEM((ROWS, D), BF16),
        pltpu.VMEM((D, Y * ROWS), BF16),
        pltpu.VMEM((Y * ROWS, D), BF16),
    ]


def body(
    latents, keyframes, key_index, timesteps, mod_weight, norm_gain, qkv_weight, query_gain,
    key_gain, out_weight,
):
    place = lax.axis_index("leaf")
    seq = lax.axis_index("seq")
    zl, x, core = place // (X * CORE), place // CORE % X, place % CORE
    zh, y = seq // Y, seq % Y

    own = latents.reshape(ROWS, D)
    mine = keyframes[0]
    by_zl = [mine] + [send(mine, zl=k) for k in (1, 2, 3)]
    by_zl = jnp.stack(by_zl)
    near = [own] + [send(own, y=k) for k in (1, 2, 3)]
    by_x = jnp.stack([by_zl] + [send(by_zl, x=k) for k in (1, 2, 3)])
    by_core = jnp.stack([by_x, send(by_x, core=1)])
    pair = key_index[0]
    pick_zl = (zl - pair // (X * CORE)) % ZL
    pick_x = (x - pair // CORE % X) % X
    pick_c = (core + pair) % CORE
    pick = (pick_c * X + pick_x) * ZL + pick_zl
    flat = by_core.reshape(CORE * X * ZL, PIECE, D)
    chosen = jnp.stack([
        lax.dynamic_index_in_dim(flat, pick[0], 0, keepdims=False),
        lax.dynamic_index_in_dim(flat, pick[1], 0, keepdims=False),
    ])
    both = jnp.stack([chosen, send(chosen, zh=1)])
    pieces = [both] + [send(both, y=k) for k in (1, 2, 3)]
    cross = send(own, zh=1)
    far = [cross] + [send(cross, y=k) for k in (1, 2, 3)]

    halfway = TEMB // 2
    freqs = jnp.exp(-math.log(10000.0) * jnp.arange(halfway, dtype=F32) / halfway)
    angles = timesteps[1].astype(F32) * freqs
    embed = jnp.concatenate([jnp.sin(angles), jnp.cos(angles)]).astype(BF16)
    modulation = jnp.dot(embed[None, :], mod_weight, preferred_element_type=F32)
    gain = norm_gain[None, :] * (1.0 + modulation[:, :D])
    shift = modulation[:, D:]
    kw = 1.0 - timesteps[0].astype(F32) / (2.0 * TSTEPS)

    wq = qkv_weight[:, :D].T
    wk = qkv_weight[:, D : 2 * D].T
    wv = qkv_weight[:, 2 * D :]
    qgain = (query_gain * QSCALE)[:, None]
    kgain = key_gain[:, None]

    steps = jnp.arange(Y, dtype=jnp.int32)
    from_y = (y - steps) % Y
    two = jnp.arange(2, dtype=jnp.int32)

    def ramps(plane):
        frames = (plane * Y + from_y)[:, None] * 2 + two[None, :]
        return (frames.astype(F32) / (FRAMES - 1)).reshape(-1)

    planes = jnp.stack([zh, 1 - zh])
    base = ((planes[None, :] * Y + from_y[:, None]) * PIECE).reshape(-1).astype(jnp.int32)
    near_ramps, far_ramps = ramps(zh), ramps(1 - zh)
    fl_near = jnp.concatenate([kw[None], near_ramps])
    fl_far = jnp.concatenate([kw[None], far_ramps, near_ramps[:2]])

    flops = 2 * 1024 * 1024 * 2048 + 4 * 16 * 256 * 1024 * 128
    params = pltpu.CompilerParams(vmem_limit_bytes=48 * 1024 * 1024)
    acc, q = pl.pallas_call(
        first_kernel,
        out_shape=(
            jax.ShapeDtypeStruct((HEADS, ROWS, 128), F32),
            jax.ShapeDtypeStruct((ROWS, D), BF16),
        ),
        in_specs=[SMEM, SMEM] + [VMEM] * 15,
        out_specs=(VMEM, VMEM),
        scratch_shapes=scratch(),
        compiler_params=params,
        cost_estimate=pl.CostEstimate(flops=flops, bytes_accessed=12 << 20, transcendentals=4 << 20),
        name="near_keys",
    )(fl_near, base, *near, *pieces, gain, shift, wq, wk, wv, qgain, kgain)
    out = pl.pallas_call(
        second_kernel,
        out_shape=jax.ShapeDtypeStruct((ROWS, D), BF16),
        in_specs=[SMEM, SMEM] + [VMEM] * 17,
        out_specs=VMEM,
        scratch_shapes=scratch() + [pltpu.VMEM((HEADS, ROWS, 128), F32)],
        compiler_params=params,
        cost_estimate=pl.CostEstimate(flops=flops, bytes_accessed=12 << 20, transcendentals=4 << 20),
        name="far_keys",
    )(fl_far, base, own, *far, *pieces, gain, shift, wk, wv, kgain, out_weight, q, acc)
    return out.reshape(latents.shape)


def solution(mesh):
    in_specs = (
        P("leaf", "seq", None, None),
        P("leaf", "seq", None),
        P("leaf", None),
        P(),
        P(),
        P(),
        P(),
        P(),
        P(),
        P(),
    )
    out_specs = P("leaf", "seq", None, None)
    return jax.shard_map(body, mesh=mesh, in_specs=in_specs, out_specs=out_specs, check_vma=False)
```

time: 373 us -> 127 us (0.34)
  waiting for transfers between devices: 252 us -> 16.4 us
  Pallas kernels: 0 us -> 51.3 us
  blocking collectives: 44.9 us -> 0 us
  matrix products: 39 us -> 0.25 us
  starting transfers between devices: 0.26 us -> 31.4 us
  between operations: 14.5 us -> 5.25 us
    all_gather x3 -> x0, waiting for transfers between devices: 252 us -> none  [the longest x1 106 us: body(): key_piece = lax.all_gather(keys_local, 'seq', axis=0, tiled=True)]
    pallas_call x0 -> x2, Pallas kernels: none -> 51.3 us  [the longest x1 25.9 us: body(): pl.pallas_call(second_kernel, out_shape=jax.ShapeDtypeStruct((ROWS, D), B...]
    all_gather x1 -> x0, blocking collectives: 44.9 us -> none  [body(): lax.all_gather(chosen.astype(jnp.bfloat16), 'seq', axis=1, tiled=True)]
    dot_general x6 -> x1, matrix products: 39 us -> 0.25 us  [body(): modulation = jnp.dot(embed[None, :], mod_weight, preferred_element_type=F32)]
    ppermute x0 -> x18, starting transfers between devices: none -> 31.4 us  [send(): return lax.ppermute(value, AXES, moves(**step))]
    ppermute x0 -> x18, waiting for transfers between devices: none -> 16.4 us  [send(): return lax.ppermute(value, AXES, moves(**step))]
    slice x3 -> x4, local copies, waits for them, and re-layouts: 4.13 us -> 7.59 us  [the longest x1 5.68 us: body(): wq = qkv_weight[:, :D].T]
    unnamed x20 -> x14, local copies, waits for them, and re-layouts: 10.9 us -> 9.34 us
  transfers between devices with their start and end apart: 3 -> 18, of which waited for: 3 -> 2; matrix products, arithmetic and copies ran while one was open for 8% -> 17% of each run, Pallas kernels for 0% -> 20%
where the time goes in v1:
time: 127 us
  Pallas kernels  51.3 us (40%)
  starting transfers between devices  31.4 us (25%)
  local copies, waits for them, and re-layouts  17.4 us (14%)
  waiting for transfers between devices  16.4 us (13%)
  between operations  5.25 us (4%)
  other arithmetic  4.76 us (4%)
    ppermute x18, starting transfers between devices, send(): return lax.ppermute(value, AXES, moves(**step))  31.4 us
    pallas_call x1, Pallas kernels, body(): pl.pallas_call(second_kernel, out_shape=jax.ShapeDtypeStruct((ROWS, D), B...  25.9 us
    pallas_call x1, Pallas kernels, body(): pl.pallas_call(first_kernel, out_shape=(jax.ShapeDtypeStruct((HEADS, ROWS...  25.4 us
    ppermute x18, waiting for transfers between devices, send(): return lax.ppermute(value, AXES, moves(**step))  16.4 us
    unnamed x14, local copies, waits for them, and re-layouts  9.34 us
    slice x1, local copies, waits for them, and re-layouts, body(): wq = qkv_weight[:, :D].T  5.68 us
  transfers between devices with their start and end apart: 18, of which 2 were waited for; matrix products, arithmetic and copies ran while one was open for 17% of the time, Pallas kernels for 20%

profile of v1, /device:TPU:2, one launch (start us, length us, event | category | flops | bytes accessed | tf_op | source)
XLA Modules:
  0.0 126.8 jit_solution(5464434132785517841)
XLA Ops:
  0.0 0.0 copy-start
  0.0 1.9 %collective-permute-start.4 = (bf16[16,1024]{1,0:T(8,128)(2,1)}, bf16[16,1024]{1,0:T(8,128)(2,1)S(1)}, u32[]{:S(2)}, u32[]{:S(2)}) collective-permute-start(bf16[16,1024]{1,0:T(8,128)(2,1)} %bitcast.68), channel_id=1, source_target_pairs={{0,64},{1,65},{2,66},{3,67},{4,68},{5,69},{6,70},{7,71},{8,72},{9,... | collective-permute-start | bytes 98312 | tf_op jit(solution)/shard_map/ppermute | solution.py:42
  1.9 3.3 %collective-permute-start.5 = (bf16[16,1024]{1,0:T(8,128)(2,1)}, bf16[16,1024]{1,0:T(8,128)(2,1)S(1)}, u32[]{:S(2)}, u32[]{:S(2)}) collective-permute-start(bf16[16,1024]{1,0:T(8,128)(2,1)} %bitcast.69), channel_id=1, source_target_pairs={{0,128},{1,129},{2,130},{3,131},{4,132},{5,133},{6,134},{7,135},{8... | collective-permute-start | bytes 98312 | tf_op jit(solution)/shard_map/ppermute | solution.py:42
  5.2 1.0 collective-permute-start.6
  6.2 1.6 %collective-permute-start.15 = (bf16[256,1024]{1,0:T(8,128)(2,1)}, bf16[256,1024]{1,0:T(8,128)(2,1)S(1)}, u32[]{:S(2)}, u32[]{:S(2)}) collective-permute-start(bf16[256,1024]{1,0:T(8,128)(2,1)} %bitcast.56), channel_id=1, source_target_pairs={{0,1},{1,2},{2,3},{3,0},{4,5},{5,6},{6,7},{7,4},{8,9},{9,10},{10,1... | collective-permute-start | bytes 1572872 | tf_op jit(solution)/shard_map/ppermute | solution.py:42
  7.8 2.9 %collective-permute-start.16 = (bf16[256,1024]{1,0:T(8,128)(2,1)}, bf16[256,1024]{1,0:T(8,128)(2,1)S(1)}, u32[]{:S(2)}, u32[]{:S(2)}) collective-permute-start(bf16[256,1024]{1,0:T(8,128)(2,1)} %bitcast.57), channel_id=1, source_target_pairs={{0,2},{1,3},{2,0},{3,1},{4,6},{5,7},{6,4},{7,5},{8,10},{9,11},{10,... | collective-permute-start | bytes 1572872 | tf_op jit(solution)/shard_map/ppermute | solution.py:42
  10.7 0.1 convert_multiply_fusion
  10.8 1.3 %fusion.15 = (s32[1]{0:T(128)}, s32[1]{0:T(128)}) fusion(s32[2]{0:T(128)} %param.13), kind=kLoop, calls=%fused_computation.61 | loop fusion | bytes 16 | tf_op jit(solution)/shard_map/slice | solution.py:232
  12.6 0.1 cosine_convert_fusion
  12.7 0.1 convert_multiply_fusion.1
  12.8 0.1 add_multiply_fusion.1
  12.9 0.1 add_multiply_fusion
  13.0 0.2 fusion.17
  13.2 0.7 fusion.14
  14.0 0.0 collective-permute-done.4
  14.0 0.0 collective-permute-done.5
  14.0 0.0 collective-permute-done.6
  14.0 0.8 fusion.11
  14.8 2.2 %collective-permute-start.8 = (bf16[4,16,1024]{2,1,0:T(8,128)(2,1)S(1)}, bf16[4,16,1024]{2,1,0:T(8,128)(2,1)S(1)}, u32[]{:S(2)}, u32[]{:S(2)}) collective-permute-start(bf16[4,16,1024]{2,1,0:T(8,128)(2,1)S(1)} %get-tuple-element.17), channel_id=1, source_target_pairs={{0,32},{1,33},{2,34},{3,35},{4,36},{5,37},{6,38},{7,39},{8,40},{9,... | collective-permute-start | bytes 393224 | tf_op jit(solution)/shard_map/ppermute | solution.py:42
  17.0 1.4 %collective-permute-start.9 = (bf16[4,16,1024]{2,1,0:T(8,128)(2,1)S(1)}, bf16[4,16,1024]{2,1,0:T(8,128)(2,1)S(1)}, u32[]{:S(2)}, u32[]{:S(2)}) collective-permute-start(bf16[4,16,1024]{2,1,0:T(8,128)(2,1)S(1)} %get-tuple-element.17), channel_id=1, source_target_pairs={{0,48},{1,49},{2,50},{3,51},{4,52},{5,53},{6,54},{7,55},{8,56},{9,... | collective-permute-start | bytes 393224 | tf_op jit(solution)/shard_map/ppermute | solution.py:42
  18.4 0.6 collective-permute-start.7
  19.0 0.7 fusion.2
  19.7 2.0 %collective-permute-done.8 = bf16[4,16,1024]{2,1,0:T(8,128)(2,1)S(1)} collective-permute-done((bf16[4,16,1024]{2,1,0:T(8,128)(2,1)S(1)}, bf16[4,16,1024]{2,1,0:T(8,128)(2,1)S(1)}, u32[]{:S(2)}, u32[]{:S(2)}) %collective-permute-start.8) | collective-permute-done | bytes 131104 | tf_op jit(solution)/shard_map/ppermute | solution.py:42
  21.7 1.3 %collective-permute-start.17 = (bf16[256,1024]{1,0:T(8,128)(2,1)}, bf16[256,1024]{1,0:T(8,128)(2,1)}, u32[]{:S(2)}, u32[]{:S(2)}) collective-permute-start(bf16[256,1024]{1,0:T(8,128)(2,1)} %bitcast.58), channel_id=1, source_target_pairs={{0,3},{1,0},{2,1},{3,2},{4,7},{5,4},{6,5},{7,6},{8,11},{9,8},{10,9... | collective-permute-start | bytes 1572872 | tf_op jit(solution)/shard_map/ppermute | solution.py:42
  23.1 0.0 collective-permute-done.9
  23.1 5.4 %collective-permute-start = (bf16[256,1024]{1,0:T(8,128)(2,1)}, bf16[256,1024]{1,0:T(8,128)(2,1)S(1)}, u32[]{:S(2)}, u32[]{:S(2)}) collective-permute-start(bf16[256,1024]{1,0:T(8,128)(2,1)} %bitcast.59), channel_id=1, source_target_pairs={{0,4},{1,5},{2,6},{3,7},{4,0},{5,1},{6,2},{7,3},{8,12},{9,13},{10,... | collective-permute-start | bytes 1572872 | tf_op jit(solution)/shard_map/ppermute | solution.py:42
  28.5 0.0 collective-permute-done.7
  28.5 0.9 fusion.12
  29.3 0.0 collective-permute-start.10
  29.4 0.6 fusion.16
  33.8 5.7 %fusion.13 = (bf16[1024,1024]{1,0:T(8,128)(2,1)}, bf16[1024,1024]{1,0:T(8,128)(2,1)}, bf16[1024,1024]{1,0:T(8,128)(2,1)}) fusion(bf16[1024,3072]{1,0:T(8,128)(2,1)} %param.16), kind=kLoop, calls=%fused_computation.59 | loop fusion | bytes 12582912 | tf_op jit(solution)/shard_map/slice | solution.py:239
  39.5 0.0 collective-permute-done.10
  39.5 1.1 pad_maximum_fusion
  40.7 0.6 collective-permute-start.11
  41.3 0.1 div.80
  42.0 14.4 %collective-permute-done.11 = bf16[2,16,1024]{2,1,0:T(8,128)(2,1)S(1)} collective-permute-done((bf16[2,16,1024]{2,1,0:T(8,128)(2,1)S(1)}, bf16[2,16,1024]{2,1,0:T(8,128)(2,1)S(1)}, u32[]{:S(2)}, u32[]{:S(2)}) %collective-permute-start.11) | collective-permute-done | bytes 65568 | tf_op jit(solution)/shard_map/ppermute | solution.py:42
  56.5 0.2 collective-permute-start.12
  56.7 0.0 collective-permute-done.15.l1
  56.7 2.7 %collective-permute-start.13 = (bf16[2,2,16,1024]{3,2,1,0:T(8,128)(2,1)S(1)}, bf16[2,2,16,1024]{3,2,1,0:T(8,128)(2,1)}, u32[]{:S(2)}, u32[]{:S(2)}) collective-permute-start(bf16[2,2,16,1024]{3,2,1,0:T(8,128)(2,1)S(1)} %pad_maximum_fusion.3.p0), channel_id=1, source_target_pairs={{0,2},{1,3},{2,0},{3,1},{4,6},{5,7},{6,4},{7,5},{8,10},{9,11},{10,... | collective-permute-start | bytes 393224 | tf_op jit(solution)/shard_map/ppermute | solution.py:42
  59.3 0.0 collective-permute-done.16.l2
  59.4 0.5 collective-permute-start.14
  59.9 0.1 pad_maximum_fusion.7.fl_ref
  59.9 0.1 mul.66.base_ref
  60.0 4.0 %copy.21 = bf16[1024,1024]{0,1:T(8,128)(2,1)} copy(bf16[1024,1024]{1,0:T(8,128)(2,1)} %get-tuple-element.10) | data formatting | bytes 4194304
  64.0 4.0 %copy.22 = bf16[1024,1024]{0,1:T(8,128)(2,1)} copy(bf16[1024,1024]{1,0:T(8,128)(2,1)} %get-tuple-element.9) | data formatting | bytes 4194304
  68.0 0.1 copy.20.kgain_ref
  68.1 0.1 copy.18.qgain_ref
  68.2 0.1 div.64
  68.3 0.1 pad_maximum_fusion.5.fl_ref
  68.4 0.0 collective-permute-done.l0
  68.4 1.7 %collective-permute-start.1 = (bf16[256,1024]{1,0:T(8,128)(2,1)S(1)}, bf16[256,1024]{1,0:T(8,128)(2,1)S(1)}, u32[]{:S(2)}, u32[]{:S(2)}) collective-permute-start(bf16[256,1024]{1,0:T(8,128)(2,1)S(1)} %collective-permute-done.l0), channel_id=1, source_target_pairs={{0,1},{1,2},{2,3},{3,0},{4,5},{5,6},{6,7},{7,4},{8,9},{9,10},{10,1... | collective-permute-start | bytes 1572872 | tf_op jit(solution)/shard_map/ppermute | solution.py:42
  70.1 0.0 collective-permute-done.17.l3
  70.1 1.4 %collective-permute-start.2 = (bf16[256,1024]{1,0:T(8,128)(2,1)S(1)}, bf16[256,1024]{1,0:T(8,128)(2,1)S(1)}, u32[]{:S(2)}, u32[]{:S(2)}) collective-permute-start(bf16[256,1024]{1,0:T(8,128)(2,1)S(1)} %collective-permute-done.l0), channel_id=1, source_target_pairs={{0,2},{1,3},{2,0},{3,1},{4,6},{5,7},{6,4},{7,5},{8,10},{9,11},{10,... | collective-permute-start | bytes 1572872 | tf_op jit(solution)/shard_map/ppermute | solution.py:42
  71.5 0.0 collective-permute-done.12.p1
  71.5 2.5 %collective-permute-start.3 = (bf16[256,1024]{1,0:T(8,128)(2,1)S(1)}, bf16[256,1024]{1,0:T(8,128)(2,1)S(1)}, u32[]{:S(2)}, u32[]{:S(2)}) collective-permute-start(bf16[256,1024]{1,0:T(8,128)(2,1)S(1)} %collective-permute-done.l0), channel_id=1, source_target_pairs={{0,3},{1,0},{2,1},{3,2},{4,7},{5,4},{6,5},{7,6},{8,11},{9,8},{10,9... | collective-permute-start | bytes 1572872 | tf_op jit(solution)/shard_map/ppermute | solution.py:42
  74.1 0.0 collective-permute-done.13.p2
  74.1 0.0 collective-permute-done.14.p3
  74.1 0.0 copy-start.1
  74.1 25.4 %near_keys.1 = (f32[16,256,128]{2,1,0:T(8,128)S(1)}, bf16[256,1024]{1,0:T(8,128)(2,1)S(1)}) custom-call(f32[9]{0:T(128)S(1)} %pad_maximum_fusion.7.fl_ref, s32[8]{0:T(128)S(1)} %mul.66.base_ref, bf16[256,1024]{1,0:T(8,128)(2,1)S(1)} %bitcast.60, bf16[256,1024]{1,0:T(8,128)(2,1)S(1)} %collective-permute-done.15.l1, ...), custom_call_target="tpu_custom_call" | custom-call | flops 6442450944 | bytes 12582912 | tf_op jit(solution)/shard_map/near_keys/pallas_call | solution.py:261
  99.5 1.3 %copy-done.3 = f32[16,256,128]{2,1,0:T(8,128)} copy-done((f32[16,256,128]{2,1,0:T(8,128)}, f32[16,256,128]{2,1,0:T(8,128)S(1)}, u32[]{:S(2)}) %copy-start.3) | copy-done | bytes 2097176
  100.8 0.0 collective-permute-done.1.l1
  100.8 0.0 collective-permute-done.2.l2
  100.8 0.0 collective-permute-done.3.l3
  100.9 25.9 %far_keys.1 = bf16[256,1024]{1,0:T(8,128)(2,1)} custom-call(f32[11]{0:T(128)S(1)} %pad_maximum_fusion.5.fl_ref, s32[8]{0:T(128)S(1)} %mul.66.base_ref, bf16[256,1024]{1,0:T(8,128)(2,1)S(1)} %bitcast.61, bf16[256,1024]{1,0:T(8,128)(2,1)S(1)} %collective-permute-done.l0, bf16[256,1024]{1,0:T(8,128)(2,1)S(1)} %collective-permute-done.1.l1, ...), custom_call_target="tpu_custom_call" | custom-call | flops 6442450944 | bytes 12582912 | tf_op jit(solution)/shard_map/far_keys/pallas_call | solution.py:274
  (18 shorter events, 0.1 us)
Async XLA Ops:
  0.0 13.0 %copy-start = (bf16[256,2048]{1,0:T(8,128)(2,1)S(1)}, bf16[256,2048]{1,0:T(8,128)(2,1)}, u32[]{:S(2)}) copy-start(bf16[256,2048]{1,0:T(8,128)(2,1)} %param.14) | copy-start | bytes 3145732
  0.0 14.0 %collective-permute-start.4 = (bf16[16,1024]{1,0:T(8,128)(2,1)}, bf16[16,1024]{1,0:T(8,128)(2,1)S(1)}, u32[]{:S(2)}, u32[]{:S(2)}) collective-permute-start(bf16[16,1024]{1,0:T(8,128)(2,1)} %bitcast.68), channel_id=1, source_target_pairs={{0,64},{1,65},{2,66},{3,67},{4,68},{5,69},{6,70},{7,71},{8,72},{9,... | collective-permute-start | bytes 98312 | tf_op jit(solution)/shard_map/ppermute | solution.py:42
  1.9 12.1 %collective-permute-start.5 = (bf16[16,1024]{1,0:T(8,128)(2,1)}, bf16[16,1024]{1,0:T(8,128)(2,1)S(1)}, u32[]{:S(2)}, u32[]{:S(2)}) collective-permute-start(bf16[16,1024]{1,0:T(8,128)(2,1)} %bitcast.69), channel_id=1, source_target_pairs={{0,128},{1,129},{2,130},{3,131},{4,132},{5,133},{6,134},{7,135},{8... | collective-permute-start | bytes 98312 | tf_op jit(solution)/shard_map/ppermute | solution.py:42
  5.2 8.8 %collective-permute-start.6 = (bf16[16,1024]{1,0:T(8,128)(2,1)}, bf16[16,1024]{1,0:T(8,128)(2,1)S(1)}, u32[]{:S(2)}, u32[]{:S(2)}) collective-permute-start(bf16[16,1024]{1,0:T(8,128)(2,1)} %bitcast.70), channel_id=1, source_target_pairs={{0,192},{1,193},{2,194},{3,195},{4,196},{5,197},{6,198},{7,199},{8... | collective-permute-start | bytes 98312 | tf_op jit(solution)/shard_map/ppermute | solution.py:42
  6.2 50.5 %collective-permute-start.15 = (bf16[256,1024]{1,0:T(8,128)(2,1)}, bf16[256,1024]{1,0:T(8,128)(2,1)S(1)}, u32[]{:S(2)}, u32[]{:S(2)}) collective-permute-start(bf16[256,1024]{1,0:T(8,128)(2,1)} %bitcast.56), channel_id=1, source_target_pairs={{0,1},{1,2},{2,3},{3,0},{4,5},{5,6},{6,7},{7,4},{8,9},{9,10},{10,1... | collective-permute-start | bytes 1572872 | tf_op jit(solution)/shard_map/ppermute | solution.py:42
  7.8 51.6 %collective-permute-start.16 = (bf16[256,1024]{1,0:T(8,128)(2,1)}, bf16[256,1024]{1,0:T(8,128)(2,1)S(1)}, u32[]{:S(2)}, u32[]{:S(2)}) collective-permute-start(bf16[256,1024]{1,0:T(8,128)(2,1)} %bitcast.57), channel_id=1, source_target_pairs={{0,2},{1,3},{2,0},{3,1},{4,6},{5,7},{6,4},{7,5},{8,10},{9,11},{10,... | collective-permute-start | bytes 1572872 | tf_op jit(solution)/shard_map/ppermute | solution.py:42
  14.8 6.9 %collective-permute-start.8 = (bf16[4,16,1024]{2,1,0:T(8,128)(2,1)S(1)}, bf16[4,16,1024]{2,1,0:T(8,128)(2,1)S(1)}, u32[]{:S(2)}, u32[]{:S(2)}) collective-permute-start(bf16[4,16,1024]{2,1,0:T(8,128)(2,1)S(1)} %get-tuple-element.17), channel_id=1, source_target_pairs={{0,32},{1,33},{2,34},{3,35},{4,36},{5,37},{6,38},{7,39},{8,40},{9,... | collective-permute-start | bytes 393224 | tf_op jit(solution)/shard_map/ppermute | solution.py:42
  17.0 6.1 %collective-permute-start.9 = (bf16[4,16,1024]{2,1,0:T(8,128)(2,1)S(1)}, bf16[4,16,1024]{2,1,0:T(8,128)(2,1)S(1)}, u32[]{:S(2)}, u32[]{:S(2)}) collective-permute-start(bf16[4,16,1024]{2,1,0:T(8,128)(2,1)S(1)} %get-tuple-element.17), channel_id=1, source_target_pairs={{0,48},{1,49},{2,50},{3,51},{4,52},{5,53},{6,54},{7,55},{8,56},{9,... | collective-permute-start | bytes 393224 | tf_op jit(solution)/shard_map/ppermute | solution.py:42
  18.4 10.0 %collective-permute-start.7 = (bf16[4,16,1024]{2,1,0:T(8,128)(2,1)S(1)}, bf16[4,16,1024]{2,1,0:T(8,128)(2,1)S(1)}, u32[]{:S(2)}, u32[]{:S(2)}) collective-permute-start(bf16[4,16,1024]{2,1,0:T(8,128)(2,1)S(1)} %get-tuple-element.17), channel_id=1, source_target_pairs={{0,16},{1,17},{2,18},{3,19},{4,20},{5,21},{6,22},{7,23},{8,24},{9,... | collective-permute-start | bytes 393224 | tf_op jit(solution)/shard_map/ppermute | solution.py:42
  21.7 48.4 %collective-permute-start.17 = (bf16[256,1024]{1,0:T(8,128)(2,1)}, bf16[256,1024]{1,0:T(8,128)(2,1)}, u32[]{:S(2)}, u32[]{:S(2)}) collective-permute-start(bf16[256,1024]{1,0:T(8,128)(2,1)} %bitcast.58), channel_id=1, source_target_pairs={{0,3},{1,0},{2,1},{3,2},{4,7},{5,4},{6,5},{7,6},{8,11},{9,8},{10,9... | collective-permute-start | bytes 1572872 | tf_op jit(solution)/shard_map/ppermute | solution.py:42
  23.1 45.3 %collective-permute-start = (bf16[256,1024]{1,0:T(8,128)(2,1)}, bf16[256,1024]{1,0:T(8,128)(2,1)S(1)}, u32[]{:S(2)}, u32[]{:S(2)}) collective-permute-start(bf16[256,1024]{1,0:T(8,128)(2,1)} %bitcast.59), channel_id=1, source_target_pairs={{0,4},{1,5},{2,6},{3,7},{4,0},{5,1},{6,2},{7,3},{8,12},{9,13},{10,... | collective-permute-start | bytes 1572872 | tf_op jit(solution)/shard_map/ppermute | solution.py:42
  29.3 10.1 %collective-permute-start.10 = (bf16[4,4,16,1024]{3,2,1,0:T(8,128)(2,1)}, bf16[4,4,16,1024]{3,2,1,0:T(8,128)(2,1)}, u32[]{:S(2)}, u32[]{:S(2)}) collective-permute-start(bf16[4,4,16,1024]{3,2,1,0:T(8,128)(2,1)} %get-tuple-element.15), channel_id=1, source_target_pairs={{0,8},{1,9},{2,10},{3,11},{4,12},{5,13},{6,14},{7,15},{8,0},{9,1},... | collective-permute-start | bytes 1572872 | tf_op jit(solution)/shard_map/ppermute | solution.py:42
  39.5 1.8 %copy-start.5 = (f32[64]{0:T(128)S(1)}, f32[64]{0:T(128)}, u32[]{:S(2)}) copy-start(f32[64]{0:T(128)} %param.17) | copy-start | bytes 772
  40.7 15.8 %collective-permute-start.11 = (bf16[2,16,1024]{2,1,0:T(8,128)(2,1)S(1)}, bf16[2,16,1024]{2,1,0:T(8,128)(2,1)S(1)}, u32[]{:S(2)}, u32[]{:S(2)}) collective-permute-start(bf16[2,16,1024]{2,1,0:T(8,128)(2,1)S(1)} %get-tuple-element.19), channel_id=1, source_target_pairs={{0,4},{1,5},{2,6},{3,7},{4,0},{5,1},{6,2},{7,3},{8,12},{9,13},{10,... | collective-permute-start | bytes 196616 | tf_op jit(solution)/shard_map/ppermute | solution.py:42
  56.5 15.1 %collective-permute-start.12 = (bf16[2,2,16,1024]{3,2,1,0:T(8,128)(2,1)S(1)}, bf16[2,2,16,1024]{3,2,1,0:T(8,128)(2,1)S(1)}, u32[]{:S(2)}, u32[]{:S(2)}) collective-permute-start(bf16[2,2,16,1024]{3,2,1,0:T(8,128)(2,1)S(1)} %pad_maximum_fusion.3.p0), channel_id=1, source_target_pairs={{0,1},{1,2},{2,3},{3,0},{4,5},{5,6},{6,7},{7,4},{8,9},{9,10},{10,1... | collective-permute-start | bytes 393224 | tf_op jit(solution)/shard_map/ppermute | solution.py:42
  56.7 17.4 %collective-permute-start.13 = (bf16[2,2,16,1024]{3,2,1,0:T(8,128)(2,1)S(1)}, bf16[2,2,16,1024]{3,2,1,0:T(8,128)(2,1)}, u32[]{:S(2)}, u32[]{:S(2)}) collective-permute-start(bf16[2,2,16,1024]{3,2,1,0:T(8,128)(2,1)S(1)} %pad_maximum_fusion.3.p0), channel_id=1, source_target_pairs={{0,2},{1,3},{2,0},{3,1},{4,6},{5,7},{6,4},{7,5},{8,10},{9,11},{10,... | collective-permute-start | bytes 393224 | tf_op jit(solution)/shard_map/ppermute | solution.py:42
  59.4 14.7 %collective-permute-start.14 = (bf16[2,2,16,1024]{3,2,1,0:T(8,128)(2,1)S(1)}, bf16[2,2,16,1024]{3,2,1,0:T(8,128)(2,1)}, u32[]{:S(2)}, u32[]{:S(2)}) collective-permute-start(bf16[2,2,16,1024]{3,2,1,0:T(8,128)(2,1)S(1)} %pad_maximum_fusion.3.p0), channel_id=1, source_target_pairs={{0,3},{1,0},{2,1},{3,2},{4,7},{5,4},{6,5},{7,6},{8,11},{9,8},{10,9... | collective-permute-start | bytes 393224 | tf_op jit(solution)/shard_map/ppermute | solution.py:42
  64.0 4.0 %copy-start.4 = (f32[64]{0:T(128)S(1)}, f32[64]{0:T(128)}, u32[]{:S(2)}) copy-start(f32[64]{0:T(128)} %param.18) | copy-start | bytes 772
  64.0 10.1 %copy-start.2 = (bf16[1,2,128,1024]{3,2,1,0:T(8,128)(2,1)S(1)}, bf16[1,2,128,1024]{3,2,1,0:T(8,128)(2,1)}, u32[]{:S(2)}) copy-start(bf16[1,2,128,1024]{3,2,1,0:T(8,128)(2,1)} %param.10) | copy-start | bytes 1572868
  68.4 32.5 %collective-permute-start.1 = (bf16[256,1024]{1,0:T(8,128)(2,1)S(1)}, bf16[256,1024]{1,0:T(8,128)(2,1)S(1)}, u32[]{:S(2)}, u32[]{:S(2)}) collective-permute-start(bf16[256,1024]{1,0:T(8,128)(2,1)S(1)} %collective-permute-done.l0), channel_id=1, source_target_pairs={{0,1},{1,2},{2,3},{3,0},{4,5},{5,6},{6,7},{7,4},{8,9},{9,10},{10,1... | collective-permute-start | bytes 1572872 | tf_op jit(solution)/shard_map/ppermute | solution.py:42
  70.1 30.7 %collective-permute-start.2 = (bf16[256,1024]{1,0:T(8,128)(2,1)S(1)}, bf16[256,1024]{1,0:T(8,128)(2,1)S(1)}, u32[]{:S(2)}, u32[]{:S(2)}) collective-permute-start(bf16[256,1024]{1,0:T(8,128)(2,1)S(1)} %collective-permute-done.l0), channel_id=1, source_target_pairs={{0,2},{1,3},{2,0},{3,1},{4,6},{5,7},{6,4},{7,5},{8,10},{9,11},{10,... | collective-permute-start | bytes 1572872 | tf_op jit(solution)/shard_map/ppermute | solution.py:42
  71.5 29.3 %collective-permute-start.3 = (bf16[256,1024]{1,0:T(8,128)(2,1)S(1)}, bf16[256,1024]{1,0:T(8,128)(2,1)S(1)}, u32[]{:S(2)}, u32[]{:S(2)}) collective-permute-start(bf16[256,1024]{1,0:T(8,128)(2,1)S(1)} %collective-permute-done.l0), channel_id=1, source_target_pairs={{0,3},{1,0},{2,1},{3,2},{4,7},{5,4},{6,5},{7,6},{8,11},{9,8},{10,9... | collective-permute-start | bytes 1572872 | tf_op jit(solution)/shard_map/ppermute | solution.py:42
  74.1 26.8 %copy-start.1 = (bf16[1024,1024]{0,1:T(8,128)(2,1)S(1)}, bf16[1024,1024]{0,1:T(8,128)(2,1)}, u32[]{:S(2)}) copy-start(bf16[1024,1024]{0,1:T(8,128)(2,1)} %copy.21) | copy-start | bytes 6291460
  99.5 1.3 %copy-start.3 = (f32[16,256,128]{2,1,0:T(8,128)}, f32[16,256,128]{2,1,0:T(8,128)S(1)}, u32[]{:S(2)}) copy-start(f32[16,256,128]{2,1,0:T(8,128)S(1)} %get-tuple-element.8.acc_ref) | copy-start | bytes 6291460

commit v2 on v1

v2 whole, which is shorter than its diff:
```python
import math

import jax
import jax.numpy as jnp
import numpy as np
from jax import lax
from jax.experimental import pallas as pl
from jax.experimental.pallas import tpu as pltpu
from jax.sharding import Mesh
from jax.sharding import PartitionSpec as P

HEADS = 16
HEAD = 64
TEMB = 256
TSTEPS = 1000
D = 1024
FRAMES = 16
TOKF = 128
AXES = ("zl", "x", "core", "zh", "y")
ZL, X, CORE, ZH, Y = 4, 4, 2, 2, 4
ROWS = 256
PIECE = 16
PAIRS = HEADS // 2
F32 = jnp.float32
BF16 = jnp.bfloat16
QSCALE = HEAD ** (-0.5) * math.log2(math.e)


def moves(zl=0, x=0, core=0, zh=0, y=0):
    pairs = []
    for i in range(ZL * X * CORE * ZH * Y):
        rest, iy = divmod(i, Y)
        rest, izh = divmod(rest, ZH)
        rest, ic = divmod(rest, CORE)
        izl, ix = divmod(rest, X)
        izl, ix, ic = (izl + zl) % ZL, (ix + x) % X, (ic + core) % CORE
        izh, iy = (izh + zh) % ZH, (iy + y) % Y
        pairs.append((i, (((izl * X + ix) * CORE + ic) * ZH + izh) * Y + iy))
    return pairs


def send(value, **step):
    return lax.ppermute(value, AXES, moves(**step))


def after(value, earlier):
    return lax.optimization_barrier((value, earlier))[0]


def dot(a, b):
    return jnp.dot(a, b, preferred_element_type=F32)


def dot_tt(a, b):
    return lax.dot_general(a, b, (((0,), (1,)), ((), ())), preferred_element_type=F32)


def blend_tables(time_ref, pieces, base_ref, first_s, diff_s):
    kw = 1.0 - time_ref[0].astype(F32) * (1.0 / (2.0 * TSTEPS))
    for i, piece in enumerate(pieces):
        for z in range(ZH):
            base = pl.multiple_of(base_ref[ZH * i + z], PIECE)
            first = piece[0, z].astype(F32) * kw
            last = piece[1, z].astype(F32) * kw
            first_s[pl.ds(base, PIECE), :] = first
            diff_s[pl.ds(base, PIECE), :] = last - first


def norm_chunk(j, lat_ref, ramp_ref, at, first_s, diff_s, gain_ref, shift_ref, x_s):
    step = 32

    def rows(i, carry):
        r = pl.multiple_of(i * step, step)
        tok = pl.multiple_of(lax.rem(i, TOKF // step) * step, step)
        ramp = ramp_ref[at + i // (TOKF // step)]
        resid = lat_ref[pl.ds(r, step), :].astype(F32) + (
            first_s[pl.ds(tok, step), :] + ramp * diff_s[pl.ds(tok, step), :]
        )
        mean = jnp.mean(resid, axis=-1, keepdims=True)
        cent = resid - mean
        var = jnp.mean(cent * cent, axis=-1, keepdims=True)
        normed = cent * lax.rsqrt(var + 1e-06) * gain_ref[...] + shift_ref[...]
        x_s[pl.ds(pl.multiple_of(j * ROWS + i * step, step), step), :] = normed.astype(BF16)
        return carry

    lax.fori_loop(0, ROWS // step, rows, 0, unroll=4)


def head_norm_t(block, gain):
    heads = block.reshape(block.shape[0] // HEAD, HEAD, block.shape[1])
    mean = jnp.mean(heads * heads, axis=1, keepdims=True)
    return (heads * lax.rsqrt(mean + 1e-06) * gain[None]).reshape(block.shape)


def keys_values(x_s, w_ref, kgain_ref, kt_s, v_s):
    def values(i, carry):
        f = pl.multiple_of(i * 256, 256)
        v_s[:, pl.ds(f, 256)] = dot(x_s[...], w_ref[:, pl.ds(2 * D + f, 256)]).astype(BF16)
        return carry

    def keys(i, carry):
        t = pl.multiple_of(i * 256, 256)
        kt = dot_tt(w_ref[:, D : 2 * D], x_s[pl.ds(t, 256), :])
        kt_s[:, pl.ds(t, 256)] = head_norm_t(kt, kgain_ref[...]).astype(BF16)
        return carry

    lax.fori_loop(0, D // 256, values, 0)
    lax.fori_loop(0, x_s.shape[0] // 256, keys, 0)


def attend(q_ref, kt_s, v_s, acc_in, acc_out):
    lane_q = lax.broadcasted_iota(jnp.int32, (ROWS, 128), 1) < HEAD
    lane_v = lax.broadcasted_iota(jnp.int32, (kt_s.shape[1], 128), 1) < HEAD
    one = jnp.ones((), BF16)
    zero = jnp.zeros((), BF16)

    def pair(p, carry):
        f = pl.multiple_of(p * 128, 128)
        qp = q_ref[:, pl.ds(f, 128)]
        vp = v_s[:, pl.ds(f, 128)]
        for odd in range(2):
            keep = lane_q if odd == 0 else jnp.logical_not(lane_q)
            keepv = lane_v if odd == 0 else jnp.logical_not(lane_v)
            s = dot(jnp.where(keep, qp, zero), kt_s[pl.ds(f, 128), :])
            total = dot(jnp.exp2(s).astype(BF16), jnp.where(keepv, vp, one))
            if acc_in is not None:
                total = total + acc_in[2 * p + odd]
            acc_out[2 * p + odd] = total
        return carry

    lax.fori_loop(0, PAIRS, pair, 0, unroll=4)


def first_kernel(
    time_ref, ramp_ref, base_ref, l0, l1, l2, l3, p0, p1, p2, p3, gain_ref, shift_ref, w_hbm,
    qgain_ref, kgain_ref, acc_ref, q_ref, first_s, diff_s, x_s, kt_s, v_s, w_ref, sem,
):
    fetch = pltpu.make_async_copy(w_hbm, w_ref, sem)
    fetch.start()
    blend_tables(time_ref, (p0, p1, p2, p3), base_ref, first_s, diff_s)
    for j, lat in enumerate((l0, l1, l2, l3)):
        norm_chunk(j, lat, ramp_ref, 2 * j, first_s, diff_s, gain_ref, shift_ref, x_s)
    fetch.wait()

    def queries(i, carry):
        f = pl.multiple_of(i * 256, 256)
        qt = dot_tt(w_ref[:, pl.ds(f, 256)], x_s[:ROWS, :])
        q_ref[:, pl.ds(f, 256)] = head_norm_t(qt, qgain_ref[...]).T.astype(BF16)
        return carry

    lax.fori_loop(0, D // 256, queries, 0)
    keys_values(x_s, w_ref, kgain_ref, kt_s, v_s)
    attend(q_ref, kt_s, v_s, None, acc_ref)


def second_kernel(
    time_ref, ramp_ref, base_ref, own, l0, l1, l2, l3, p0, p1, p2, p3, gain_ref, shift_ref, w_hbm,
    kgain_ref, wo_ref, q_ref, acc_ref, out_ref, first_s, diff_s, x_s, kt_s, v_s, w_ref, sem, acc_s,
):
    fetch = pltpu.make_async_copy(w_hbm, w_ref, sem)
    fetch.start()
    blend_tables(time_ref, (p0, p1, p2, p3), base_ref, first_s, diff_s)
    for j, lat in enumerate((l0, l1, l2, l3)):
        norm_chunk(j, lat, ramp_ref, 8 + 2 * j, first_s, diff_s, gain_ref, shift_ref, x_s)
    fetch.wait()
    keys_values(x_s, w_ref, kgain_ref, kt_s, v_s)
    attend(q_ref, kt_s, v_s, acc_ref, acc_s)

    lane = lax.broadcasted_iota(jnp.int32, (ROWS, 128), 1) < HEAD
    for p in range(PAIRS):
        even = acc_s[2 * p]
        odd = acc_s[2 * p + 1]
        num = jnp.where(lane, even, odd)
        den = pltpu.roll(jnp.where(lane, odd, even), HEAD, 1)
        x_s[:ROWS, p * 128 : (p + 1) * 128] = (num / den).astype(BF16)

    def block(i, carry):
        f = pl.multiple_of(i * 256, 256)
        o = dot(x_s[:ROWS, :], wo_ref[:, pl.ds(f, 256)])
        for k in range(2):
            r = slice(k * TOKF, (k + 1) * TOKF)
            resid = own[r, pl.ds(f, 256)].astype(F32) + (
                first_s[:, pl.ds(f, 256)] + ramp_ref[16 + k] * diff_s[:, pl.ds(f, 256)]
            )
            out_ref[r, pl.ds(f, 256)] = (resid + o[r]).astype(BF16)
        return carry

    lax.fori_loop(0, D // 256, block, 0)


def mask_kernel(pick_ref, mine, other, *out_refs):
    for t in range(X):
        for k in range(2):
            pick = pick_ref[2 * t + k]

            @pl.when(pick < 0)
            def _():
                out_refs[t][k] = jnp.zeros_like(out_refs[t][k])

            for c, held in enumerate((mine, other)):

                @pl.when(jnp.logical_and(pick >= ZL * c, pick < ZL * (c + 1)))
                def _():
                    out_refs[t][k] = held[pick - ZL * c]


VMEM = pl.BlockSpec(memory_space=pltpu.VMEM)
SMEM = pl.BlockSpec(memory_space=pltpu.SMEM)
HBM = pl.BlockSpec(memory_space=pltpu.HBM)


def scratch():
    return [
        pltpu.VMEM((TOKF, D), F32),
        pltpu.VMEM((TOKF, D), F32),
        pltpu.VMEM((Y * ROWS, D), BF16),
        pltpu.VMEM((D, Y * ROWS), BF16),
        pltpu.VMEM((Y * ROWS, D), BF16),
        pltpu.VMEM((D, 3 * D), BF16),
        pltpu.SemaphoreType.DMA,
    ]


def tables():
    ramps, bases = [], []
    for seq in range(ZH * Y):
        zh, y = divmod(seq, Y)
        near = [2 * (zh * Y + (y - j) % Y) + k for j in range(Y) for k in range(2)]
        far = [2 * ((1 - zh) * Y + (y - j) % Y) + k for j in range(Y) for k in range(2)]
        own = [2 * seq, 2 * seq + 1]
        ramps.append([frame / (FRAMES - 1) for frame in near + far + own])
        base = [(z * Y + (y - j) % Y) * PIECE for j in range(Y) for z in (zh, 1 - zh)]
        bases.append(base + [y])
    return np.array(ramps, np.float32), np.array(bases, np.int32)


def body(
    latents, keyframes, key_index, timesteps, mod_weight, norm_gain, qkv_weight, query_gain,
    key_gain, out_weight,
):
    zl, x, core = lax.axis_index("zl"), lax.axis_index("x"), lax.axis_index("core")
    seq = lax.axis_index("zh") * Y + lax.axis_index("y")

    own = latents.reshape(ROWS, D)
    mine = keyframes[0]
    pair = key_index

    planes = jnp.stack([mine, send(mine, zh=1)])
    near_1 = send(own, y=1)
    near_3 = send(own, y=3)
    by_zl = jnp.stack([planes] + [send(planes, zl=k) for k in (1, 2, 3)])
    pairs = [key_index] + [send(after(key_index, planes), x=k) for k in (1, 2, 3)]
    near_2 = send(after(own, near_1), y=2)
    near = [own, near_1, near_2, near_3]
    cross = send(after(own, by_zl), zh=1)

    wanted = jnp.concatenate(pairs).reshape(-1)
    entry = ((core + wanted) % CORE) * ZL + (zl - wanted // (X * CORE)) % ZL
    picks = jnp.where(wanted // CORE % X == x, entry, -1)
    picks = after(picks, (near_1, near_3))
    masked = pl.pallas_call(
        mask_kernel,
        out_shape=(jax.ShapeDtypeStruct((2, ZH, PIECE, D), BF16),) * X,
        in_specs=[SMEM] + [VMEM] * 2,
        out_specs=(VMEM,) * X,
        name="mask",
    )(picks, by_zl, send(by_zl, core=1))
    found = [send(masked[t], x=X - t) for t in (1, 2, 3)]
    both = after(masked[0], near_2) + found[0] + found[1] + found[2]
    pieces = [both] + [send(both, y=k) for k in (1, 2, 3)]
    late = after(cross, pieces[1])
    far = [cross] + [send(late, y=k) for k in (1, 2, 3)]

    halfway = TEMB // 2
    freqs = jnp.exp(-math.log(10000.0) * jnp.arange(halfway, dtype=F32) / halfway)
    angles = timesteps[1].astype(F32) * freqs
    embed = jnp.concatenate([jnp.sin(angles), jnp.cos(angles)]).astype(BF16)
    modulation = jnp.dot(embed[None, :], mod_weight, preferred_element_type=F32)
    gain = norm_gain[None, :] * (1.0 + modulation[:, :D])
    shift = modulation[:, D:]

    qgain = (query_gain * QSCALE)[:, None]
    kgain = key_gain[:, None]
    ramp_table, base_table = tables()
    ramps = lax.dynamic_index_in_dim(jnp.asarray(ramp_table), seq, 0, keepdims=False)
    base = lax.dynamic_index_in_dim(jnp.asarray(base_table), seq, 0, keepdims=False)

    flops = 2 * 1024 * 1024 * 2048 + 4 * 16 * 256 * 1024 * 128
    params = pltpu.CompilerParams(vmem_limit_bytes=32 * 1024 * 1024)
    acc, q = pl.pallas_call(
        first_kernel,
        out_shape=(
            jax.ShapeDtypeStruct((HEADS, ROWS, 128), F32),
            jax.ShapeDtypeStruct((ROWS, D), BF16),
        ),
        in_specs=[SMEM] * 3 + [VMEM] * 10 + [HBM] + [VMEM] * 2,
        out_specs=(VMEM, VMEM),
        scratch_shapes=scratch(),
        compiler_params=params,
        cost_estimate=pl.CostEstimate(flops=flops, bytes_accessed=12 << 20, transcendentals=4 << 20),
        name="near_keys",
    )(timesteps, ramps, base, *near, *pieces, gain, shift, qkv_weight, qgain, kgain)
    out = pl.pallas_call(
        second_kernel,
        out_shape=jax.ShapeDtypeStruct((ROWS, D), BF16),
        in_specs=[SMEM] * 3 + [VMEM] * 11 + [HBM] + [VMEM] * 4,
        out_specs=VMEM,
        scratch_shapes=scratch() + [pltpu.VMEM((HEADS, ROWS, 128), F32)],
        compiler_params=params,
        cost_estimate=pl.CostEstimate(flops=flops, bytes_accessed=12 << 20, transcendentals=4 << 20),
        name="far_keys",
    )(timesteps, ramps, base, own, *far, *pieces, gain, shift, qkv_weight, kgain, out_weight, q, acc)
    return out.reshape(latents.shape)


def solution(mesh):
    split = Mesh(mesh.devices.reshape(ZL, X, CORE, ZH, Y), AXES)
    leaf, seq = ("zl", "x", "core"), ("zh", "y")
    in_specs = (P(leaf, seq, None, None), P(leaf, seq, None), P(leaf, None)) + (P(),) * 7
    out_specs = P(leaf, seq, None, None)
    return jax.shard_map(body, mesh=split, in_specs=in_specs, out_specs=out_specs, check_vma=False)
```

time: 127 us -> 103 us (0.81)
  the two profiles are of different devices: /device:TPU:2 before, /device:TPU:4 now
where the time goes in v2:
time: 103 us; the launch traced here: 102 us
  starting transfers between devices  38.8 us (38%)
  Pallas kernels  36.3 us (35%)
  waiting for transfers between devices  14.4 us (14%)
  local copies, waits for them, and re-layouts  6.35 us (6%)
  other arithmetic  5.05 us (5%)
    ppermute x21, starting transfers between devices, send(): return lax.ppermute(value, AXES, moves(**step))  38.8 us
    pallas_call x1, Pallas kernels, body(): pl.pallas_call(second_kernel, out_shape=jax.ShapeDtypeStruct((ROWS, D), B...  17.4 us
    pallas_call x1, Pallas kernels, body(): pl.pallas_call(first_kernel, out_shape=(jax.ShapeDtypeStruct((HEADS, ROWS...  16.9 us
    ppermute x21, waiting for transfers between devices, send(): return lax.ppermute(value, AXES, moves(**step))  14.4 us
    unnamed x16, local copies, waits for them, and re-layouts  2.81 us
  transfers between devices with their start and end apart: 21, of which 9 were waited for; matrix products, arithmetic and copies ran while one was open for 9% of the time, Pallas kernels for 19%

profile of v2, /device:TPU:4, one launch (start us, length us, event | category | flops | bytes accessed | tf_op | source)
XLA Modules:
  0.0 102.1 jit_solution(13084912820062112001)
XLA Ops:
  0.0 1.7 %collective-permute-start.8 = (bf16[256,1024]{1,0:T(8,128)(2,1)}, bf16[256,1024]{1,0:T(8,128)(2,1)S(1)}, u32[]{:S(2)}, u32[]{:S(2)}) collective-permute-start(bf16[256,1024]{1,0:T(8,128)(2,1)} %bitcast.21), channel_id=1, source_target_pairs={{0,1},{1,2},{2,3},{3,0},{4,5},{5,6},{6,7},{7,4},{8,9},{9,10},{10,1... | collective-permute-start | bytes 1572872 | tf_op jit(solution)/shard_map/ppermute | solution.py:43
  1.7 1.7 %collective-permute-start.9 = (bf16[256,1024]{1,0:T(8,128)(2,1)}, bf16[256,1024]{1,0:T(8,128)(2,1)S(1)}, u32[]{:S(2)}, u32[]{:S(2)}) collective-permute-start(bf16[256,1024]{1,0:T(8,128)(2,1)} %bitcast.22), channel_id=1, source_target_pairs={{0,3},{1,0},{2,1},{3,2},{4,7},{5,4},{6,5},{7,6},{8,11},{9,8},{10,9... | collective-permute-start | bytes 1572872 | tf_op jit(solution)/shard_map/ppermute | solution.py:43
  3.3 7.2 %collective-permute-start = (bf16[16,1024]{1,0:T(8,128)(2,1)}, bf16[16,1024]{1,0:T(8,128)(2,1)S(1)}, u32[]{:S(2)}, u32[]{:S(2)}) collective-permute-start(bf16[16,1024]{1,0:T(8,128)(2,1)} %bitcast.30), channel_id=1, source_target_pairs={{0,4},{1,5},{2,6},{3,7},{4,0},{5,1},{6,2},{7,3},{8,12},{9,13},{10,... | collective-permute-start | bytes 98312 | tf_op jit(solution)/shard_map/ppermute | solution.py:43
  10.5 1.2 %slice.9 = s32[1]{0:T(128)} slice(s32[2]{0:T(128)} %time_ref.3), slice={[1:2]} | slice | bytes 8 | tf_op jit(solution)/shard_map/slice | solution.py:276
  12.4 0.1 cosine_convert_fusion
  12.5 0.0 copy-done
  12.5 0.2 fusion.8
  12.8 0.0 collective-permute-done
  12.8 0.8 fusion.6
  13.5 1.1 %collective-permute-start.1 = (bf16[2,16,1024]{2,1,0:T(8,128)(2,1)S(1)}, bf16[2,16,1024]{2,1,0:T(8,128)(2,1)S(1)}, u32[]{:S(2)}, u32[]{:S(2)}) collective-permute-start(bf16[2,16,1024]{2,1,0:T(8,128)(2,1)S(1)} %get-tuple-element.30), channel_id=1, source_target_pairs={{0,64},{1,65},{2,66},{3,67},{4,68},{5,69},{6,70},{7,71},{8,72},{9,... | collective-permute-start | bytes 196616 | tf_op jit(solution)/shard_map/ppermute | solution.py:43
  14.6 2.8 %collective-permute-start.2 = (bf16[2,16,1024]{2,1,0:T(8,128)(2,1)S(1)}, bf16[2,16,1024]{2,1,0:T(8,128)(2,1)S(1)}, u32[]{:S(2)}, u32[]{:S(2)}) collective-permute-start(bf16[2,16,1024]{2,1,0:T(8,128)(2,1)S(1)} %get-tuple-element.30), channel_id=1, source_target_pairs={{0,128},{1,129},{2,130},{3,131},{4,132},{5,133},{6,134},{7,135},{8... | collective-permute-start | bytes 196616 | tf_op jit(solution)/shard_map/ppermute | solution.py:43
  17.4 1.0 collective-permute-start.3
  18.4 0.7 fusion.7
  19.1 0.9 collective-permute-done.1
  20.0 1.2 %collective-permute-start.5 = (s32[1,2]{1,0:T(1,128)}, s32[1,2]{1,0:T(1,128)S(1)}, u32[]{:S(2)}, u32[]{:S(2)}) collective-permute-start(s32[1,2]{1,0:T(1,128)} %param.14), channel_id=1, source_target_pairs={{0,16},{1,17},{2,18},{3,19},{4,20},{5,21},{6,22},{7,23},{8,24},{9,... | collective-permute-start | bytes 32 | tf_op jit(solution)/shard_map/ppermute | solution.py:43
  21.2 0.8 collective-permute-done.2
  22.0 0.5 collective-permute-start.6
  22.5 0.0 collective-permute-done.3
  22.5 2.1 %collective-permute-start.7 = (s32[1,2]{1,0:T(1,128)}, s32[1,2]{1,0:T(1,128)S(1)}, u32[]{:S(2)}, u32[]{:S(2)}) collective-permute-start(s32[1,2]{1,0:T(1,128)} %param.14), channel_id=1, source_target_pairs={{0,48},{1,49},{2,50},{3,51},{4,52},{5,53},{6,54},{7,55},{8,56},{9,... | collective-permute-start | bytes 32 | tf_op jit(solution)/shard_map/ppermute | solution.py:43
  24.7 0.7 pad_maximum_fusion.mine
  25.4 0.0 collective-permute-done.8.l1
  25.4 0.0 collective-permute-start.10
  25.4 0.0 collective-permute-done.5
  25.4 1.9 %collective-permute-start.11 = (bf16[256,1024]{1,0:T(8,128)(2,1)}, bf16[256,1024]{1,0:T(8,128)(2,1)S(1)}, u32[]{:S(2)}, u32[]{:S(2)}) collective-permute-start(bf16[256,1024]{1,0:T(8,128)(2,1)} %bitcast.23), channel_id=1, source_target_pairs={{0,2},{1,3},{2,0},{3,1},{4,6},{5,7},{6,4},{7,5},{8,10},{9,11},{10,... | collective-permute-start | bytes 1572872 | tf_op jit(solution)/shard_map/ppermute | solution.py:43
  27.4 0.0 collective-permute-done.6
  27.4 0.0 collective-permute-done.7
  27.4 0.7 pad_add_fusion
  28.0 0.1 reshape.16
  28.1 0.6 compare_select_fusion.6.pick_ref
  28.7 5.0 %collective-permute-start.4 = (bf16[256,1024]{1,0:T(8,128)(2,1)}, bf16[256,1024]{1,0:T(8,128)(2,1)}, u32[]{:S(2)}, u32[]{:S(2)}) collective-permute-start(bf16[256,1024]{1,0:T(8,128)(2,1)} %bitcast.24), channel_id=1, source_target_pairs={{0,4},{1,5},{2,6},{3,7},{4,0},{5,1},{6,2},{7,3},{8,12},{9,13},{10,... | collective-permute-start | bytes 1572872 | tf_op jit(solution)/shard_map/ppermute | solution.py:43
  33.7 0.0 collective-permute-done.9.l3
  33.7 0.0 collective-permute-done.10.other
  33.7 2.0 %mask.1 = (bf16[2,2,16,1024]{3,2,1,0:T(8,128)(2,1)}, bf16[2,2,16,1024]{3,2,1,0:T(8,128)(2,1)}, bf16[2,2,16,1024]{3,2,1,0:T(8,128)(2,1)}, bf16[2,2,16,1024]{3,2,1,0:T(8,128)(2,1)}) custom-call(s32[8]{0:T(128)} %compare_select_fusion.6.pick_ref, bf16[4,2,16,1024]{3,2,1,0:T(8,128)(2,1)} %pad_maximum_fusion.mine, ...), custom_call_target="tpu_custom_call" | custom-call | tf_op jit(solution)/shard_map/mask/pallas_call | solution.py:261
  35.8 1.4 %collective-permute-start.12 = (bf16[2,2,16,1024]{3,2,1,0:T(8,128)(2,1)}, bf16[2,2,16,1024]{3,2,1,0:T(8,128)(2,1)S(1)}, u32[]{:S(2)}, u32[]{:S(2)}) collective-permute-start(bf16[2,2,16,1024]{3,2,1,0:T(8,128)(2,1)} %get-tuple-element.23), channel_id=1, source_target_pairs={{0,48},{1,49},{2,50},{3,51},{4,52},{5,53},{6,54},{7,55},{8,56},{9,... | collective-permute-start | bytes 393224 | tf_op jit(solution)/shard_map/ppermute | solution.py:43
  37.2 2.8 %collective-permute-start.13 = (bf16[2,2,16,1024]{3,2,1,0:T(8,128)(2,1)}, bf16[2,2,16,1024]{3,2,1,0:T(8,128)(2,1)S(1)}, u32[]{:S(2)}, u32[]{:S(2)}) collective-permute-start(bf16[2,2,16,1024]{3,2,1,0:T(8,128)(2,1)} %get-tuple-element.24), channel_id=1, source_target_pairs={{0,32},{1,33},{2,34},{3,35},{4,36},{5,37},{6,38},{7,39},{8,40},{9,... | collective-permute-start | bytes 393224 | tf_op jit(solution)/shard_map/ppermute | solution.py:43
  40.0 0.6 collective-permute-start.14
  40.6 0.5 multiply_bitcast_fusion
  41.1 0.4 collective-permute-done.11.l2
  41.5 0.1 collective-permute-done.12
  41.5 3.8 %collective-permute-done.13 = bf16[2,2,16,1024]{3,2,1,0:T(8,128)(2,1)S(1)} collective-permute-done((bf16[2,2,16,1024]{3,2,1,0:T(8,128)(2,1)}, bf16[2,2,16,1024]{3,2,1,0:T(8,128)(2,1)S(1)}, u32[]{:S(2)}, u32[]{:S(2)}) %collective-permute-start.13) | collective-permute-done | bytes 131104 | tf_op jit(solution)/shard_map/ppermute | solution.py:43
  45.3 0.7 collective-permute-done.14
  46.1 1.0 add_add_fusion.p0
  47.1 0.8 collective-permute-start.15
  47.8 2.3 %collective-permute-start.19 = (bf16[2,2,16,1024]{3,2,1,0:T(8,128)(2,1)S(1)}, bf16[2,2,16,1024]{3,2,1,0:T(8,128)(2,1)}, u32[]{:S(2)}, u32[]{:S(2)}) collective-permute-start(bf16[2,2,16,1024]{3,2,1,0:T(8,128)(2,1)S(1)} %add_add_fusion.p0), channel_id=1, source_target_pairs={{0,2},{1,3},{2,0},{3,1},{4,6},{5,7},{6,4},{7,5},{8,10},{9,11},{10,... | collective-permute-start | bytes 393224 | tf_op jit(solution)/shard_map/ppermute | solution.py:43
  50.1 1.4 %collective-permute-start.20 = (bf16[2,2,16,1024]{3,2,1,0:T(8,128)(2,1)S(1)}, bf16[2,2,16,1024]{3,2,1,0:T(8,128)(2,1)}, u32[]{:S(2)}, u32[]{:S(2)}) collective-permute-start(bf16[2,2,16,1024]{3,2,1,0:T(8,128)(2,1)S(1)} %add_add_fusion.p0), channel_id=1, source_target_pairs={{0,3},{1,0},{2,1},{3,2},{4,7},{5,4},{6,5},{7,6},{8,11},{9,8},{10,9... | collective-permute-start | bytes 393224 | tf_op jit(solution)/shard_map/ppermute | solution.py:43
  51.5 0.7 dynamic-slice_bitcast_fusion.base_ref
  52.2 0.1 copy.18.kgain_ref
  52.3 0.7 copy.16.qgain_ref
  53.1 0.7 dynamic-slice_bitcast_fusion.1.ramp_ref
  53.8 4.4 %collective-permute-done.4.l0 = bf16[256,1024]{1,0:T(8,128)(2,1)} collective-permute-done((bf16[256,1024]{1,0:T(8,128)(2,1)}, bf16[256,1024]{1,0:T(8,128)(2,1)}, u32[]{:S(2)}, u32[]{:S(2)}) %collective-permute-start.4) | collective-permute-done | bytes 524320 | tf_op jit(solution)/shard_map/ppermute | solution.py:43
  58.2 0.0 collective-permute-done.15.p1
  58.2 0.7 collective-permute-start.16
  58.8 1.8 %collective-permute-start.17 = (bf16[256,1024]{1,0:T(8,128)(2,1)}, bf16[256,1024]{1,0:T(8,128)(2,1)S(1)}, u32[]{:S(2)}, u32[]{:S(2)}) collective-permute-start(bf16[256,1024]{1,0:T(8,128)(2,1)} %collective-permute-done.4.l0), channel_id=1, source_target_pairs={{0,2},{1,3},{2,0},{3,1},{4,6},{5,7},{6,4},{7,5},{8,10},{9,11},{10,... | collective-permute-start | bytes 1572872 | tf_op jit(solution)/shard_map/ppermute | solution.py:43
  60.7 0.8 collective-permute-start.18
  61.5 0.0 collective-permute-done.19.p2
  61.5 0.0 collective-permute-done.20.p3
  61.5 0.0 copy-done.4
  61.5 0.0 copy-start.1
  61.6 2.8 %copy-done.1 = bf16[1024,3072]{1,0:T(8,128)(2,1)S(1)} copy-done((bf16[1024,3072]{1,0:T(8,128)(2,1)S(1)}, bf16[1024,3072]{1,0:T(8,128)(2,1)}, u32[]{:S(2)}) %copy-start.1) | copy-done | bytes 6291480
  64.3 16.9 %near_keys.1 = (f32[16,256,128]{2,1,0:T(8,128)S(1)}, bf16[256,1024]{1,0:T(8,128)(2,1)S(1)}) custom-call(s32[2]{0:T(128)S(1)} %copy-done.5, f32[18]{0:T(128)S(1)} %dynamic-slice_bitcast_fusion.1.ramp_ref, s32[9]{0:T(128)S(1)} %dynamic-slice_bitcast_fusion.base_ref, bf16[256,1024]{1,0:T(8,128)(2,1)S(1)} %bitcast.25, ...), custom_call_target="tpu_custom_call" | custom-call | flops 6442450944 | bytes 12582912 | tf_op jit(solution)/shard_map/near_keys/pallas_call | solution.py:290
  81.2 2.7 %collective-permute-done.16.l1 = bf16[256,1024]{1,0:T(8,128)(2,1)S(1)} collective-permute-done((bf16[256,1024]{1,0:T(8,128)(2,1)}, bf16[256,1024]{1,0:T(8,128)(2,1)S(1)}, u32[]{:S(2)}, u32[]{:S(2)}) %collective-permute-start.16) | collective-permute-done | bytes 524320 | tf_op jit(solution)/shard_map/ppermute | solution.py:43
  83.9 0.0 collective-permute-done.17.l2
  83.9 0.6 collective-permute-done.18.l3
  84.6 17.4 %far_keys.1 = bf16[256,1024]{1,0:T(8,128)(2,1)} custom-call(s32[2]{0:T(128)S(1)} %copy-done.5, f32[18]{0:T(128)S(1)} %dynamic-slice_bitcast_fusion.1.ramp_ref, s32[9]{0:T(128)S(1)} %dynamic-slice_bitcast_fusion.base_ref, bf16[256,1024]{1,0:T(8,128)(2,1)S(1)} %bitcast.26, bf16[256,1024]{1,0:T(8,128)(2,1)} %collective-permute-done.4.l0, ...), custom_call_target="tpu_custom_call" | custom-call | flops 6442450944 | bytes 12582912 | tf_op jit(solution)/shard_map/far_keys/pallas_call | solution.py:303
  (14 shorter events, 0.0 us)
Async XLA Ops:
  0.0 12.5 %copy-start = (bf16[256,2048]{1,0:T(8,128)(2,1)S(1)}, bf16[256,2048]{1,0:T(8,128)(2,1)}, u32[]{:S(2)}) copy-start(bf16[256,2048]{1,0:T(8,128)(2,1)} %param.16) | copy-start | bytes 3145732
  0.0 61.5 %copy-start.4 = (bf16[1,2,128,1024]{3,2,1,0:T(8,128)(2,1)S(1)}, bf16[1,2,128,1024]{3,2,1,0:T(8,128)(2,1)}, u32[]{:S(2)}) copy-start(bf16[1,2,128,1024]{3,2,1,0:T(8,128)(2,1)} %param.12) | copy-start | bytes 1572868
  0.0 61.5 %copy-start.5 = (s32[2]{0:T(128)S(1)}, s32[2]{0:T(128)}, u32[]{:S(2)}) copy-start(s32[2]{0:T(128)} %time_ref.3) | copy-start | bytes 28
  0.0 40.6 %copy-start.7 = (f32[64]{0:T(128)S(1)}, f32[64]{0:T(128)}, u32[]{:S(2)}) copy-start(f32[64]{0:T(128)} %param.19) | copy-start | bytes 772
  0.0 52.2 %copy-start.6 = (f32[64]{0:T(128)S(1)}, f32[64]{0:T(128)}, u32[]{:S(2)}) copy-start(f32[64]{0:T(128)} %param.20) | copy-start | bytes 772
  0.0 25.4 %collective-permute-start.8 = (bf16[256,1024]{1,0:T(8,128)(2,1)}, bf16[256,1024]{1,0:T(8,128)(2,1)S(1)}, u32[]{:S(2)}, u32[]{:S(2)}) collective-permute-start(bf16[256,1024]{1,0:T(8,128)(2,1)} %bitcast.21), channel_id=1, source_target_pairs={{0,1},{1,2},{2,3},{3,0},{4,5},{5,6},{6,7},{7,4},{8,9},{9,10},{10,1... | collective-permute-start | bytes 1572872 | tf_op jit(solution)/shard_map/ppermute | solution.py:43
  1.7 32.1 %collective-permute-start.9 = (bf16[256,1024]{1,0:T(8,128)(2,1)}, bf16[256,1024]{1,0:T(8,128)(2,1)S(1)}, u32[]{:S(2)}, u32[]{:S(2)}) collective-permute-start(bf16[256,1024]{1,0:T(8,128)(2,1)} %bitcast.22), channel_id=1, source_target_pairs={{0,3},{1,0},{2,1},{3,2},{4,7},{5,4},{6,5},{7,6},{8,11},{9,8},{10,9... | collective-permute-start | bytes 1572872 | tf_op jit(solution)/shard_map/ppermute | solution.py:43
  3.3 9.4 %collective-permute-start = (bf16[16,1024]{1,0:T(8,128)(2,1)}, bf16[16,1024]{1,0:T(8,128)(2,1)S(1)}, u32[]{:S(2)}, u32[]{:S(2)}) collective-permute-start(bf16[16,1024]{1,0:T(8,128)(2,1)} %bitcast.30), channel_id=1, source_target_pairs={{0,4},{1,5},{2,6},{3,7},{4,0},{5,1},{6,2},{7,3},{8,12},{9,13},{10,... | collective-permute-start | bytes 98312 | tf_op jit(solution)/shard_map/ppermute | solution.py:43
  13.5 6.5 %collective-permute-start.1 = (bf16[2,16,1024]{2,1,0:T(8,128)(2,1)S(1)}, bf16[2,16,1024]{2,1,0:T(8,128)(2,1)S(1)}, u32[]{:S(2)}, u32[]{:S(2)}) collective-permute-start(bf16[2,16,1024]{2,1,0:T(8,128)(2,1)S(1)} %get-tuple-element.30), channel_id=1, source_target_pairs={{0,64},{1,65},{2,66},{3,67},{4,68},{5,69},{6,70},{7,71},{8,72},{9,... | collective-permute-start | bytes 196616 | tf_op jit(solution)/shard_map/ppermute | solution.py:43
  14.6 7.4 %collective-permute-start.2 = (bf16[2,16,1024]{2,1,0:T(8,128)(2,1)S(1)}, bf16[2,16,1024]{2,1,0:T(8,128)(2,1)S(1)}, u32[]{:S(2)}, u32[]{:S(2)}) collective-permute-start(bf16[2,16,1024]{2,1,0:T(8,128)(2,1)S(1)} %get-tuple-element.30), channel_id=1, source_target_pairs={{0,128},{1,129},{2,130},{3,131},{4,132},{5,133},{6,134},{7,135},{8... | collective-permute-start | bytes 196616 | tf_op jit(solution)/shard_map/ppermute | solution.py:43
  17.4 5.1 %collective-permute-start.3 = (bf16[2,16,1024]{2,1,0:T(8,128)(2,1)S(1)}, bf16[2,16,1024]{2,1,0:T(8,128)(2,1)S(1)}, u32[]{:S(2)}, u32[]{:S(2)}) collective-permute-start(bf16[2,16,1024]{2,1,0:T(8,128)(2,1)S(1)} %get-tuple-element.30), channel_id=1, source_target_pairs={{0,192},{1,193},{2,194},{3,195},{4,196},{5,197},{6,198},{7,199},{8... | collective-permute-start | bytes 196616 | tf_op jit(solution)/shard_map/ppermute | solution.py:43
  20.0 5.4 %collective-permute-start.5 = (s32[1,2]{1,0:T(1,128)}, s32[1,2]{1,0:T(1,128)S(1)}, u32[]{:S(2)}, u32[]{:S(2)}) collective-permute-start(s32[1,2]{1,0:T(1,128)} %param.14), channel_id=1, source_target_pairs={{0,16},{1,17},{2,18},{3,19},{4,20},{5,21},{6,22},{7,23},{8,24},{9,... | collective-permute-start | bytes 32 | tf_op jit(solution)/shard_map/ppermute | solution.py:43
  22.0 5.3 %collective-permute-start.6 = (s32[1,2]{1,0:T(1,128)}, s32[1,2]{1,0:T(1,128)S(1)}, u32[]{:S(2)}, u32[]{:S(2)}) collective-permute-start(s32[1,2]{1,0:T(1,128)} %param.14), channel_id=1, source_target_pairs={{0,32},{1,33},{2,34},{3,35},{4,36},{5,37},{6,38},{7,39},{8,40},{9,... | collective-permute-start | bytes 32 | tf_op jit(solution)/shard_map/ppermute | solution.py:43
  22.5 4.8 %collective-permute-start.7 = (s32[1,2]{1,0:T(1,128)}, s32[1,2]{1,0:T(1,128)S(1)}, u32[]{:S(2)}, u32[]{:S(2)}) collective-permute-start(s32[1,2]{1,0:T(1,128)} %param.14), channel_id=1, source_target_pairs={{0,48},{1,49},{2,50},{3,51},{4,52},{5,53},{6,54},{7,55},{8,56},{9,... | collective-permute-start | bytes 32 | tf_op jit(solution)/shard_map/ppermute | solution.py:43
  25.4 8.3 %collective-permute-start.10 = (bf16[4,2,16,1024]{3,2,1,0:T(8,128)(2,1)}, bf16[4,2,16,1024]{3,2,1,0:T(8,128)(2,1)}, u32[]{:S(2)}, u32[]{:S(2)}) collective-permute-start(bf16[4,2,16,1024]{3,2,1,0:T(8,128)(2,1)} %pad_maximum_fusion.mine), channel_id=1, source_target_pairs={{0,8},{1,9},{2,10},{3,11},{4,12},{5,13},{6,14},{7,15},{8,0},{9,1},... | collective-permute-start | bytes 786440 | tf_op jit(solution)/shard_map/ppermute | solution.py:43
  25.4 16.1 %collective-permute-start.11 = (bf16[256,1024]{1,0:T(8,128)(2,1)}, bf16[256,1024]{1,0:T(8,128)(2,1)S(1)}, u32[]{:S(2)}, u32[]{:S(2)}) collective-permute-start(bf16[256,1024]{1,0:T(8,128)(2,1)} %bitcast.23), channel_id=1, source_target_pairs={{0,2},{1,3},{2,0},{3,1},{4,6},{5,7},{6,4},{7,5},{8,10},{9,11},{10,... | collective-permute-start | bytes 1572872 | tf_op jit(solution)/shard_map/ppermute | solution.py:43
  28.7 29.4 %collective-permute-start.4 = (bf16[256,1024]{1,0:T(8,128)(2,1)}, bf16[256,1024]{1,0:T(8,128)(2,1)}, u32[]{:S(2)}, u32[]{:S(2)}) collective-permute-start(bf16[256,1024]{1,0:T(8,128)(2,1)} %bitcast.24), channel_id=1, source_target_pairs={{0,4},{1,5},{2,6},{3,7},{4,0},{5,1},{6,2},{7,3},{8,12},{9,13},{10,... | collective-permute-start | bytes 1572872 | tf_op jit(solution)/shard_map/ppermute | solution.py:43
  35.8 5.8 %collective-permute-start.12 = (bf16[2,2,16,1024]{3,2,1,0:T(8,128)(2,1)}, bf16[2,2,16,1024]{3,2,1,0:T(8,128)(2,1)S(1)}, u32[]{:S(2)}, u32[]{:S(2)}) collective-permute-start(bf16[2,2,16,1024]{3,2,1,0:T(8,128)(2,1)} %get-tuple-element.23), channel_id=1, source_target_pairs={{0,48},{1,49},{2,50},{3,51},{4,52},{5,53},{6,54},{7,55},{8,56},{9,... | collective-permute-start | bytes 393224 | tf_op jit(solution)/shard_map/ppermute | solution.py:43
  37.2 8.1 %collective-permute-start.13 = (bf16[2,2,16,1024]{3,2,1,0:T(8,128)(2,1)}, bf16[2,2,16,1024]{3,2,1,0:T(8,128)(2,1)S(1)}, u32[]{:S(2)}, u32[]{:S(2)}) collective-permute-start(bf16[2,2,16,1024]{3,2,1,0:T(8,128)(2,1)} %get-tuple-element.24), channel_id=1, source_target_pairs={{0,32},{1,33},{2,34},{3,35},{4,36},{5,37},{6,38},{7,39},{8,40},{9,... | collective-permute-start | bytes 393224 | tf_op jit(solution)/shard_map/ppermute | solution.py:43
  40.0 6.1 %collective-permute-start.14 = (bf16[2,2,16,1024]{3,2,1,0:T(8,128)(2,1)}, bf16[2,2,16,1024]{3,2,1,0:T(8,128)(2,1)}, u32[]{:S(2)}, u32[]{:S(2)}) collective-permute-start(bf16[2,2,16,1024]{3,2,1,0:T(8,128)(2,1)} %get-tuple-element.25), channel_id=1, source_target_pairs={{0,16},{1,17},{2,18},{3,19},{4,20},{5,21},{6,22},{7,23},{8,24},{9,... | collective-permute-start | bytes 393224 | tf_op jit(solution)/shard_map/ppermute | solution.py:43
  47.1 11.1 %collective-permute-start.15 = (bf16[2,2,16,1024]{3,2,1,0:T(8,128)(2,1)S(1)}, bf16[2,2,16,1024]{3,2,1,0:T(8,128)(2,1)S(1)}, u32[]{:S(2)}, u32[]{:S(2)}) collective-permute-start(bf16[2,2,16,1024]{3,2,1,0:T(8,128)(2,1)S(1)} %add_add_fusion.p0), channel_id=1, source_target_pairs={{0,1},{1,2},{2,3},{3,0},{4,5},{5,6},{6,7},{7,4},{8,9},{9,10},{10,1... | collective-permute-start | bytes 393224 | tf_op jit(solution)/shard_map/ppermute | solution.py:43
  47.8 13.7 %collective-permute-start.19 = (bf16[2,2,16,1024]{3,2,1,0:T(8,128)(2,1)S(1)}, bf16[2,2,16,1024]{3,2,1,0:T(8,128)(2,1)}, u32[]{:S(2)}, u32[]{:S(2)}) collective-permute-start(bf16[2,2,16,1024]{3,2,1,0:T(8,128)(2,1)S(1)} %add_add_fusion.p0), channel_id=1, source_target_pairs={{0,2},{1,3},{2,0},{3,1},{4,6},{5,7},{6,4},{7,5},{8,10},{9,11},{10,... | collective-permute-start | bytes 393224 | tf_op jit(solution)/shard_map/ppermute | solution.py:43
  50.1 11.4 %collective-permute-start.20 = (bf16[2,2,16,1024]{3,2,1,0:T(8,128)(2,1)S(1)}, bf16[2,2,16,1024]{3,2,1,0:T(8,128)(2,1)}, u32[]{:S(2)}, u32[]{:S(2)}) collective-permute-start(bf16[2,2,16,1024]{3,2,1,0:T(8,128)(2,1)S(1)} %add_add_fusion.p0), channel_id=1, source_target_pairs={{0,3},{1,0},{2,1},{3,2},{4,7},{5,4},{6,5},{7,6},{8,11},{9,8},{10,9... | collective-permute-start | bytes 393224 | tf_op jit(solution)/shard_map/ppermute | solution.py:43
  58.2 25.8 %collective-permute-start.16 = (bf16[256,1024]{1,0:T(8,128)(2,1)}, bf16[256,1024]{1,0:T(8,128)(2,1)S(1)}, u32[]{:S(2)}, u32[]{:S(2)}) collective-permute-start(bf16[256,1024]{1,0:T(8,128)(2,1)} %collective-permute-done.4.l0), channel_id=1, source_target_pairs={{0,1},{1,2},{2,3},{3,0},{4,5},{5,6},{6,7},{7,4},{8,9},{9,10},{10,1... | collective-permute-start | bytes 1572872 | tf_op jit(solution)/shard_map/ppermute | solution.py:43
  58.8 25.1 %collective-permute-start.17 = (bf16[256,1024]{1,0:T(8,128)(2,1)}, bf16[256,1024]{1,0:T(8,128)(2,1)S(1)}, u32[]{:S(2)}, u32[]{:S(2)}) collective-permute-start(bf16[256,1024]{1,0:T(8,128)(2,1)} %collective-permute-done.4.l0), channel_id=1, source_target_pairs={{0,2},{1,3},{2,0},{3,1},{4,6},{5,7},{6,4},{7,5},{8,10},{9,11},{10,... | collective-permute-start | bytes 1572872 | tf_op jit(solution)/shard_map/ppermute | solution.py:43
  60.7 23.9 %collective-permute-start.18 = (bf16[256,1024]{1,0:T(8,128)(2,1)}, bf16[256,1024]{1,0:T(8,128)(2,1)S(1)}, u32[]{:S(2)}, u32[]{:S(2)}) collective-permute-start(bf16[256,1024]{1,0:T(8,128)(2,1)} %collective-permute-done.4.l0), channel_id=1, source_target_pairs={{0,3},{1,0},{2,1},{3,2},{4,7},{5,4},{6,5},{7,6},{8,11},{9,8},{10,9... | collective-permute-start | bytes 1572872 | tf_op jit(solution)/shard_map/ppermute | solution.py:43
  61.5 2.8 %copy-start.1 = (bf16[1024,3072]{1,0:T(8,128)(2,1)S(1)}, bf16[1024,3072]{1,0:T(8,128)(2,1)}, u32[]{:S(2)}) copy-start(bf16[1024,3072]{1,0:T(8,128)(2,1)} %w_hbm.3) | copy-start | bytes 18874372
  64.3 20.2 %copy-start.2 = (bf16[1024,3072]{1,0:T(8,128)(2,1)S(1)}, bf16[1024,3072]{1,0:T(8,128)(2,1)}, u32[]{:S(2)}) copy-start(bf16[1024,3072]{1,0:T(8,128)(2,1)} %w_hbm.3) | copy-start | bytes 18874372
  64.3 20.2 %copy-start.3 = (bf16[1024,1024]{1,0:T(8,128)(2,1)S(1)}, bf16[1024,1024]{1,0:T(8,128)(2,1)}, u32[]{:S(2)}) copy-start(bf16[1024,1024]{1,0:T(8,128)(2,1)} %wo_ref.1) | copy-start | bytes 6291460

commit v3 on v2

v3 whole, which is shorter than its diff:
```python
import math

import jax
import jax.numpy as jnp
from jax import lax
from jax.experimental import pallas as pl
from jax.experimental.pallas import tpu as pltpu
from jax.sharding import Mesh
from jax.sharding import PartitionSpec as P

HEADS = 16
HEAD = 64
TEMB = 256
TSTEPS = 1000
D = 1024
FRAMES = 16
TOKF = 128
AXES = ("zl", "x", "core", "zh", "y")
ZL, X, CORE, ZH, Y = 4, 4, 2, 2, 4
ROWS = 256
PIECE = 16
PAIRS = HEADS // 2
F32 = jnp.float32
BF16 = jnp.bfloat16
QSCALE = HEAD ** (-0.5) * math.log2(math.e)


def moves(zl=0, x=0, core=0, zh=0, y=0):
    pairs = []
    for i in range(ZL * X * CORE * ZH * Y):
        rest, iy = divmod(i, Y)
        rest, izh = divmod(rest, ZH)
        rest, ic = divmod(rest, CORE)
        izl, ix = divmod(rest, X)
        izl, ix, ic = (izl + zl) % ZL, (ix + x) % X, (ic + core) % CORE
        izh, iy = (izh + zh) % ZH, (iy + y) % Y
        pairs.append((i, (((izl * X + ix) * CORE + ic) * ZH + izh) * Y + iy))
    return pairs


def send(value, **step):
    return lax.ppermute(value, AXES, moves(**step))


def after(value, earlier):
    return lax.optimization_barrier((value, earlier))[0]


def dot(a, b):
    return jnp.dot(a, b, preferred_element_type=F32)


def dot_tt(a, b):
    return lax.dot_general(a, b, (((0,), (1,)), ((), ())), preferred_element_type=F32)


def blend_tables(time_ref, pieces, first_s, diff_s):
    zh, y = lax.axis_index("zh"), lax.axis_index("y")
    kw = 1.0 - time_ref[0].astype(F32) * (1.0 / (2.0 * TSTEPS))
    for i, piece in enumerate(pieces):
        for z in range(ZH):
            slot = ((zh + z) % ZH) * Y + (y + Y - i) % Y
            base = pl.multiple_of(slot * PIECE, PIECE)
            first = piece[0, z].astype(F32) * kw
            last = piece[1, z].astype(F32) * kw
            first_s[pl.ds(base, PIECE), :] = first
            diff_s[pl.ds(base, PIECE), :] = last - first


def ramp_of(z, back, which):
    zh, y = lax.axis_index("zh"), lax.axis_index("y")
    frame = 2 * (((zh + z) % ZH) * Y + (y + Y - back) % Y) + which
    return frame.astype(F32) * (1.0 / (FRAMES - 1))


def norm_rows(j, i, step, source, lat_s, x_s, first_s, diff_s, gain_ref, shift_ref):
    rows = pl.ds(pl.multiple_of(j * ROWS + i * step, step), step)
    tok = pl.ds(pl.multiple_of(lax.rem(i, TOKF // step) * step, step), step)
    ramp = ramp_of(*source, i // (TOKF // step))
    resid = lat_s[rows, :].astype(F32) + (first_s[tok, :] + ramp * diff_s[tok, :])
    mean = jnp.mean(resid, axis=-1, keepdims=True)
    cent = resid - mean
    var = jnp.mean(cent * cent, axis=-1, keepdims=True)
    normed = cent * lax.rsqrt(var + 1e-06) * gain_ref[...] + shift_ref[...]
    x_s[rows, :] = normed.astype(BF16)


def norm_chunk(j, source, *refs):
    step = 32

    def rows(i, carry):
        norm_rows(j, i, step, source, *refs)
        return carry

    lax.fori_loop(0, ROWS // step, rows, 0, unroll=4)


def head_norm_t(block, gain):
    heads = block.reshape(block.shape[0] // HEAD, HEAD, block.shape[1])
    mean = jnp.mean(heads * heads, axis=1, keepdims=True)
    return (heads * lax.rsqrt(mean + 1e-06) * gain[None]).reshape(block.shape)


def keys_values(x_s, w_ref, kgain_ref, kt_s, v_s):
    rows = x_s.shape[0]
    wide = 512 if rows % 512 == 0 else 256

    def values(i, carry):
        f = pl.multiple_of(i * 512, 512)
        v_s[:, pl.ds(f, 512)] = dot(x_s[...], w_ref[:, pl.ds(2 * D + f, 512)]).astype(BF16)
        return carry

    def keys(i, carry):
        t = pl.multiple_of(i * wide, wide)
        kt = dot_tt(w_ref[:, D : 2 * D], x_s[pl.ds(t, wide), :])
        kt_s[:, pl.ds(t, wide)] = head_norm_t(kt, kgain_ref[...]).astype(BF16)
        return carry

    lax.fori_loop(0, rows // wide, keys, 0)
    lax.fori_loop(0, D // 512, values, 0)


def attend(q_s, kt_s, v_s, use):
    lane = lax.broadcasted_iota(jnp.int32, (ROWS, 128), 1) < HEAD
    lane_v = lax.broadcasted_iota(jnp.int32, (kt_s.shape[1], 128), 1) < HEAD
    one = jnp.ones((), BF16)
    zero = jnp.zeros((), BF16)

    def pair(p, carry):
        f = pl.multiple_of(p * 128, 128)
        qp = q_s[:, pl.ds(f, 128)]
        vp = v_s[:, pl.ds(f, 128)]
        kt = kt_s[pl.ds(f, 128), :]
        even = dot(
            jnp.exp2(dot(jnp.where(lane, qp, zero), kt)).astype(BF16), jnp.where(lane_v, vp, one)
        )
        odd = dot(
            jnp.exp2(dot(jnp.where(lane, zero, qp), kt)).astype(BF16), jnp.where(lane_v, one, vp)
        )
        use(p, even, odd)
        return carry

    lax.fori_loop(0, PAIRS, pair, 0, unroll=4)


def prepare(time_ref, lats, sources, pieces, gain_ref, shift_ref, rest, scr):
    piece_s, lat_s, first_s, diff_s, x_s, sems = scr
    targets = [piece_s.at[i] for i in range(len(pieces))]
    targets += [lat_s.at[pl.ds(j * ROWS, ROWS)] for j in range(len(lats))]
    copies = [
        pltpu.make_async_copy(source, target, sems.at[i])
        for i, (source, target) in enumerate(zip(pieces + lats, targets))
    ]
    for copy in copies + rest:
        copy.start()
    for copy in copies[: len(pieces)]:
        copy.wait()
    blend_tables(time_ref, targets[: len(pieces)], first_s, diff_s)
    for j in range(len(lats)):
        copies[len(pieces) + j].wait()
        norm_chunk(j, sources[j], lat_s, x_s, first_s, diff_s, gain_ref, shift_ref)


def prelude_kernel(embed_ref, mod_ref, norm_ref, qgain_ref, kgain_ref, w_ref, wo_ref, *out_refs):
    gain, shift, qgain, kgain = out_refs
    embed = jnp.broadcast_to(embed_ref[...], (16, TEMB))
    modulation = dot(embed, mod_ref[...])
    gain[...] = norm_ref[...] * (1.0 + modulation[:1, :D])
    shift[...] = modulation[:1, D:]
    qgain[...] = jnp.broadcast_to(qgain_ref[...] * QSCALE, (8, HEAD)).T[:, :1]
    kgain[...] = jnp.broadcast_to(kgain_ref[...], (8, HEAD)).T[:, :1]


def near_kernel(
    time_ref, l0, l1, l2, l3, l4, p0, p1, p2, p3, gain_ref, shift_ref, w_ref, qgain_ref, kgain_ref,
    acc_ref, q_ref, piece_s, lat_s, first_s, diff_s, x_s, sems, kt_s, v_s,
):
    prepare(
        time_ref, (l0, l1, l2, l3, l4), ((0, 0), (0, 1), (0, 2), (0, 3), (1, 0)), (p0, p1, p2, p3),
        gain_ref, shift_ref, [], (piece_s, lat_s, first_s, diff_s, x_s, sems),
    )
    qt = head_norm_t(dot_tt(w_ref[:, :D], x_s[:ROWS, :]), qgain_ref[...])
    q_ref[...] = qt.astype(BF16).T
    keys_values(x_s, w_ref, kgain_ref, kt_s, v_s)

    def use(p, even, odd):
        acc_ref[2 * p] = even
        acc_ref[2 * p + 1] = odd

    attend(q_ref, kt_s, v_s, use)


def far_kernel(
    time_ref, own, l0, l1, l2, p0, p1, p2, p3, gain_ref, shift_ref, w_ref, kgain_ref, wo_ref, q_ref,
    acc_ref, out_ref, piece_s, lat_s, first_s, diff_s, x_s, sems, kt_s, v_s, own_s, att_s, own_sem,
):
    rest = [pltpu.make_async_copy(own, own_s, own_sem)]
    prepare(
        time_ref, (l0, l1, l2), ((1, 1), (1, 2), (1, 3)), (p0, p1, p2, p3), gain_ref, shift_ref,
        rest, (piece_s, lat_s, first_s, diff_s, x_s, sems),
    )
    keys_values(x_s, w_ref, kgain_ref, kt_s, v_s)
    for copy in rest:
        copy.wait()
    lane = lax.broadcasted_iota(jnp.int32, (ROWS, 128), 1) < HEAD

    def use(p, even, odd):
        even = even + acc_ref[2 * p]
        odd = odd + acc_ref[2 * p + 1]
        total = pltpu.roll(jnp.where(lane, odd, even), HEAD, 1)
        f = pl.multiple_of(p * 128, 128)
        att_s[:, pl.ds(f, 128)] = (jnp.where(lane, even, odd) / total).astype(BF16)

    attend(q_ref, kt_s, v_s, use)

    def block(i, carry):
        f = pl.multiple_of(i * 256, 256)
        o = dot(att_s[...], wo_ref[:, pl.ds(f, 256)])
        for k in range(2):
            r = slice(k * TOKF, (k + 1) * TOKF)
            resid = own_s[r, pl.ds(f, 256)].astype(F32) + (
                first_s[:, pl.ds(f, 256)] + ramp_of(0, 0, k) * diff_s[:, pl.ds(f, 256)]
            )
            out_ref[r, pl.ds(f, 256)] = (resid + o[r]).astype(BF16)
        return carry

    lax.fori_loop(0, D // 256, block, 0)


def pick_kernel(pair_ref, other_ref, x0, x1, x2, x3, *out_refs):
    zl, x, core = lax.axis_index("zl"), lax.axis_index("x"), lax.axis_index("core")
    for wants, out_ref in zip((pair_ref, other_ref), out_refs):
        for k in range(2):
            wanted = wants[0, k]
            back = (x + X - wanted // CORE % X) % X
            entry = (zl + ZL - wanted // (X * CORE)) % ZL
            back = jnp.where(wanted % CORE == core, back, -1)

            @pl.when(back < 0)
            def _():
                out_ref[k] = jnp.zeros_like(out_ref[k])

            for t, held in enumerate((x0, x1, x2, x3)):

                @pl.when(back == t)
                def _():
                    out_ref[k] = held[entry]


VMEM = pl.BlockSpec(memory_space=pltpu.VMEM)
LIMIT = 32 * 1024 * 1024
SMEM = pl.BlockSpec(memory_space=pltpu.SMEM)
HBM = pl.BlockSpec(memory_space=pltpu.HBM)


def scratch(chunks):
    rows = chunks * ROWS
    return [
        pltpu.VMEM((Y, 2, ZH, PIECE, D), BF16),
        pltpu.VMEM((rows, D), BF16),
        pltpu.VMEM((TOKF, D), F32),
        pltpu.VMEM((TOKF, D), F32),
        pltpu.VMEM((rows, D), BF16),
        pltpu.SemaphoreType.DMA((Y + chunks,)),
        pltpu.VMEM((D, rows), BF16),
        pltpu.VMEM((rows, D), BF16),
    ]


def body(
    latents, keyframes, key_index, timesteps, mod_weight, norm_gain, qkv_weight, query_gain,
    key_gain, out_weight,
):
    own = latents.reshape(ROWS, D)
    mine = keyframes[0]
    pair = key_index

    near_1, near_3 = send(own, y=1), send(own, y=3)
    pair_other = send(key_index, core=1)
    planes = jnp.stack([after(mine, pair_other), send(mine, zh=1)])
    from_zl = [send(planes, zl=k) for k in (1, 2, 3)]
    by_zl = jnp.stack([planes] + from_zl)
    by_x = [by_zl] + [send(by_zl, x=k) for k in (1, 2, 3)]
    cross = send(after(own, from_zl), zh=1)
    near_2 = send(after(own, near_3), y=2)
    picked = jax.ShapeDtypeStruct((2, ZH, PIECE, D), BF16)
    held, asked = pl.pallas_call(
        pick_kernel,
        out_shape=(picked, picked),
        in_specs=[SMEM] * 2 + [VMEM] * 4,
        out_specs=(VMEM, VMEM),
        name="pick",
    )(key_index, after(pair_other, (near_1, near_3)), *by_x)
    both = after(held, near_2) + send(asked, core=1)
    pieces = [both] + [send(both, y=k) for k in (1, 2, 3)]
    late = after(cross, both)
    far_1, far_2, far_3 = [send(late, y=k) for k in (1, 2, 3)]

    halfway = TEMB // 2
    freqs = jnp.exp(-math.log(10000.0) * jnp.arange(halfway, dtype=F32) / halfway)
    angles = timesteps[1].astype(F32) * freqs
    embed = jnp.concatenate([jnp.sin(angles), jnp.cos(angles)]).astype(BF16)[None, :]
    gain, shift, qgain, kgain = pl.pallas_call(
        prelude_kernel,
        out_shape=(jax.ShapeDtypeStruct((1, D), F32),) * 2 + (jax.ShapeDtypeStruct((HEAD, 1), F32),) * 2,
        in_specs=[VMEM] * 7,
        out_specs=(VMEM,) * 4,
        compiler_params=pltpu.CompilerParams(vmem_limit_bytes=LIMIT),
        name="prelude",
    )(
        embed, mod_weight, norm_gain[None, :], query_gain[None, :], key_gain[None, :], qkv_weight,
        out_weight,
    )

    params = pltpu.CompilerParams(vmem_limit_bytes=LIMIT)
    cost = pl.CostEstimate(flops=6 << 30, bytes_accessed=12 << 20, transcendentals=4 << 20)
    acc, q = pl.pallas_call(
        near_kernel,
        out_shape=(
            jax.ShapeDtypeStruct((HEADS, ROWS, 128), F32),
            jax.ShapeDtypeStruct((ROWS, D), BF16),
        ),
        in_specs=[SMEM] + [HBM] * 9 + [VMEM] * 5,
        out_specs=(VMEM, VMEM),
        scratch_shapes=scratch(5),
        compiler_params=params,
        cost_estimate=cost,
        name="near_keys",
    )(
        timesteps, own, near_1, near_2, near_3, cross, *pieces, gain, shift,
        qkv_weight, qgain, kgain,
    )
    out = pl.pallas_call(
        far_kernel,
        out_shape=jax.ShapeDtypeStruct((ROWS, D), BF16),
        in_specs=[SMEM] + [HBM] * 8 + [VMEM] * 7,
        out_specs=VMEM,
        scratch_shapes=scratch(3) + [
            pltpu.VMEM((ROWS, D), BF16),
            pltpu.VMEM((ROWS, D), BF16),
            pltpu.SemaphoreType.DMA,
        ],
        compiler_params=params,
        cost_estimate=cost,
        name="far_keys",
    )(
        timesteps, own, far_1, far_2, far_3, *pieces, gain, shift, qkv_weight, kgain,
        out_weight, q, acc,
    )
    return out.reshape(latents.shape)


def solution(mesh):
    split = Mesh(mesh.devices.reshape(ZL, X, CORE, ZH, Y), AXES)
    leaf, seq = ("zl", "x", "core"), ("zh", "y")
    in_specs = (P(leaf, seq, None, None), P(leaf, seq, None), P(leaf, None)) + (P(),) * 7
    out_specs = P(leaf, seq, None, None)
    return jax.shard_map(body, mesh=split, in_specs=in_specs, out_specs=out_specs, check_vma=False)
```

time: 103 us -> 96.3 us (0.935)
  the two profiles are of different devices: /device:TPU:4 before, /device:TPU:34 now
where the time goes in v3:
time: 96.3 us; the launch traced here: 96 us
  starting transfers between devices  36 us (37%)
  Pallas kernels  34.9 us (36%)
  waiting for transfers between devices  15.8 us (16%)
  local copies, waits for them, and re-layouts  6.53 us (7%)
  other arithmetic  1.8 us (2%)
  between operations  0.97 us (1%)
    ppermute x19, starting transfers between devices, send(): return lax.ppermute(value, AXES, moves(**step))  36 us
    pallas_call x1, Pallas kernels, body(): pl.pallas_call(near_kernel, out_shape=(jax.ShapeDtypeStruct((HEADS, ROWS,...  18.6 us
    ppermute x19, waiting for transfers between devices, send(): return lax.ppermute(value, AXES, moves(**step))  15.8 us
    pallas_call x1, Pallas kernels, body(): pl.pallas_call(far_kernel, out_shape=jax.ShapeDtypeStruct((ROWS, D), BF16...  14 us
    unnamed x26, local copies, waits for them, and re-layouts  5.29 us
    pallas_call x1, Pallas kernels, body(): pl.pallas_call(pick_kernel, out_shape=(picked, picked), in_specs=[SMEM] *...  2.09 us
  transfers between devices with their start and end apart: 19, of which 8 were waited for; matrix products, arithmetic and copies ran while one was open for 3% of the time, Pallas kernels for 22%

profile of v3, /device:TPU:34, one launch (start us, length us, event | category | flops | bytes accessed | tf_op | source)
XLA Modules:
  0.0 96.0 jit_solution(16710098475214875103)
XLA Ops:
  0.0 0.0 copy-start.4
  0.0 0.0 copy-start.5
  0.0 0.0 copy-start.6
  0.0 0.0 copy-start.2
  0.0 3.1 %collective-permute-start.7 = (bf16[256,1024]{1,0:T(8,128)(2,1)}, bf16[256,1024]{1,0:T(8,128)(2,1)S(1)}, u32[]{:S(2)}, u32[]{:S(2)}) collective-permute-start(bf16[256,1024]{1,0:T(8,128)(2,1)} %bitcast.21), channel_id=1, source_target_pairs={{0,3},{1,0},{2,1},{3,2},{4,7},{5,4},{6,5},{7,6},{8,11},{9,8},{10,9... | collective-permute-start | bytes 1572872 | tf_op jit(solution)/shard_map/ppermute | solution.py:42
  3.1 0.0 collective-permute-start.6
  3.1 6.3 %collective-permute-start.1 = (bf16[16,1024]{1,0:T(8,128)(2,1)}, bf16[16,1024]{1,0:T(8,128)(2,1)S(1)}, u32[]{:S(2)}, u32[]{:S(2)}) collective-permute-start(bf16[16,1024]{1,0:T(8,128)(2,1)} %bitcast.30), channel_id=1, source_target_pairs={{0,4},{1,5},{2,6},{3,7},{4,0},{5,1},{6,2},{7,3},{8,12},{9,13},{10,... | collective-permute-start | bytes 98312 | tf_op jit(solution)/shard_map/ppermute | solution.py:42
  9.4 0.0 collective-permute-start
  9.4 1.3 %collective-permute-done.other_ref = s32[1,2]{1,0:T(1,128)S(1)} collective-permute-done((s32[1,2]{1,0:T(1,128)}, s32[1,2]{1,0:T(1,128)S(1)}, u32[]{:S(2)}, u32[]{:S(2)}) %collective-permute-start) | collective-permute-done | bytes 40 | tf_op jit(solution)/shard_map/ppermute | solution.py:42
  10.7 0.9 collective-permute-done.1
  11.5 0.8 fusion
  12.3 1.6 %collective-permute-start.2 = (bf16[2,16,1024]{2,1,0:T(8,128)(2,1)S(1)}, bf16[2,16,1024]{2,1,0:T(8,128)(2,1)S(1)}, u32[]{:S(2)}, u32[]{:S(2)}) collective-permute-start(bf16[2,16,1024]{2,1,0:T(8,128)(2,1)S(1)} %get-tuple-element.34), channel_id=1, source_target_pairs={{0,64},{1,65},{2,66},{3,67},{4,68},{5,69},{6,70},{7,71},{8,72},{9,... | collective-permute-start | bytes 196616 | tf_op jit(solution)/shard_map/ppermute | solution.py:42
  13.9 1.8 %collective-permute-start.3 = (bf16[2,16,1024]{2,1,0:T(8,128)(2,1)S(1)}, bf16[2,16,1024]{2,1,0:T(8,128)(2,1)S(1)}, u32[]{:S(2)}, u32[]{:S(2)}) collective-permute-start(bf16[2,16,1024]{2,1,0:T(8,128)(2,1)S(1)} %get-tuple-element.34), channel_id=1, source_target_pairs={{0,128},{1,129},{2,130},{3,131},{4,132},{5,133},{6,134},{7,135},{8... | collective-permute-start | bytes 196616 | tf_op jit(solution)/shard_map/ppermute | solution.py:42
  15.7 1.6 %collective-permute-start.4 = (bf16[2,16,1024]{2,1,0:T(8,128)(2,1)S(1)}, bf16[2,16,1024]{2,1,0:T(8,128)(2,1)S(1)}, u32[]{:S(2)}, u32[]{:S(2)}) collective-permute-start(bf16[2,16,1024]{2,1,0:T(8,128)(2,1)S(1)} %get-tuple-element.34), channel_id=1, source_target_pairs={{0,192},{1,193},{2,194},{3,195},{4,196},{5,197},{6,198},{7,199},{8... | collective-permute-start | bytes 196616 | tf_op jit(solution)/shard_map/ppermute | solution.py:42
  17.3 0.0 collective-permute-done.7.l3
  17.3 2.2 %collective-permute-start.11 = (bf16[256,1024]{1,0:T(8,128)(2,1)}, bf16[256,1024]{1,0:T(8,128)(2,1)}, u32[]{:S(2)}, u32[]{:S(2)}) collective-permute-start(bf16[256,1024]{1,0:T(8,128)(2,1)} %bitcast.23), channel_id=1, source_target_pairs={{0,2},{1,3},{2,0},{3,1},{4,6},{5,7},{6,4},{7,5},{8,10},{9,11},{10,... | collective-permute-start | bytes 1572872 | tf_op jit(solution)/shard_map/ppermute | solution.py:42
  19.5 0.0 collective-permute-done.2
  19.5 0.4 collective-permute-done.3
  19.9 1.2 %collective-permute-done.4 = bf16[2,16,1024]{2,1,0:T(8,128)(2,1)S(1)} collective-permute-done((bf16[2,16,1024]{2,1,0:T(8,128)(2,1)S(1)}, bf16[2,16,1024]{2,1,0:T(8,128)(2,1)S(1)}, u32[]{:S(2)}, u32[]{:S(2)}) %collective-permute-start.4) | collective-permute-done | bytes 65568 | tf_op jit(solution)/shard_map/ppermute | solution.py:42
  21.2 0.0 copy-start.9
  21.2 0.6 collective-permute-start.10
  21.8 1.5 %collective-permute-start.8 = (bf16[4,2,16,1024]{3,2,1,0:T(8,128)(2,1)S(1)}, bf16[4,2,16,1024]{3,2,1,0:T(8,128)(2,1)S(1)}, u32[]{:S(2)}, u32[]{:S(2)}) collective-permute-start(bf16[4,2,16,1024]{3,2,1,0:T(8,128)(2,1)S(1)} %pad_maximum_fusion.x0), channel_id=1, source_target_pairs={{0,16},{1,17},{2,18},{3,19},{4,20},{5,21},{6,22},{7,23},{8,24},{9,... | collective-permute-start | bytes 786440 | tf_op jit(solution)/shard_map/ppermute | solution.py:42
  23.3 3.3 %collective-permute-start.9 = (bf16[4,2,16,1024]{3,2,1,0:T(8,128)(2,1)S(1)}, bf16[4,2,16,1024]{3,2,1,0:T(8,128)(2,1)}, u32[]{:S(2)}, u32[]{:S(2)}) collective-permute-start(bf16[4,2,16,1024]{3,2,1,0:T(8,128)(2,1)S(1)} %pad_maximum_fusion.x0), channel_id=1, source_target_pairs={{0,32},{1,33},{2,34},{3,35},{4,36},{5,37},{6,38},{7,39},{8,40},{9,... | collective-permute-start | bytes 786440 | tf_op jit(solution)/shard_map/ppermute | solution.py:42
  26.6 0.0 collective-permute-done.6.l1
  26.6 5.0 %collective-permute-start.5 = (bf16[256,1024]{1,0:T(8,128)(2,1)}, bf16[256,1024]{1,0:T(8,128)(2,1)}, u32[]{:S(2)}, u32[]{:S(2)}) collective-permute-start(bf16[256,1024]{1,0:T(8,128)(2,1)} %bitcast.24), channel_id=1, source_target_pairs={{0,4},{1,5},{2,6},{3,7},{4,0},{5,1},{6,2},{7,3},{8,12},{9,13},{10,... | collective-permute-start | bytes 1572872 | tf_op jit(solution)/shard_map/ppermute | solution.py:42
  31.6 0.0 collective-permute-done.10.x3
  31.6 0.2 collective-permute-done.8.x1
  31.7 0.5 copy-done.10
  32.3 0.7 copy-done.11
  33.0 2.7 %collective-permute-done.9.x2 = bf16[4,2,16,1024]{3,2,1,0:T(8,128)(2,1)} collective-permute-done((bf16[4,2,16,1024]{3,2,1,0:T(8,128)(2,1)S(1)}, bf16[4,2,16,1024]{3,2,1,0:T(8,128)(2,1)}, u32[]{:S(2)}, u32[]{:S(2)}) %collective-permute-start.9) | collective-permute-done | bytes 262176 | tf_op jit(solution)/shard_map/ppermute | solution.py:42
  35.7 0.0 copy-done.12
  35.7 0.0 copy-done.9
  35.7 2.1 %pick.1 = (bf16[2,2,16,1024]{3,2,1,0:T(8,128)(2,1)}, bf16[2,2,16,1024]{3,2,1,0:T(8,128)(2,1)}) custom-call(s32[1,2]{1,0:T(1,128)} %pair_ref.1, s32[1,2]{1,0:T(1,128)} %copy-done.12, bf16[4,2,16,1024]{3,2,1,0:T(8,128)(2,1)} %copy-done.9, bf16[4,2,16,1024]{3,2,1,0:T(8,128)(2,1)} %copy-done.11, bf16[4,2,16,1024]{3,2,1,0:T(8,128)(2,1)} %collective-permute-done.9.x2, ...), custom_call_target="tpu_custom_call" | custom-call | tf_op jit(solution)/shard_map/pick/pallas_call | solution.py:287
  37.8 0.0 collective-permute-start.12
  37.8 1.2 %slice.3 = s32[1]{0:T(128)} slice(s32[2]{0:T(128)} %time_ref.3), slice={[1:2]} | slice | bytes 8 | tf_op jit(solution)/shard_map/slice | solution.py:301
  39.7 0.0 collective-permute-done.11.l2
  39.7 0.0 collective-permute-done.12
  39.7 0.9 add.3.p0
  40.6 0.6 collective-permute-start.16
  41.3 4.1 %collective-permute-start.17 = (bf16[2,2,16,1024]{3,2,1,0:T(8,128)(2,1)S(1)}, bf16[2,2,16,1024]{3,2,1,0:T(8,128)(2,1)S(1)}, u32[]{:S(2)}, u32[]{:S(2)}) collective-permute-start(bf16[2,2,16,1024]{3,2,1,0:T(8,128)(2,1)S(1)} %add.3.p0), channel_id=1, source_target_pairs={{0,2},{1,3},{2,0},{3,1},{4,6},{5,7},{6,4},{7,5},{8,10},{9,11},{10,... | collective-permute-start | bytes 393224 | tf_op jit(solution)/shard_map/ppermute | solution.py:42
  45.4 0.1 collective-permute-start.18
  45.6 0.0 copy-done.4
  45.6 0.0 copy-done.5
  45.6 0.0 copy-done.6
  45.6 0.0 copy-done.2
  45.6 0.0 copy-start
  45.6 2.8 %copy-done = bf16[1024,3072]{1,0:T(8,128)(2,1)S(1)} copy-done((bf16[1024,3072]{1,0:T(8,128)(2,1)S(1)}, bf16[1024,3072]{1,0:T(8,128)(2,1)}, u32[]{:S(2)}) %copy-start) | copy-done | bytes 6291480
  48.4 1.2 %copy-done.3 = bf16[256,2048]{1,0:T(8,128)(2,1)S(1)} copy-done((bf16[256,2048]{1,0:T(8,128)(2,1)S(1)}, bf16[256,2048]{1,0:T(8,128)(2,1)}, u32[]{:S(2)}) %copy-start.3) | copy-done | bytes 1048600
  49.6 0.2 prelude.1
  49.9 4.8 %collective-permute-done.5.l4 = bf16[256,1024]{1,0:T(8,128)(2,1)} collective-permute-done((bf16[256,1024]{1,0:T(8,128)(2,1)}, bf16[256,1024]{1,0:T(8,128)(2,1)}, u32[]{:S(2)}, u32[]{:S(2)}) %collective-permute-start.5) | collective-permute-done | bytes 524320 | tf_op jit(solution)/shard_map/ppermute | solution.py:42
  54.7 0.0 collective-permute-start.13
  54.7 4.0 %collective-permute-start.14 = (bf16[256,1024]{1,0:T(8,128)(2,1)}, bf16[256,1024]{1,0:T(8,128)(2,1)S(1)}, u32[]{:S(2)}, u32[]{:S(2)}) collective-permute-start(bf16[256,1024]{1,0:T(8,128)(2,1)} %collective-permute-done.5.l4), channel_id=1, source_target_pairs={{0,2},{1,3},{2,0},{3,1},{4,6},{5,7},{6,4},{7,5},{8,10},{9,11},{10,... | collective-permute-start | bytes 1572872 | tf_op jit(solution)/shard_map/ppermute | solution.py:42
  58.8 0.0 collective-permute-done.16.p1
  58.8 0.1 collective-permute-start.15
  58.9 0.0 collective-permute-done.17.p2
  58.9 0.0 collective-permute-done.18.p3
  58.9 0.0 copy-done.1
  58.9 0.0 copy-done.7
  58.9 0.0 copy-done.8
  58.9 18.6 %near_keys.1 = (f32[16,256,128]{2,1,0:T(8,128)S(1)}, bf16[256,1024]{1,0:T(8,128)(2,1)S(1)}) custom-call(s32[2]{0:T(128)S(1)} %copy-done.8, bf16[256,1024]{1,0:T(8,128)(2,1)S(1)} %bitcast.25, bf16[256,1024]{1,0:T(8,128)(2,1)S(1)} %collective-permute-done.6.l1, bf16[256,1024]{1,0:T(8,128)(2,1)} %collective-permute-done.11.l2, ...), custom_call_target="tpu_custom_call" | custom-call | flops 6442450944 | bytes 12582912 | tf_op jit(solution)/shard_map/near_keys/pallas_call | solution.py:317
  77.5 0.0 collective-permute-done.13.l0
  77.5 4.3 %collective-permute-done.14.l1 = bf16[256,1024]{1,0:T(8,128)(2,1)S(1)} collective-permute-done((bf16[256,1024]{1,0:T(8,128)(2,1)}, bf16[256,1024]{1,0:T(8,128)(2,1)S(1)}, u32[]{:S(2)}, u32[]{:S(2)}) %collective-permute-start.14) | collective-permute-done | bytes 524320 | tf_op jit(solution)/shard_map/ppermute | solution.py:42
  81.9 0.0 collective-permute-done.15.l2
  81.9 14.0 %far_keys.1 = bf16[256,1024]{1,0:T(8,128)(2,1)} custom-call(s32[2]{0:T(128)S(1)} %copy-done.8, bf16[256,1024]{1,0:T(8,128)(2,1)S(1)} %bitcast.26, bf16[256,1024]{1,0:T(8,128)(2,1)S(1)} %collective-permute-done.13.l0, bf16[256,1024]{1,0:T(8,128)(2,1)S(1)} %collective-permute-done.14.l1, bf16[256,1024]{1,0:T(8,128)(2,1)S(1)} %collective-permute-done.15.l2, ...), custom_call_target="tpu_custom_call" | custom-call | flops 6442450944 | bytes 12582912 | tf_op jit(solution)/shard_map/far_keys/pallas_call | solution.py:333
  (10 shorter events, 0.1 us)
Async XLA Ops:
  0.0 45.6 %copy-start.4 = (f32[1024]{0:T(1024)S(1)}, f32[1024]{0:T(1024)}, u32[]{:S(2)}) copy-start(f32[1024]{0:T(1024)} %param.15) | copy-start | bytes 12292
  0.0 45.6 %copy-start.5 = (f32[64]{0:T(128)S(1)}, f32[64]{0:T(128)}, u32[]{:S(2)}) copy-start(f32[64]{0:T(128)} %param.17) | copy-start | bytes 772
  0.0 45.6 %copy-start.6 = (f32[64]{0:T(128)S(1)}, f32[64]{0:T(128)}, u32[]{:S(2)}) copy-start(f32[64]{0:T(128)} %param.18) | copy-start | bytes 772
  0.0 45.6 %copy-start.2 = (bf16[1024,1024]{1,0:T(8,128)(2,1)S(1)}, bf16[1024,1024]{1,0:T(8,128)(2,1)}, u32[]{:S(2)}) copy-start(bf16[1024,1024]{1,0:T(8,128)(2,1)} %wo_ref.3) | copy-start | bytes 6291460
  0.0 17.3 %collective-permute-start.7 = (bf16[256,1024]{1,0:T(8,128)(2,1)}, bf16[256,1024]{1,0:T(8,128)(2,1)S(1)}, u32[]{:S(2)}, u32[]{:S(2)}) collective-permute-start(bf16[256,1024]{1,0:T(8,128)(2,1)} %bitcast.21), channel_id=1, source_target_pairs={{0,3},{1,0},{2,1},{3,2},{4,7},{5,4},{6,5},{7,6},{8,11},{9,8},{10,9... | collective-permute-start | bytes 1572872 | tf_op jit(solution)/shard_map/ppermute | solution.py:42
  3.1 23.5 %collective-permute-start.6 = (bf16[256,1024]{1,0:T(8,128)(2,1)}, bf16[256,1024]{1,0:T(8,128)(2,1)S(1)}, u32[]{:S(2)}, u32[]{:S(2)}) collective-permute-start(bf16[256,1024]{1,0:T(8,128)(2,1)} %bitcast.22), channel_id=1, source_target_pairs={{0,1},{1,2},{2,3},{3,0},{4,5},{5,6},{6,7},{7,4},{8,9},{9,10},{10,1... | collective-permute-start | bytes 1572872 | tf_op jit(solution)/shard_map/ppermute | solution.py:42
  3.1 8.4 %collective-permute-start.1 = (bf16[16,1024]{1,0:T(8,128)(2,1)}, bf16[16,1024]{1,0:T(8,128)(2,1)S(1)}, u32[]{:S(2)}, u32[]{:S(2)}) collective-permute-start(bf16[16,1024]{1,0:T(8,128)(2,1)} %bitcast.30), channel_id=1, source_target_pairs={{0,4},{1,5},{2,6},{3,7},{4,0},{5,1},{6,2},{7,3},{8,12},{9,13},{10,... | collective-permute-start | bytes 98312 | tf_op jit(solution)/shard_map/ppermute | solution.py:42
  9.4 1.3 %collective-permute-start = (s32[1,2]{1,0:T(1,128)}, s32[1,2]{1,0:T(1,128)S(1)}, u32[]{:S(2)}, u32[]{:S(2)}) collective-permute-start(s32[1,2]{1,0:T(1,128)} %pair_ref.1), channel_id=1, source_target_pairs={{0,8},{1,9},{2,10},{3,11},{4,12},{5,13},{6,14},{7,15},{8,0},{9,1},... | collective-permute-start | bytes 32 | tf_op jit(solution)/shard_map/ppermute | solution.py:42
  10.7 25.0 %copy-start.12 = (s32[1,2]{1,0:T(1,128)}, s32[1,2]{1,0:T(1,128)S(1)}, u32[]{:S(2)}) copy-start(s32[1,2]{1,0:T(1,128)S(1)} %collective-permute-done.other_ref) | copy-start | bytes 28
  12.3 7.2 %collective-permute-start.2 = (bf16[2,16,1024]{2,1,0:T(8,128)(2,1)S(1)}, bf16[2,16,1024]{2,1,0:T(8,128)(2,1)S(1)}, u32[]{:S(2)}, u32[]{:S(2)}) collective-permute-start(bf16[2,16,1024]{2,1,0:T(8,128)(2,1)S(1)} %get-tuple-element.34), channel_id=1, source_target_pairs={{0,64},{1,65},{2,66},{3,67},{4,68},{5,69},{6,70},{7,71},{8,72},{9,... | collective-permute-start | bytes 196616 | tf_op jit(solution)/shard_map/ppermute | solution.py:42
  13.9 6.0 %collective-permute-start.3 = (bf16[2,16,1024]{2,1,0:T(8,128)(2,1)S(1)}, bf16[2,16,1024]{2,1,0:T(8,128)(2,1)S(1)}, u32[]{:S(2)}, u32[]{:S(2)}) collective-permute-start(bf16[2,16,1024]{2,1,0:T(8,128)(2,1)S(1)} %get-tuple-element.34), channel_id=1, source_target_pairs={{0,128},{1,129},{2,130},{3,131},{4,132},{5,133},{6,134},{7,135},{8... | collective-permute-start | bytes 196616 | tf_op jit(solution)/shard_map/ppermute | solution.py:42
  15.7 5.4 %collective-permute-start.4 = (bf16[2,16,1024]{2,1,0:T(8,128)(2,1)S(1)}, bf16[2,16,1024]{2,1,0:T(8,128)(2,1)S(1)}, u32[]{:S(2)}, u32[]{:S(2)}) collective-permute-start(bf16[2,16,1024]{2,1,0:T(8,128)(2,1)S(1)} %get-tuple-element.34), channel_id=1, source_target_pairs={{0,192},{1,193},{2,194},{3,195},{4,196},{5,197},{6,198},{7,199},{8... | collective-permute-start | bytes 196616 | tf_op jit(solution)/shard_map/ppermute | solution.py:42
  17.3 22.4 %collective-permute-start.11 = (bf16[256,1024]{1,0:T(8,128)(2,1)}, bf16[256,1024]{1,0:T(8,128)(2,1)}, u32[]{:S(2)}, u32[]{:S(2)}) collective-permute-start(bf16[256,1024]{1,0:T(8,128)(2,1)} %bitcast.23), channel_id=1, source_target_pairs={{0,2},{1,3},{2,0},{3,1},{4,6},{5,7},{6,4},{7,5},{8,10},{9,11},{10,... | collective-permute-start | bytes 1572872 | tf_op jit(solution)/shard_map/ppermute | solution.py:42
  21.2 14.5 %copy-start.9 = (bf16[4,2,16,1024]{3,2,1,0:T(8,128)(2,1)}, bf16[4,2,16,1024]{3,2,1,0:T(8,128)(2,1)S(1)}, u32[]{:S(2)}) copy-start(bf16[4,2,16,1024]{3,2,1,0:T(8,128)(2,1)S(1)} %pad_maximum_fusion.x0) | copy-start | bytes 786436
  21.2 10.4 %collective-permute-start.10 = (bf16[4,2,16,1024]{3,2,1,0:T(8,128)(2,1)S(1)}, bf16[4,2,16,1024]{3,2,1,0:T(8,128)(2,1)S(1)}, u32[]{:S(2)}, u32[]{:S(2)}) collective-permute-start(bf16[4,2,16,1024]{3,2,1,0:T(8,128)(2,1)S(1)} %pad_maximum_fusion.x0), channel_id=1, source_target_pairs={{0,48},{1,49},{2,50},{3,51},{4,52},{5,53},{6,54},{7,55},{8,56},{9,... | collective-permute-start | bytes 786440 | tf_op jit(solution)/shard_map/ppermute | solution.py:42
  21.8 10.0 %collective-permute-start.8 = (bf16[4,2,16,1024]{3,2,1,0:T(8,128)(2,1)S(1)}, bf16[4,2,16,1024]{3,2,1,0:T(8,128)(2,1)S(1)}, u32[]{:S(2)}, u32[]{:S(2)}) collective-permute-start(bf16[4,2,16,1024]{3,2,1,0:T(8,128)(2,1)S(1)} %pad_maximum_fusion.x0), channel_id=1, source_target_pairs={{0,16},{1,17},{2,18},{3,19},{4,20},{5,21},{6,22},{7,23},{8,24},{9,... | collective-permute-start | bytes 786440 | tf_op jit(solution)/shard_map/ppermute | solution.py:42
  23.3 12.4 %collective-permute-start.9 = (bf16[4,2,16,1024]{3,2,1,0:T(8,128)(2,1)S(1)}, bf16[4,2,16,1024]{3,2,1,0:T(8,128)(2,1)}, u32[]{:S(2)}, u32[]{:S(2)}) collective-permute-start(bf16[4,2,16,1024]{3,2,1,0:T(8,128)(2,1)S(1)} %pad_maximum_fusion.x0), channel_id=1, source_target_pairs={{0,32},{1,33},{2,34},{3,35},{4,36},{5,37},{6,38},{7,39},{8,40},{9,... | collective-permute-start | bytes 786440 | tf_op jit(solution)/shard_map/ppermute | solution.py:42
  26.6 28.1 %collective-permute-start.5 = (bf16[256,1024]{1,0:T(8,128)(2,1)}, bf16[256,1024]{1,0:T(8,128)(2,1)}, u32[]{:S(2)}, u32[]{:S(2)}) collective-permute-start(bf16[256,1024]{1,0:T(8,128)(2,1)} %bitcast.24), channel_id=1, source_target_pairs={{0,4},{1,5},{2,6},{3,7},{4,0},{5,1},{6,2},{7,3},{8,12},{9,13},{10,... | collective-permute-start | bytes 1572872 | tf_op jit(solution)/shard_map/ppermute | solution.py:42
  31.6 0.7 copy-start.10
  32.3 0.7 copy-start.11
  37.8 1.9 %collective-permute-start.12 = (bf16[2,2,16,1024]{3,2,1,0:T(8,128)(2,1)}, bf16[2,2,16,1024]{3,2,1,0:T(8,128)(2,1)S(1)}, u32[]{:S(2)}, u32[]{:S(2)}) collective-permute-start(bf16[2,2,16,1024]{3,2,1,0:T(8,128)(2,1)} %get-tuple-element.25), channel_id=1, source_target_pairs={{0,8},{1,9},{2,10},{3,11},{4,12},{5,13},{6,14},{7,15},{8,0},{9,1},... | collective-permute-start | bytes 393224 | tf_op jit(solution)/shard_map/ppermute | solution.py:42
  40.6 18.1 %collective-permute-start.16 = (bf16[2,2,16,1024]{3,2,1,0:T(8,128)(2,1)S(1)}, bf16[2,2,16,1024]{3,2,1,0:T(8,128)(2,1)S(1)}, u32[]{:S(2)}, u32[]{:S(2)}) collective-permute-start(bf16[2,2,16,1024]{3,2,1,0:T(8,128)(2,1)S(1)} %add.3.p0), channel_id=1, source_target_pairs={{0,1},{1,2},{2,3},{3,0},{4,5},{5,6},{6,7},{7,4},{8,9},{9,10},{10,1... | collective-permute-start | bytes 393224 | tf_op jit(solution)/shard_map/ppermute | solution.py:42
  41.3 17.6 %collective-permute-start.17 = (bf16[2,2,16,1024]{3,2,1,0:T(8,128)(2,1)S(1)}, bf16[2,2,16,1024]{3,2,1,0:T(8,128)(2,1)S(1)}, u32[]{:S(2)}, u32[]{:S(2)}) collective-permute-start(bf16[2,2,16,1024]{3,2,1,0:T(8,128)(2,1)S(1)} %add.3.p0), channel_id=1, source_target_pairs={{0,2},{1,3},{2,0},{3,1},{4,6},{5,7},{6,4},{7,5},{8,10},{9,11},{10,... | collective-permute-start | bytes 393224 | tf_op jit(solution)/shard_map/ppermute | solution.py:42
  45.4 13.5 %collective-permute-start.18 = (bf16[2,2,16,1024]{3,2,1,0:T(8,128)(2,1)S(1)}, bf16[2,2,16,1024]{3,2,1,0:T(8,128)(2,1)S(1)}, u32[]{:S(2)}, u32[]{:S(2)}) collective-permute-start(bf16[2,2,16,1024]{3,2,1,0:T(8,128)(2,1)S(1)} %add.3.p0), channel_id=1, source_target_pairs={{0,3},{1,0},{2,1},{3,2},{4,7},{5,4},{6,5},{7,6},{8,11},{9,8},{10,9... | collective-permute-start | bytes 393224 | tf_op jit(solution)/shard_map/ppermute | solution.py:42
  45.6 2.8 %copy-start = (bf16[1024,3072]{1,0:T(8,128)(2,1)S(1)}, bf16[1024,3072]{1,0:T(8,128)(2,1)}, u32[]{:S(2)}) copy-start(bf16[1024,3072]{1,0:T(8,128)(2,1)} %w_ref.5) | copy-start | bytes 18874372
  48.4 1.2 %copy-start.3 = (bf16[256,2048]{1,0:T(8,128)(2,1)S(1)}, bf16[256,2048]{1,0:T(8,128)(2,1)}, u32[]{:S(2)}) copy-start(bf16[256,2048]{1,0:T(8,128)(2,1)} %mod_ref.1) | copy-start | bytes 3145732
  49.6 9.3 %copy-start.1 = (bf16[1024,3072]{1,0:T(8,128)(2,1)S(1)}, bf16[1024,3072]{1,0:T(8,128)(2,1)}, u32[]{:S(2)}) copy-start(bf16[1024,3072]{1,0:T(8,128)(2,1)} %w_ref.5) | copy-start | bytes 18874372
  49.6 9.3 %copy-start.7 = (bf16[1,2,128,1024]{3,2,1,0:T(8,128)(2,1)S(1)}, bf16[1,2,128,1024]{3,2,1,0:T(8,128)(2,1)}, u32[]{:S(2)}) copy-start(bf16[1,2,128,1024]{3,2,1,0:T(8,128)(2,1)} %param.10) | copy-start | bytes 1572868
  49.6 9.3 %copy-start.8 = (s32[2]{0:T(128)S(1)}, s32[2]{0:T(128)}, u32[]{:S(2)}) copy-start(s32[2]{0:T(128)} %time_ref.3) | copy-start | bytes 28
  54.7 22.8 %collective-permute-start.13 = (bf16[256,1024]{1,0:T(8,128)(2,1)}, bf16[256,1024]{1,0:T(8,128)(2,1)S(1)}, u32[]{:S(2)}, u32[]{:S(2)}) collective-permute-start(bf16[256,1024]{1,0:T(8,128)(2,1)} %collective-permute-done.5.l4), channel_id=1, source_target_pairs={{0,1},{1,2},{2,3},{3,0},{4,5},{5,6},{6,7},{7,4},{8,9},{9,10},{10,1... | collective-permute-start | bytes 1572872 | tf_op jit(solution)/shard_map/ppermute | solution.py:42
  54.7 27.1 %collective-permute-start.14 = (bf16[256,1024]{1,0:T(8,128)(2,1)}, bf16[256,1024]{1,0:T(8,128)(2,1)S(1)}, u32[]{:S(2)}, u32[]{:S(2)}) collective-permute-start(bf16[256,1024]{1,0:T(8,128)(2,1)} %collective-permute-done.5.l4), channel_id=1, source_target_pairs={{0,2},{1,3},{2,0},{3,1},{4,6},{5,7},{6,4},{7,5},{8,10},{9,11},{10,... | collective-permute-start | bytes 1572872 | tf_op jit(solution)/shard_map/ppermute | solution.py:42
  58.8 23.1 %collective-permute-start.15 = (bf16[256,1024]{1,0:T(8,128)(2,1)}, bf16[256,1024]{1,0:T(8,128)(2,1)S(1)}, u32[]{:S(2)}, u32[]{:S(2)}) collective-permute-start(bf16[256,1024]{1,0:T(8,128)(2,1)} %collective-permute-done.5.l4), channel_id=1, source_target_pairs={{0,3},{1,0},{2,1},{3,2},{4,7},{5,4},{6,5},{7,6},{8,11},{9,8},{10,9... | collective-permute-start | bytes 1572872 | tf_op jit(solution)/shard_map/ppermute | solution.py:42

commit v4 on v3

--- a/solution.py
+++ b/solution.py
@@ -92,7 +92,7 @@
         norm_rows(j, i, step, source, *refs)
         return carry
 
-    lax.fori_loop(0, ROWS // step, rows, 0, unroll=4)
+    lax.fori_loop(0, ROWS // step, rows, 0, unroll=8)
 
 
 def head_norm_t(block, gain):
@@ -102,25 +102,12 @@
 
 
 def keys_values(x_s, w_ref, kgain_ref, kt_s, v_s):
-    rows = x_s.shape[0]
-    wide = 512 if rows % 512 == 0 else 256
-
-    def values(i, carry):
-        f = pl.multiple_of(i * 512, 512)
-        v_s[:, pl.ds(f, 512)] = dot(x_s[...], w_ref[:, pl.ds(2 * D + f, 512)]).astype(BF16)
-        return carry
-
-    def keys(i, carry):
-        t = pl.multiple_of(i * wide, wide)
-        kt = dot_tt(w_ref[:, D : 2 * D], x_s[pl.ds(t, wide), :])
-        kt_s[:, pl.ds(t, wide)] = head_norm_t(kt, kgain_ref[...]).astype(BF16)
-        return carry
-
-    lax.fori_loop(0, rows // wide, keys, 0)
-    lax.fori_loop(0, D // 512, values, 0)
-
-
-def attend(q_s, kt_s, v_s, use):
+    kt = dot_tt(w_ref[:, D : 2 * D], x_s[...])
+    kt_s[...] = head_norm_t(kt, kgain_ref[...]).astype(BF16)
+    v_s[...] = dot(x_s[...], w_ref[:, 2 * D :]).astype(BF16)
+
+
+def attend(q_s, kt_s, v_s, use, unroll):
     lane = lax.broadcasted_iota(jnp.int32, (ROWS, 128), 1) < HEAD
     lane_v = lax.broadcasted_iota(jnp.int32, (kt_s.shape[1], 128), 1) < HEAD
     one = jnp.ones((), BF16)
@@ -140,7 +127,7 @@
         use(p, even, odd)
         return carry
 
-    lax.fori_loop(0, PAIRS, pair, 0, unroll=4)
+    lax.fori_loop(0, PAIRS, pair, 0, unroll=unroll)
 
 
 def prepare(time_ref, lats, sources, pieces, gain_ref, shift_ref, rest, scr):
@@ -171,12 +158,12 @@
     kgain[...] = jnp.broadcast_to(kgain_ref[...], (8, HEAD)).T[:, :1]
 
 
-def near_kernel(
-    time_ref, l0, l1, l2, l3, l4, p0, p1, p2, p3, gain_ref, shift_ref, w_ref, qgain_ref, kgain_ref,
+def first_kernel(
+    time_ref, l0, l1, l2, p0, p1, p2, p3, gain_ref, shift_ref, w_ref, qgain_ref, kgain_ref,
     acc_ref, q_ref, piece_s, lat_s, first_s, diff_s, x_s, sems, kt_s, v_s,
 ):
     prepare(
-        time_ref, (l0, l1, l2, l3, l4), ((0, 0), (0, 1), (0, 2), (0, 3), (1, 0)), (p0, p1, p2, p3),
+        time_ref, (l0, l1, l2), ((0, 0), (0, 1), (0, 3)), (p0, p1, p2, p3),
         gain_ref, shift_ref, [], (piece_s, lat_s, first_s, diff_s, x_s, sems),
     )
     qt = head_norm_t(dot_tt(w_ref[:, :D], x_s[:ROWS, :]), qgain_ref[...])
@@ -187,16 +174,33 @@
         acc_ref[2 * p] = even
         acc_ref[2 * p + 1] = odd
 
-    attend(q_ref, kt_s, v_s, use)
-
-
-def far_kernel(
-    time_ref, own, l0, l1, l2, p0, p1, p2, p3, gain_ref, shift_ref, w_ref, kgain_ref, wo_ref, q_ref,
+    attend(q_ref, kt_s, v_s, use, 8)
+
+
+def middle_kernel(
+    time_ref, l0, l1, l2, l3, p0, p1, p2, p3, gain_ref, shift_ref, w_ref, kgain_ref, q_ref, acc_ref,
+    sum_ref, piece_s, lat_s, first_s, diff_s, x_s, sems, kt_s, v_s,
+):
+    prepare(
+        time_ref, (l0, l1, l2, l3), ((0, 2), (1, 0), (1, 1), (1, 3)), (p0, p1, p2, p3),
+        gain_ref, shift_ref, [], (piece_s, lat_s, first_s, diff_s, x_s, sems),
+    )
+    keys_values(x_s, w_ref, kgain_ref, kt_s, v_s)
+
+    def use(p, even, odd):
+        sum_ref[2 * p] = even + acc_ref[2 * p]
+        sum_ref[2 * p + 1] = odd + acc_ref[2 * p + 1]
+
+    attend(q_ref, kt_s, v_s, use, 8)
+
+
+def last_kernel(
+    time_ref, own, l0, p0, p1, p2, p3, gain_ref, shift_ref, w_ref, kgain_ref, wo_ref, q_ref,
     acc_ref, out_ref, piece_s, lat_s, first_s, diff_s, x_s, sems, kt_s, v_s, own_s, att_s, own_sem,
 ):
     rest = [pltpu.make_async_copy(own, own_s, own_sem)]
     prepare(
-        time_ref, (l0, l1, l2), ((1, 1), (1, 2), (1, 3)), (p0, p1, p2, p3), gain_ref, shift_ref,
+        time_ref, (l0,), ((1, 2),), (p0, p1, p2, p3), gain_ref, shift_ref,
         rest, (piece_s, lat_s, first_s, diff_s, x_s, sems),
     )
     keys_values(x_s, w_ref, kgain_ref, kt_s, v_s)
@@ -211,7 +215,7 @@
         f = pl.multiple_of(p * 128, 128)
         att_s[:, pl.ds(f, 128)] = (jnp.where(lane, even, odd) / total).astype(BF16)
 
-    attend(q_ref, kt_s, v_s, use)
+    attend(q_ref, kt_s, v_s, use, 4)
 
     def block(i, carry):
         f = pl.multiple_of(i * 256, 256)
@@ -282,7 +286,7 @@
     by_zl = jnp.stack([planes] + from_zl)
     by_x = [by_zl] + [send(by_zl, x=k) for k in (1, 2, 3)]
     cross = send(after(own, from_zl), zh=1)
-    near_2 = send(after(own, near_3), y=2)
+    near_2 = send(after(own, (near_1, near_3)), y=2)
     picked = jax.ShapeDtypeStruct((2, ZH, PIECE, D), BF16)
     held, asked = pl.pallas_call(
         pick_kernel,
@@ -293,8 +297,7 @@
     )(key_index, after(pair_other, (near_1, near_3)), *by_x)
     both = after(held, near_2) + send(asked, core=1)
     pieces = [both] + [send(both, y=k) for k in (1, 2, 3)]
-    late = after(cross, both)
-    far_1, far_2, far_3 = [send(late, y=k) for k in (1, 2, 3)]
+    far_1, far_3 = [send(after(cross, both), y=k) for k in (1, 3)]
 
     halfway = TEMB // 2
     freqs = jnp.exp(-math.log(10000.0) * jnp.arange(halfway, dtype=F32) / halfway)
@@ -313,39 +316,47 @@
     )
 
     params = pltpu.CompilerParams(vmem_limit_bytes=LIMIT)
-    cost = pl.CostEstimate(flops=6 << 30, bytes_accessed=12 << 20, transcendentals=4 << 20)
+    cost = pl.CostEstimate(flops=4 << 30, bytes_accessed=8 << 20, transcendentals=3 << 20)
+    sums = jax.ShapeDtypeStruct((HEADS, ROWS, 128), F32)
+    token = jax.ShapeDtypeStruct((ROWS, D), BF16)
     acc, q = pl.pallas_call(
-        near_kernel,
-        out_shape=(
-            jax.ShapeDtypeStruct((HEADS, ROWS, 128), F32),
-            jax.ShapeDtypeStruct((ROWS, D), BF16),
-        ),
-        in_specs=[SMEM] + [HBM] * 9 + [VMEM] * 5,
+        first_kernel,
+        out_shape=(sums, token),
+        in_specs=[SMEM] + [HBM] * 7 + [VMEM] * 5,
         out_specs=(VMEM, VMEM),
-        scratch_shapes=scratch(5),
+        scratch_shapes=scratch(3),
         compiler_params=params,
         cost_estimate=cost,
-        name="near_keys",
+        name="first_keys",
+    )(timesteps, own, near_1, near_3, *pieces, gain, shift, qkv_weight, qgain, kgain)
+    far_2 = send(after(cross, acc), y=2)
+    acc = pl.pallas_call(
+        middle_kernel,
+        out_shape=sums,
+        in_specs=[SMEM] + [HBM] * 8 + [VMEM] * 6,
+        out_specs=VMEM,
+        scratch_shapes=scratch(4),
+        compiler_params=params,
+        cost_estimate=cost,
+        name="middle_keys",
     )(
-        timesteps, own, near_1, near_2, near_3, cross, *pieces, gain, shift,
-        qkv_weight, qgain, kgain,
+        timesteps, near_2, cross, far_1, far_3, *pieces, gain, shift, qkv_weight, kgain, q, acc,
     )
     out = pl.pallas_call(
-        far_kernel,
-        out_shape=jax.ShapeDtypeStruct((ROWS, D), BF16),
-        in_specs=[SMEM] + [HBM] * 8 + [VMEM] * 7,
+        last_kernel,
+        out_shape=token,
+        in_specs=[SMEM] + [HBM] * 6 + [VMEM] * 7,
         out_specs=VMEM,
-        scratch_shapes=scratch(3) + [
+        scratch_shapes=scratch(1) + [
             pltpu.VMEM((ROWS, D), BF16),
             pltpu.VMEM((ROWS, D), BF16),
             pltpu.SemaphoreType.DMA,
         ],
         compiler_params=params,
         cost_estimate=cost,
-        name="far_keys",
+        name="last_keys",
     )(
-        timesteps, own, far_1, far_2, far_3, *pieces, gain, shift, qkv_weight, kgain,
-        out_weight, q, acc,
+        timesteps, own, far_2, *pieces, gain, shift, qkv_weight, kgain, out_weight, q, acc,
     )
     return out.reshape(latents.shape)
 

time: 96.3 us -> 92 us (0.955)
  the two profiles are of different devices: /device:TPU:34 before, /device:TPU:2 now
where the time goes in v4:
time: 92 us; the launch traced here: 91.2 us
  starting transfers between devices  35.2 us (38%)
  Pallas kernels  33.7 us (37%)
  waiting for transfers between devices  13.5 us (15%)
  local copies, waits for them, and re-layouts  5.98 us (6%)
  other arithmetic  1.8 us (2%)
  between operations  1.03 us (1%)
    ppermute x19, starting transfers between devices, send(): return lax.ppermute(value, AXES, moves(**step))  35.2 us
    ppermute x19, waiting for transfers between devices, send(): return lax.ppermute(value, AXES, moves(**step))  13.5 us
    pallas_call x1, Pallas kernels, body(): pl.pallas_call(middle_kernel, out_shape=sums, in_specs=[SMEM] + [HBM] * 8...  13 us
    pallas_call x1, Pallas kernels, body(): pl.pallas_call(first_kernel, out_shape=(sums, token), in_specs=[SMEM] + [...  10.6 us
    pallas_call x1, Pallas kernels, body(): pl.pallas_call(last_kernel, out_shape=token, in_specs=[SMEM] + [HBM] * 6...  7.75 us
    unnamed x26, local copies, waits for them, and re-layouts  4.75 us
    pallas_call x1, Pallas kernels, body(): pl.pallas_call(pick_kernel, out_shape=(picked, picked), in_specs=[SMEM] *...  2.09 us
  transfers between devices with their start and end apart: 19, of which 9 were waited for; matrix products, arithmetic and copies ran while one was open for 3% of the time, Pallas kernels for 28%

profile of v4, /device:TPU:2, one launch (start us, length us, event | category | flops | bytes accessed | tf_op | source)
XLA Modules:
  0.0 91.2 jit_solution(8081198934892399264)
XLA Ops:
  0.0 0.0 copy-start.2
  0.0 0.0 copy-start.6
  0.0 0.0 copy-start.4
  0.0 3.1 %collective-permute-start.7 = (bf16[256,1024]{1,0:T(8,128)(2,1)}, bf16[256,1024]{1,0:T(8,128)(2,1)S(1)}, u32[]{:S(2)}, u32[]{:S(2)}) collective-permute-start(bf16[256,1024]{1,0:T(8,128)(2,1)} %bitcast.21), channel_id=1, source_target_pairs={{0,3},{1,0},{2,1},{3,2},{4,7},{5,4},{6,5},{7,6},{8,11},{9,8},{10,9... | collective-permute-start | bytes 1572872 | tf_op jit(solution)/shard_map/ppermute | solution.py:42
  3.1 0.0 collective-permute-start.6
  3.1 7.2 %collective-permute-start.1 = (bf16[16,1024]{1,0:T(8,128)(2,1)}, bf16[16,1024]{1,0:T(8,128)(2,1)S(1)}, u32[]{:S(2)}, u32[]{:S(2)}) collective-permute-start(bf16[16,1024]{1,0:T(8,128)(2,1)} %bitcast.30), channel_id=1, source_target_pairs={{0,4},{1,5},{2,6},{3,7},{4,0},{5,1},{6,2},{7,3},{8,12},{9,13},{10,... | collective-permute-start | bytes 98312 | tf_op jit(solution)/shard_map/ppermute | solution.py:42
  10.3 0.0 collective-permute-start
  10.3 1.3 %collective-permute-done.other_ref = s32[1,2]{1,0:T(1,128)S(1)} collective-permute-done((s32[1,2]{1,0:T(1,128)}, s32[1,2]{1,0:T(1,128)S(1)}, u32[]{:S(2)}, u32[]{:S(2)}) %collective-permute-start) | collective-permute-done | bytes 40 | tf_op jit(solution)/shard_map/ppermute | solution.py:42
  11.6 0.8 collective-permute-done.1
  12.4 0.8 fusion
  13.2 3.4 %collective-permute-start.4 = (bf16[2,16,1024]{2,1,0:T(8,128)(2,1)S(1)}, bf16[2,16,1024]{2,1,0:T(8,128)(2,1)S(1)}, u32[]{:S(2)}, u32[]{:S(2)}) collective-permute-start(bf16[2,16,1024]{2,1,0:T(8,128)(2,1)S(1)} %get-tuple-element.36), channel_id=1, source_target_pairs={{0,192},{1,193},{2,194},{3,195},{4,196},{5,197},{6,198},{7,199},{8... | collective-permute-start | bytes 196616 | tf_op jit(solution)/shard_map/ppermute | solution.py:42
  16.6 0.0 collective-permute-start.3
  16.6 0.7 collective-permute-start.2
  17.3 0.0 collective-permute-done.7.l2
  17.3 0.6 collective-permute-done.6.l1
  17.9 1.6 %collective-permute-start.11 = (bf16[256,1024]{1,0:T(8,128)(2,1)}, bf16[256,1024]{1,0:T(8,128)(2,1)}, u32[]{:S(2)}, u32[]{:S(2)}) collective-permute-start(bf16[256,1024]{1,0:T(8,128)(2,1)} %bitcast.23), channel_id=1, source_target_pairs={{0,2},{1,3},{2,0},{3,1},{4,6},{5,7},{6,4},{7,5},{8,10},{9,11},{10,... | collective-permute-start | bytes 1572872 | tf_op jit(solution)/shard_map/ppermute | solution.py:42
  19.5 0.0 collective-permute-done.4
  19.5 2.3 %collective-permute-done.3 = bf16[2,16,1024]{2,1,0:T(8,128)(2,1)S(1)} collective-permute-done((bf16[2,16,1024]{2,1,0:T(8,128)(2,1)S(1)}, bf16[2,16,1024]{2,1,0:T(8,128)(2,1)S(1)}, u32[]{:S(2)}, u32[]{:S(2)}) %collective-permute-start.3) | collective-permute-done | bytes 65568 | tf_op jit(solution)/shard_map/ppermute | solution.py:42
  21.8 0.9 collective-permute-done.2
  22.7 0.0 copy-start.9
  22.7 0.6 collective-permute-start.10
  23.4 2.4 %collective-permute-start.9 = (bf16[4,2,16,1024]{3,2,1,0:T(8,128)(2,1)S(1)}, bf16[4,2,16,1024]{3,2,1,0:T(8,128)(2,1)S(1)}, u32[]{:S(2)}, u32[]{:S(2)}) collective-permute-start(bf16[4,2,16,1024]{3,2,1,0:T(8,128)(2,1)S(1)} %pad_maximum_fusion.x0), channel_id=1, source_target_pairs={{0,32},{1,33},{2,34},{3,35},{4,36},{5,37},{6,38},{7,39},{8,40},{9,... | collective-permute-start | bytes 786440 | tf_op jit(solution)/shard_map/ppermute | solution.py:42
  25.8 1.8 %collective-permute-start.8 = (bf16[4,2,16,1024]{3,2,1,0:T(8,128)(2,1)S(1)}, bf16[4,2,16,1024]{3,2,1,0:T(8,128)(2,1)}, u32[]{:S(2)}, u32[]{:S(2)}) collective-permute-start(bf16[4,2,16,1024]{3,2,1,0:T(8,128)(2,1)S(1)} %pad_maximum_fusion.x0), channel_id=1, source_target_pairs={{0,16},{1,17},{2,18},{3,19},{4,20},{5,21},{6,22},{7,23},{8,24},{9,... | collective-permute-start | bytes 786440 | tf_op jit(solution)/shard_map/ppermute | solution.py:42
  27.6 5.2 %collective-permute-start.5 = (bf16[256,1024]{1,0:T(8,128)(2,1)}, bf16[256,1024]{1,0:T(8,128)(2,1)}, u32[]{:S(2)}, u32[]{:S(2)}) collective-permute-start(bf16[256,1024]{1,0:T(8,128)(2,1)} %bitcast.24), channel_id=1, source_target_pairs={{0,4},{1,5},{2,6},{3,7},{4,0},{5,1},{6,2},{7,3},{8,12},{9,13},{10,... | collective-permute-start | bytes 1572872 | tf_op jit(solution)/shard_map/ppermute | solution.py:42
  32.8 0.0 collective-permute-done.10.x3
  32.8 2.8 %collective-permute-done.9.x2 = bf16[4,2,16,1024]{3,2,1,0:T(8,128)(2,1)S(1)} collective-permute-done((bf16[4,2,16,1024]{3,2,1,0:T(8,128)(2,1)S(1)}, bf16[4,2,16,1024]{3,2,1,0:T(8,128)(2,1)S(1)}, u32[]{:S(2)}, u32[]{:S(2)}) %collective-permute-start.9) | collective-permute-done | bytes 262176 | tf_op jit(solution)/shard_map/ppermute | solution.py:42
  35.5 0.0 copy-done.10
  35.5 0.7 copy-done.11
  36.2 0.3 collective-permute-done.8.x1
  36.5 0.0 copy-done.12
  36.5 0.0 copy-done.9
  36.5 2.1 %pick.1 = (bf16[2,2,16,1024]{3,2,1,0:T(8,128)(2,1)}, bf16[2,2,16,1024]{3,2,1,0:T(8,128)(2,1)}) custom-call(s32[1,2]{1,0:T(1,128)} %pair_ref.1, s32[1,2]{1,0:T(1,128)} %copy-done.12, bf16[4,2,16,1024]{3,2,1,0:T(8,128)(2,1)} %copy-done.9, bf16[4,2,16,1024]{3,2,1,0:T(8,128)(2,1)} %collective-permute-done.8.x1, bf16[4,2,16,1024]{3,2,1,0:T(8,128)(2,1)} %copy-done.11, ...), custom_call_target="tpu_custom_call" | custom-call | tf_op jit(solution)/shard_map/pick/pallas_call | solution.py:291
  38.6 0.0 collective-permute-start.12
  38.6 1.2 %slice.3 = s32[1]{0:T(128)} slice(s32[2]{0:T(128)} %time_ref.5), slice={[1:2]} | slice | bytes 8 | tf_op jit(solution)/shard_map/slice | solution.py:304
  40.5 0.0 collective-permute-done.11.l0
  40.5 0.0 collective-permute-done.12
  40.5 0.9 %add.3.p0 = bf16[2,2,16,1024]{3,2,1,0:T(8,128)(2,1)S(1)} add(bf16[2,2,16,1024]{3,2,1,0:T(8,128)(2,1)} %get-tuple-element.25, bf16[2,2,16,1024]{3,2,1,0:T(8,128)(2,1)S(1)} %collective-permute-done.12) | non-fusion elementwise | flops 65536 | bytes 393216 | tf_op jit(solution)/shard_map/add | solution.py:298
  41.5 3.3 %collective-permute-start.15 = (bf16[2,2,16,1024]{3,2,1,0:T(8,128)(2,1)S(1)}, bf16[2,2,16,1024]{3,2,1,0:T(8,128)(2,1)S(1)}, u32[]{:S(2)}, u32[]{:S(2)}) collective-permute-start(bf16[2,2,16,1024]{3,2,1,0:T(8,128)(2,1)S(1)} %add.3.p0), channel_id=1, source_target_pairs={{0,3},{1,0},{2,1},{3,2},{4,7},{5,4},{6,5},{7,6},{8,11},{9,8},{10,9... | collective-permute-start | bytes 393224 | tf_op jit(solution)/shard_map/ppermute | solution.py:42
  44.8 0.0 collective-permute-start.14
  44.8 1.0 %collective-permute-start.13 = (bf16[2,2,16,1024]{3,2,1,0:T(8,128)(2,1)S(1)}, bf16[2,2,16,1024]{3,2,1,0:T(8,128)(2,1)S(1)}, u32[]{:S(2)}, u32[]{:S(2)}) collective-permute-start(bf16[2,2,16,1024]{3,2,1,0:T(8,128)(2,1)S(1)} %add.3.p0), channel_id=1, source_target_pairs={{0,1},{1,2},{2,3},{3,0},{4,5},{5,6},{6,7},{7,4},{8,9},{9,10},{10,1... | collective-permute-start | bytes 393224 | tf_op jit(solution)/shard_map/ppermute | solution.py:42
  45.8 0.0 copy-done.2
  45.8 0.0 copy-done.6
  45.8 0.0 copy-done.5
  45.8 0.0 copy-done.4
  45.9 0.0 copy-start
  45.9 2.8 %copy-done = bf16[1024,3072]{1,0:T(8,128)(2,1)S(1)} copy-done((bf16[1024,3072]{1,0:T(8,128)(2,1)S(1)}, bf16[1024,3072]{1,0:T(8,128)(2,1)}, u32[]{:S(2)}) %copy-start) | copy-done | bytes 6291480
  48.6 1.2 %copy-done.3 = bf16[256,2048]{1,0:T(8,128)(2,1)S(1)} copy-done((bf16[256,2048]{1,0:T(8,128)(2,1)S(1)}, bf16[256,2048]{1,0:T(8,128)(2,1)}, u32[]{:S(2)}) %copy-start.3) | copy-done | bytes 1048600
  49.9 0.2 prelude.1
  50.1 4.0 %collective-permute-done.5.l1 = bf16[256,1024]{1,0:T(8,128)(2,1)} collective-permute-done((bf16[256,1024]{1,0:T(8,128)(2,1)}, bf16[256,1024]{1,0:T(8,128)(2,1)}, u32[]{:S(2)}, u32[]{:S(2)}) %collective-permute-start.5) | collective-permute-done | bytes 524320 | tf_op jit(solution)/shard_map/ppermute | solution.py:42
  54.1 3.2 %collective-permute-start.18 = (bf16[256,1024]{1,0:T(8,128)(2,1)}, bf16[256,1024]{1,0:T(8,128)(2,1)S(1)}, u32[]{:S(2)}, u32[]{:S(2)}) collective-permute-start(bf16[256,1024]{1,0:T(8,128)(2,1)} %collective-permute-done.5.l1), channel_id=1, source_target_pairs={{0,3},{1,0},{2,1},{3,2},{4,7},{5,4},{6,5},{7,6},{8,11},{9,8},{10,9... | collective-permute-start | bytes 1572872 | tf_op jit(solution)/shard_map/ppermute | solution.py:42
  57.3 0.0 collective-permute-start.17
  57.3 0.0 collective-permute-done.15.p3
  57.3 0.0 collective-permute-done.14.p2
  57.3 0.0 collective-permute-done.13.p1
  57.3 0.0 copy-done.1
  57.3 0.0 copy-done.7
  57.3 0.0 copy-done.8
  57.3 10.6 %first_keys.1 = (f32[16,256,128]{2,1,0:T(8,128)S(1)}, bf16[256,1024]{1,0:T(8,128)(2,1)S(1)}) custom-call(s32[2]{0:T(128)S(1)} %copy-done.8, bf16[256,1024]{1,0:T(8,128)(2,1)S(1)} %bitcast.25, bf16[256,1024]{1,0:T(8,128)(2,1)S(1)} %collective-permute-done.6.l1, bf16[256,1024]{1,0:T(8,128)(2,1)S(1)} %collective-permute-done.7.l2, ...), custom_call_target="tpu_custom_call" | custom-call | flops 4294967296 | bytes 8388608 | tf_op jit(solution)/shard_map/first_keys/pallas_call | solution.py:322
  67.9 1.8 %collective-permute-start.16 = (bf16[256,1024]{1,0:T(8,128)(2,1)}, bf16[256,1024]{1,0:T(8,128)(2,1)S(1)}, u32[]{:S(2)}, u32[]{:S(2)}) collective-permute-start(bf16[256,1024]{1,0:T(8,128)(2,1)} %collective-permute-done.5.l1), channel_id=1, source_target_pairs={{0,2},{1,3},{2,0},{3,1},{4,6},{5,7},{6,4},{7,5},{8,10},{9,11},{10,... | collective-permute-start | bytes 1572872 | tf_op jit(solution)/shard_map/ppermute | solution.py:42
  69.7 0.0 collective-permute-done.18.l3
  69.7 0.5 collective-permute-done.17.l2
  70.2 13.0 %middle_keys.1.acc_ref = f32[16,256,128]{2,1,0:T(8,128)S(1)} custom-call(s32[2]{0:T(128)S(1)} %copy-done.8, bf16[256,1024]{1,0:T(8,128)(2,1)} %collective-permute-done.11.l0, bf16[256,1024]{1,0:T(8,128)(2,1)} %collective-permute-done.5.l1, bf16[256,1024]{1,0:T(8,128)(2,1)S(1)} %collective-permute-done.17.l2, ...), custom_call_target="tpu_custom_call" | custom-call | flops 4294967296 | bytes 8388608 | tf_op jit(solution)/shard_map/middle_keys/pallas_call | solution.py:333
  83.2 0.0 collective-permute-done.16.l0
  83.2 7.7 %last_keys.1 = bf16[256,1024]{1,0:T(8,128)(2,1)} custom-call(s32[2]{0:T(128)S(1)} %copy-done.8, bf16[256,1024]{1,0:T(8,128)(2,1)S(1)} %bitcast.26, bf16[256,1024]{1,0:T(8,128)(2,1)S(1)} %collective-permute-done.16.l0, bf16[2,2,16,1024]{3,2,1,0:T(8,128)(2,1)S(1)} %add.3.p0, bf16[2,2,16,1024]{3,2,1,0:T(8,128)(2,1)S(1)} %collective-permute-done.13.p1, ...), custom_call_target="tpu_custom_call" | custom-call | flops 4294967296 | bytes 8388608 | tf_op jit(solution)/shard_map/last_keys/pallas_call | solution.py:345
  (11 shorter events, 0.1 us)
Async XLA Ops:
  0.0 45.8 %copy-start.2 = (bf16[1024,1024]{1,0:T(8,128)(2,1)S(1)}, bf16[1024,1024]{1,0:T(8,128)(2,1)}, u32[]{:S(2)}) copy-start(bf16[1024,1024]{1,0:T(8,128)(2,1)} %wo_ref.3) | copy-start | bytes 6291460
  0.0 45.8 %copy-start.6 = (f32[64]{0:T(128)S(1)}, f32[64]{0:T(128)}, u32[]{:S(2)}) copy-start(f32[64]{0:T(128)} %param.18) | copy-start | bytes 772
  0.0 45.8 %copy-start.5 = (f32[64]{0:T(128)S(1)}, f32[64]{0:T(128)}, u32[]{:S(2)}) copy-start(f32[64]{0:T(128)} %param.17) | copy-start | bytes 772
  0.0 45.8 %copy-start.4 = (f32[1024]{0:T(1024)S(1)}, f32[1024]{0:T(1024)}, u32[]{:S(2)}) copy-start(f32[1024]{0:T(1024)} %param.15) | copy-start | bytes 12292
  0.0 17.3 %collective-permute-start.7 = (bf16[256,1024]{1,0:T(8,128)(2,1)}, bf16[256,1024]{1,0:T(8,128)(2,1)S(1)}, u32[]{:S(2)}, u32[]{:S(2)}) collective-permute-start(bf16[256,1024]{1,0:T(8,128)(2,1)} %bitcast.21), channel_id=1, source_target_pairs={{0,3},{1,0},{2,1},{3,2},{4,7},{5,4},{6,5},{7,6},{8,11},{9,8},{10,9... | collective-permute-start | bytes 1572872 | tf_op jit(solution)/shard_map/ppermute | solution.py:42
  3.1 14.8 %collective-permute-start.6 = (bf16[256,1024]{1,0:T(8,128)(2,1)}, bf16[256,1024]{1,0:T(8,128)(2,1)S(1)}, u32[]{:S(2)}, u32[]{:S(2)}) collective-permute-start(bf16[256,1024]{1,0:T(8,128)(2,1)} %bitcast.22), channel_id=1, source_target_pairs={{0,1},{1,2},{2,3},{3,0},{4,5},{5,6},{6,7},{7,4},{8,9},{9,10},{10,1... | collective-permute-start | bytes 1572872 | tf_op jit(solution)/shard_map/ppermute | solution.py:42
  3.1 9.3 %collective-permute-start.1 = (bf16[16,1024]{1,0:T(8,128)(2,1)}, bf16[16,1024]{1,0:T(8,128)(2,1)S(1)}, u32[]{:S(2)}, u32[]{:S(2)}) collective-permute-start(bf16[16,1024]{1,0:T(8,128)(2,1)} %bitcast.30), channel_id=1, source_target_pairs={{0,4},{1,5},{2,6},{3,7},{4,0},{5,1},{6,2},{7,3},{8,12},{9,13},{10,... | collective-permute-start | bytes 98312 | tf_op jit(solution)/shard_map/ppermute | solution.py:42
  10.3 1.3 %collective-permute-start = (s32[1,2]{1,0:T(1,128)}, s32[1,2]{1,0:T(1,128)S(1)}, u32[]{:S(2)}, u32[]{:S(2)}) collective-permute-start(s32[1,2]{1,0:T(1,128)} %pair_ref.1), channel_id=1, source_target_pairs={{0,8},{1,9},{2,10},{3,11},{4,12},{5,13},{6,14},{7,15},{8,0},{9,1},... | collective-permute-start | bytes 32 | tf_op jit(solution)/shard_map/ppermute | solution.py:42
  11.6 25.0 %copy-start.12 = (s32[1,2]{1,0:T(1,128)}, s32[1,2]{1,0:T(1,128)S(1)}, u32[]{:S(2)}) copy-start(s32[1,2]{1,0:T(1,128)S(1)} %collective-permute-done.other_ref) | copy-start | bytes 28
  13.2 6.3 %collective-permute-start.4 = (bf16[2,16,1024]{2,1,0:T(8,128)(2,1)S(1)}, bf16[2,16,1024]{2,1,0:T(8,128)(2,1)S(1)}, u32[]{:S(2)}, u32[]{:S(2)}) collective-permute-start(bf16[2,16,1024]{2,1,0:T(8,128)(2,1)S(1)} %get-tuple-element.36), channel_id=1, source_target_pairs={{0,192},{1,193},{2,194},{3,195},{4,196},{5,197},{6,198},{7,199},{8... | collective-permute-start | bytes 196616 | tf_op jit(solution)/shard_map/ppermute | solution.py:42
  16.6 5.2 %collective-permute-start.3 = (bf16[2,16,1024]{2,1,0:T(8,128)(2,1)S(1)}, bf16[2,16,1024]{2,1,0:T(8,128)(2,1)S(1)}, u32[]{:S(2)}, u32[]{:S(2)}) collective-permute-start(bf16[2,16,1024]{2,1,0:T(8,128)(2,1)S(1)} %get-tuple-element.36), channel_id=1, source_target_pairs={{0,128},{1,129},{2,130},{3,131},{4,132},{5,133},{6,134},{7,135},{8... | collective-permute-start | bytes 196616 | tf_op jit(solution)/shard_map/ppermute | solution.py:42
  16.6 6.1 %collective-permute-start.2 = (bf16[2,16,1024]{2,1,0:T(8,128)(2,1)S(1)}, bf16[2,16,1024]{2,1,0:T(8,128)(2,1)S(1)}, u32[]{:S(2)}, u32[]{:S(2)}) collective-permute-start(bf16[2,16,1024]{2,1,0:T(8,128)(2,1)S(1)} %get-tuple-element.36), channel_id=1, source_target_pairs={{0,64},{1,65},{2,66},{3,67},{4,68},{5,69},{6,70},{7,71},{8,72},{9,... | collective-permute-start | bytes 196616 | tf_op jit(solution)/shard_map/ppermute | solution.py:42
  17.9 22.6 %collective-permute-start.11 = (bf16[256,1024]{1,0:T(8,128)(2,1)}, bf16[256,1024]{1,0:T(8,128)(2,1)}, u32[]{:S(2)}, u32[]{:S(2)}) collective-permute-start(bf16[256,1024]{1,0:T(8,128)(2,1)} %bitcast.23), channel_id=1, source_target_pairs={{0,2},{1,3},{2,0},{3,1},{4,6},{5,7},{6,4},{7,5},{8,10},{9,11},{10,... | collective-permute-start | bytes 1572872 | tf_op jit(solution)/shard_map/ppermute | solution.py:42
  22.7 13.8 %copy-start.9 = (bf16[4,2,16,1024]{3,2,1,0:T(8,128)(2,1)}, bf16[4,2,16,1024]{3,2,1,0:T(8,128)(2,1)S(1)}, u32[]{:S(2)}) copy-start(bf16[4,2,16,1024]{3,2,1,0:T(8,128)(2,1)S(1)} %pad_maximum_fusion.x0) | copy-start | bytes 786436
  22.7 10.0 %collective-permute-start.10 = (bf16[4,2,16,1024]{3,2,1,0:T(8,128)(2,1)S(1)}, bf16[4,2,16,1024]{3,2,1,0:T(8,128)(2,1)S(1)}, u32[]{:S(2)}, u32[]{:S(2)}) collective-permute-start(bf16[4,2,16,1024]{3,2,1,0:T(8,128)(2,1)S(1)} %pad_maximum_fusion.x0), channel_id=1, source_target_pairs={{0,48},{1,49},{2,50},{3,51},{4,52},{5,53},{6,54},{7,55},{8,56},{9,... | collective-permute-start | bytes 786440 | tf_op jit(solution)/shard_map/ppermute | solution.py:42
  23.4 12.2 %collective-permute-start.9 = (bf16[4,2,16,1024]{3,2,1,0:T(8,128)(2,1)S(1)}, bf16[4,2,16,1024]{3,2,1,0:T(8,128)(2,1)S(1)}, u32[]{:S(2)}, u32[]{:S(2)}) collective-permute-start(bf16[4,2,16,1024]{3,2,1,0:T(8,128)(2,1)S(1)} %pad_maximum_fusion.x0), channel_id=1, source_target_pairs={{0,32},{1,33},{2,34},{3,35},{4,36},{5,37},{6,38},{7,39},{8,40},{9,... | collective-permute-start | bytes 786440 | tf_op jit(solution)/shard_map/ppermute | solution.py:42
  25.8 10.8 %collective-permute-start.8 = (bf16[4,2,16,1024]{3,2,1,0:T(8,128)(2,1)S(1)}, bf16[4,2,16,1024]{3,2,1,0:T(8,128)(2,1)}, u32[]{:S(2)}, u32[]{:S(2)}) collective-permute-start(bf16[4,2,16,1024]{3,2,1,0:T(8,128)(2,1)S(1)} %pad_maximum_fusion.x0), channel_id=1, source_target_pairs={{0,16},{1,17},{2,18},{3,19},{4,20},{5,21},{6,22},{7,23},{8,24},{9,... | collective-permute-start | bytes 786440 | tf_op jit(solution)/shard_map/ppermute | solution.py:42
  27.6 26.6 %collective-permute-start.5 = (bf16[256,1024]{1,0:T(8,128)(2,1)}, bf16[256,1024]{1,0:T(8,128)(2,1)}, u32[]{:S(2)}, u32[]{:S(2)}) collective-permute-start(bf16[256,1024]{1,0:T(8,128)(2,1)} %bitcast.24), channel_id=1, source_target_pairs={{0,4},{1,5},{2,6},{3,7},{4,0},{5,1},{6,2},{7,3},{8,12},{9,13},{10,... | collective-permute-start | bytes 1572872 | tf_op jit(solution)/shard_map/ppermute | solution.py:42
  32.8 2.8 %copy-start.10 = (bf16[4,2,16,1024]{3,2,1,0:T(8,128)(2,1)}, bf16[4,2,16,1024]{3,2,1,0:T(8,128)(2,1)S(1)}, u32[]{:S(2)}) copy-start(bf16[4,2,16,1024]{3,2,1,0:T(8,128)(2,1)S(1)} %collective-permute-done.10.x3) | copy-start | bytes 786436
  35.5 0.7 copy-start.11
  38.6 1.9 %collective-permute-start.12 = (bf16[2,2,16,1024]{3,2,1,0:T(8,128)(2,1)}, bf16[2,2,16,1024]{3,2,1,0:T(8,128)(2,1)S(1)}, u32[]{:S(2)}, u32[]{:S(2)}) collective-permute-start(bf16[2,2,16,1024]{3,2,1,0:T(8,128)(2,1)} %get-tuple-element.26), channel_id=1, source_target_pairs={{0,8},{1,9},{2,10},{3,11},{4,12},{5,13},{6,14},{7,15},{8,0},{9,1},... | collective-permute-start | bytes 393224 | tf_op jit(solution)/shard_map/ppermute | solution.py:42
  41.5 15.8 %collective-permute-start.15 = (bf16[2,2,16,1024]{3,2,1,0:T(8,128)(2,1)S(1)}, bf16[2,2,16,1024]{3,2,1,0:T(8,128)(2,1)S(1)}, u32[]{:S(2)}, u32[]{:S(2)}) collective-permute-start(bf16[2,2,16,1024]{3,2,1,0:T(8,128)(2,1)S(1)} %add.3.p0), channel_id=1, source_target_pairs={{0,3},{1,0},{2,1},{3,2},{4,7},{5,4},{6,5},{7,6},{8,11},{9,8},{10,9... | collective-permute-start | bytes 393224 | tf_op jit(solution)/shard_map/ppermute | solution.py:42
  44.8 12.5 %collective-permute-start.14 = (bf16[2,2,16,1024]{3,2,1,0:T(8,128)(2,1)S(1)}, bf16[2,2,16,1024]{3,2,1,0:T(8,128)(2,1)S(1)}, u32[]{:S(2)}, u32[]{:S(2)}) collective-permute-start(bf16[2,2,16,1024]{3,2,1,0:T(8,128)(2,1)S(1)} %add.3.p0), channel_id=1, source_target_pairs={{0,2},{1,3},{2,0},{3,1},{4,6},{5,7},{6,4},{7,5},{8,10},{9,11},{10,... | collective-permute-start | bytes 393224 | tf_op jit(solution)/shard_map/ppermute | solution.py:42
  44.8 12.5 %collective-permute-start.13 = (bf16[2,2,16,1024]{3,2,1,0:T(8,128)(2,1)S(1)}, bf16[2,2,16,1024]{3,2,1,0:T(8,128)(2,1)S(1)}, u32[]{:S(2)}, u32[]{:S(2)}) collective-permute-start(bf16[2,2,16,1024]{3,2,1,0:T(8,128)(2,1)S(1)} %add.3.p0), channel_id=1, source_target_pairs={{0,1},{1,2},{2,3},{3,0},{4,5},{5,6},{6,7},{7,4},{8,9},{9,10},{10,1... | collective-permute-start | bytes 393224 | tf_op jit(solution)/shard_map/ppermute | solution.py:42
  45.9 2.8 %copy-start = (bf16[1024,3072]{1,0:T(8,128)(2,1)S(1)}, bf16[1024,3072]{1,0:T(8,128)(2,1)}, u32[]{:S(2)}) copy-start(bf16[1024,3072]{1,0:T(8,128)(2,1)} %w_ref.7) | copy-start | bytes 18874372
  48.6 1.2 %copy-start.3 = (bf16[256,2048]{1,0:T(8,128)(2,1)S(1)}, bf16[256,2048]{1,0:T(8,128)(2,1)}, u32[]{:S(2)}) copy-start(bf16[256,2048]{1,0:T(8,128)(2,1)} %mod_ref.1) | copy-start | bytes 3145732
  49.9 7.4 %copy-start.1 = (bf16[1024,3072]{1,0:T(8,128)(2,1)S(1)}, bf16[1024,3072]{1,0:T(8,128)(2,1)}, u32[]{:S(2)}) copy-start(bf16[1024,3072]{1,0:T(8,128)(2,1)} %w_ref.7) | copy-start | bytes 18874372
  49.9 7.5 %copy-start.7 = (bf16[1,2,128,1024]{3,2,1,0:T(8,128)(2,1)S(1)}, bf16[1,2,128,1024]{3,2,1,0:T(8,128)(2,1)}, u32[]{:S(2)}) copy-start(bf16[1,2,128,1024]{3,2,1,0:T(8,128)(2,1)} %param.10) | copy-start | bytes 1572868
  49.9 7.5 %copy-start.8 = (s32[2]{0:T(128)S(1)}, s32[2]{0:T(128)}, u32[]{:S(2)}) copy-start(s32[2]{0:T(128)} %time_ref.5) | copy-start | bytes 28
  54.1 15.6 %collective-permute-start.18 = (bf16[256,1024]{1,0:T(8,128)(2,1)}, bf16[256,1024]{1,0:T(8,128)(2,1)S(1)}, u32[]{:S(2)}, u32[]{:S(2)}) collective-permute-start(bf16[256,1024]{1,0:T(8,128)(2,1)} %collective-permute-done.5.l1), channel_id=1, source_target_pairs={{0,3},{1,0},{2,1},{3,2},{4,7},{5,4},{6,5},{7,6},{8,11},{9,8},{10,9... | collective-permute-start | bytes 1572872 | tf_op jit(solution)/shard_map/ppermute | solution.py:42
  57.3 12.9 %collective-permute-start.17 = (bf16[256,1024]{1,0:T(8,128)(2,1)}, bf16[256,1024]{1,0:T(8,128)(2,1)S(1)}, u32[]{:S(2)}, u32[]{:S(2)}) collective-permute-start(bf16[256,1024]{1,0:T(8,128)(2,1)} %collective-permute-done.5.l1), channel_id=1, source_target_pairs={{0,1},{1,2},{2,3},{3,0},{4,5},{5,6},{6,7},{7,4},{8,9},{9,10},{10,1... | collective-permute-start | bytes 1572872 | tf_op jit(solution)/shard_map/ppermute | solution.py:42
  67.9 15.3 %collective-permute-start.16 = (bf16[256,1024]{1,0:T(8,128)(2,1)}, bf16[256,1024]{1,0:T(8,128)(2,1)S(1)}, u32[]{:S(2)}, u32[]{:S(2)}) collective-permute-start(bf16[256,1024]{1,0:T(8,128)(2,1)} %collective-permute-done.5.l1), channel_id=1, source_target_pairs={{0,2},{1,3},{2,0},{3,1},{4,6},{5,7},{6,4},{7,5},{8,10},{9,11},{10,... | collective-permute-start | bytes 1572872 | tf_op jit(solution)/shard_map/ppermute | solution.py:42

commit v5 on v4

--- a/solution.py
+++ b/solution.py
@@ -130,22 +130,18 @@
     lax.fori_loop(0, PAIRS, pair, 0, unroll=unroll)
 
 
-def prepare(time_ref, lats, sources, pieces, gain_ref, shift_ref, rest, scr):
-    piece_s, lat_s, first_s, diff_s, x_s, sems = scr
-    targets = [piece_s.at[i] for i in range(len(pieces))]
-    targets += [lat_s.at[pl.ds(j * ROWS, ROWS)] for j in range(len(lats))]
-    copies = [
-        pltpu.make_async_copy(source, target, sems.at[i])
-        for i, (source, target) in enumerate(zip(pieces + lats, targets))
+def prepare(lats, sources, first, diff, gain_ref, shift_ref, copies, scr, between):
+    lat_s, x_s, sems = scr
+    lat_copies = [
+        pltpu.make_async_copy(lat, lat_s.at[pl.ds(j * ROWS, ROWS)], sems.at[j])
+        for j, lat in enumerate(lats)
     ]
-    for copy in copies + rest:
+    for copy in copies + lat_copies:
         copy.start()
-    for copy in copies[: len(pieces)]:
+    between()
+    for j, copy in enumerate(lat_copies):
         copy.wait()
-    blend_tables(time_ref, targets[: len(pieces)], first_s, diff_s)
-    for j in range(len(lats)):
-        copies[len(pieces) + j].wait()
-        norm_chunk(j, sources[j], lat_s, x_s, first_s, diff_s, gain_ref, shift_ref)
+        norm_chunk(j, sources[j], lat_s, x_s, first, diff, gain_ref, shift_ref)
 
 
 def prelude_kernel(embed_ref, mod_ref, norm_ref, qgain_ref, kgain_ref, w_ref, wo_ref, *out_refs):
@@ -160,11 +156,21 @@
 
 def first_kernel(
     time_ref, l0, l1, l2, p0, p1, p2, p3, gain_ref, shift_ref, w_ref, qgain_ref, kgain_ref,
-    acc_ref, q_ref, piece_s, lat_s, first_s, diff_s, x_s, sems, kt_s, v_s,
+    acc_ref, q_ref, first, diff, lat_s, x_s, sems, kt_s, v_s, piece_s, piece_sems,
 ):
+    copies = [
+        pltpu.make_async_copy(piece, piece_s.at[i], piece_sems.at[i])
+        for i, piece in enumerate((p0, p1, p2, p3))
+    ]
+
+    def between():
+        for copy in copies:
+            copy.wait()
+        blend_tables(time_ref, [piece_s.at[i] for i in range(Y)], first, diff)
+
     prepare(
-        time_ref, (l0, l1, l2), ((0, 0), (0, 1), (0, 3)), (p0, p1, p2, p3),
-        gain_ref, shift_ref, [], (piece_s, lat_s, first_s, diff_s, x_s, sems),
+        (l0, l1, l2), ((0, 0), (0, 1), (0, 3)), first, diff, gain_ref, shift_ref, copies,
+        (lat_s, x_s, sems), between,
     )
     qt = head_norm_t(dot_tt(w_ref[:, :D], x_s[:ROWS, :]), qgain_ref[...])
     q_ref[...] = qt.astype(BF16).T
@@ -178,12 +184,12 @@
 
 
 def middle_kernel(
-    time_ref, l0, l1, l2, l3, p0, p1, p2, p3, gain_ref, shift_ref, w_ref, kgain_ref, q_ref, acc_ref,
-    sum_ref, piece_s, lat_s, first_s, diff_s, x_s, sems, kt_s, v_s,
+    l0, l1, l2, l3, first, diff, gain_ref, shift_ref, w_ref, kgain_ref, q_ref, acc_ref, sum_ref,
+    lat_s, x_s, sems, kt_s, v_s,
 ):
     prepare(
-        time_ref, (l0, l1, l2, l3), ((0, 2), (1, 0), (1, 1), (1, 3)), (p0, p1, p2, p3),
-        gain_ref, shift_ref, [], (piece_s, lat_s, first_s, diff_s, x_s, sems),
+        (l0, l1, l2, l3), ((0, 2), (1, 0), (1, 1), (1, 3)), first, diff, gain_ref, shift_ref, [],
+        (lat_s, x_s, sems), lambda: None,
     )
     keys_values(x_s, w_ref, kgain_ref, kt_s, v_s)
 
@@ -195,13 +201,12 @@
 
 
 def last_kernel(
-    time_ref, own, l0, p0, p1, p2, p3, gain_ref, shift_ref, w_ref, kgain_ref, wo_ref, q_ref,
-    acc_ref, out_ref, piece_s, lat_s, first_s, diff_s, x_s, sems, kt_s, v_s, own_s, att_s, own_sem,
+    own, l0, first, diff, gain_ref, shift_ref, w_ref, kgain_ref, wo_ref, q_ref, acc_ref, out_ref,
+    lat_s, x_s, sems, kt_s, v_s, own_s, att_s, own_sem,
 ):
     rest = [pltpu.make_async_copy(own, own_s, own_sem)]
     prepare(
-        time_ref, (l0,), ((1, 2),), (p0, p1, p2, p3), gain_ref, shift_ref,
-        rest, (piece_s, lat_s, first_s, diff_s, x_s, sems),
+        (l0,), ((1, 2),), first, diff, gain_ref, shift_ref, rest, (lat_s, x_s, sems), lambda: None
     )
     keys_values(x_s, w_ref, kgain_ref, kt_s, v_s)
     for copy in rest:
@@ -215,7 +220,7 @@
         f = pl.multiple_of(p * 128, 128)
         att_s[:, pl.ds(f, 128)] = (jnp.where(lane, even, odd) / total).astype(BF16)
 
-    attend(q_ref, kt_s, v_s, use, 4)
+    attend(q_ref, kt_s, v_s, use, 8)
 
     def block(i, carry):
         f = pl.multiple_of(i * 256, 256)
@@ -223,7 +228,7 @@
         for k in range(2):
             r = slice(k * TOKF, (k + 1) * TOKF)
             resid = own_s[r, pl.ds(f, 256)].astype(F32) + (
-                first_s[:, pl.ds(f, 256)] + ramp_of(0, 0, k) * diff_s[:, pl.ds(f, 256)]
+                first[:, pl.ds(f, 256)] + ramp_of(0, 0, k) * diff[:, pl.ds(f, 256)]
             )
             out_ref[r, pl.ds(f, 256)] = (resid + o[r]).astype(BF16)
         return carry
@@ -260,12 +265,9 @@
 def scratch(chunks):
     rows = chunks * ROWS
     return [
-        pltpu.VMEM((Y, 2, ZH, PIECE, D), BF16),
         pltpu.VMEM((rows, D), BF16),
-        pltpu.VMEM((TOKF, D), F32),
-        pltpu.VMEM((TOKF, D), F32),
         pltpu.VMEM((rows, D), BF16),
-        pltpu.SemaphoreType.DMA((Y + chunks,)),
+        pltpu.SemaphoreType.DMA((chunks,)),
         pltpu.VMEM((D, rows), BF16),
         pltpu.VMEM((rows, D), BF16),
     ]
@@ -319,12 +321,16 @@
     cost = pl.CostEstimate(flops=4 << 30, bytes_accessed=8 << 20, transcendentals=3 << 20)
     sums = jax.ShapeDtypeStruct((HEADS, ROWS, 128), F32)
     token = jax.ShapeDtypeStruct((ROWS, D), BF16)
-    acc, q = pl.pallas_call(
+    table = jax.ShapeDtypeStruct((TOKF, D), F32)
+    acc, q, first, diff = pl.pallas_call(
         first_kernel,
-        out_shape=(sums, token),
+        out_shape=(sums, token, table, table),
         in_specs=[SMEM] + [HBM] * 7 + [VMEM] * 5,
-        out_specs=(VMEM, VMEM),
-        scratch_shapes=scratch(3),
+        out_specs=(VMEM,) * 4,
+        scratch_shapes=scratch(3) + [
+            pltpu.VMEM((Y, 2, ZH, PIECE, D), BF16),
+            pltpu.SemaphoreType.DMA((Y,)),
+        ],
         compiler_params=params,
         cost_estimate=cost,
         name="first_keys",
@@ -333,19 +339,19 @@
     acc = pl.pallas_call(
         middle_kernel,
         out_shape=sums,
-        in_specs=[SMEM] + [HBM] * 8 + [VMEM] * 6,
+        in_specs=[HBM] * 4 + [VMEM] * 8,
         out_specs=VMEM,
         scratch_shapes=scratch(4),
         compiler_params=params,
         cost_estimate=cost,
         name="middle_keys",
     )(
-        timesteps, near_2, cross, far_1, far_3, *pieces, gain, shift, qkv_weight, kgain, q, acc,
+        near_2, cross, far_1, far_3, first, diff, gain, shift, qkv_weight, kgain, q, acc,
     )
     out = pl.pallas_call(
         last_kernel,
         out_shape=token,
-        in_specs=[SMEM] + [HBM] * 6 + [VMEM] * 7,
+        in_specs=[HBM] * 2 + [VMEM] * 9,
         out_specs=VMEM,
         scratch_shapes=scratch(1) + [
             pltpu.VMEM((ROWS, D), BF16),
@@ -356,7 +362,7 @@
         cost_estimate=cost,
         name="last_keys",
     )(
-        timesteps, own, far_2, *pieces, gain, shift, qkv_weight, kgain, out_weight, q, acc,
+        own, far_2, first, diff, gain, shift, qkv_weight, kgain, out_weight, q, acc,
     )
     return out.reshape(latents.shape)
 

time: 92 us -> 89.3 us (0.971)
  Pallas kernels: 33.7 us -> 31 us
    pallas_call x3, Pallas kernels: 31.3 us -> 28.7 us  [the longest x1 11.9 us: body(): pl.pallas_call(middle_kernel, out_shape=sums, in_specs=[HBM] * 4 + [VMEM]...]
where the time goes in v5:
time: 89.3 us; the launch traced here: 88.5 us
  starting transfers between devices  35.2 us (39%)
  Pallas kernels  31 us (35%)
  waiting for transfers between devices  13.5 us (15%)
  local copies, waits for them, and re-layouts  5.98 us (7%)
  other arithmetic  1.8 us (2%)
  between operations  1.03 us (1%)
    ppermute x19, starting transfers between devices, send(): return lax.ppermute(value, AXES, moves(**step))  35.2 us
    ppermute x19, waiting for transfers between devices, send(): return lax.ppermute(value, AXES, moves(**step))  13.5 us
    pallas_call x1, Pallas kernels, body(): pl.pallas_call(middle_kernel, out_shape=sums, in_specs=[HBM] * 4 + [VMEM]...  11.9 us
    pallas_call x1, Pallas kernels, body(): pl.pallas_call(first_kernel, out_shape=(sums, token, table, table), in_sp...  10.6 us
    pallas_call x1, Pallas kernels, body(): pl.pallas_call(last_kernel, out_shape=token, in_specs=[HBM] * 2 + [VMEM]...  6.18 us
    unnamed x26, local copies, waits for them, and re-layouts  4.75 us
    pallas_call x1, Pallas kernels, body(): pl.pallas_call(pick_kernel, out_shape=(picked, picked), in_specs=[SMEM] *...  2.09 us
  transfers between devices with their start and end apart: 19, of which 9 were waited for; matrix products, arithmetic and copies ran while one was open for 3% of the time, Pallas kernels for 28%

profile of v5, /device:TPU:2, one launch (start us, length us, event | category | flops | bytes accessed | tf_op | source)
XLA Modules:
  0.0 88.5 jit_solution(10548833916583642385)
XLA Ops:
  0.0 0.0 copy-start.2
  0.0 0.0 copy-start.6
  0.0 0.0 copy-start.4
  0.0 3.1 %collective-permute-start.7 = (bf16[256,1024]{1,0:T(8,128)(2,1)}, bf16[256,1024]{1,0:T(8,128)(2,1)S(1)}, u32[]{:S(2)}, u32[]{:S(2)}) collective-permute-start(bf16[256,1024]{1,0:T(8,128)(2,1)} %bitcast.21), channel_id=1, source_target_pairs={{0,3},{1,0},{2,1},{3,2},{4,7},{5,4},{6,5},{7,6},{8,11},{9,8},{10,9... | collective-permute-start | bytes 1572872 | tf_op jit(solution)/shard_map/ppermute | solution.py:42
  3.1 0.0 collective-permute-start.6
  3.1 7.2 %collective-permute-start.1 = (bf16[16,1024]{1,0:T(8,128)(2,1)}, bf16[16,1024]{1,0:T(8,128)(2,1)S(1)}, u32[]{:S(2)}, u32[]{:S(2)}) collective-permute-start(bf16[16,1024]{1,0:T(8,128)(2,1)} %bitcast.30), channel_id=1, source_target_pairs={{0,4},{1,5},{2,6},{3,7},{4,0},{5,1},{6,2},{7,3},{8,12},{9,13},{10,... | collective-permute-start | bytes 98312 | tf_op jit(solution)/shard_map/ppermute | solution.py:42
  10.3 0.0 collective-permute-start
  10.3 1.3 %collective-permute-done.other_ref = s32[1,2]{1,0:T(1,128)S(1)} collective-permute-done((s32[1,2]{1,0:T(1,128)}, s32[1,2]{1,0:T(1,128)S(1)}, u32[]{:S(2)}, u32[]{:S(2)}) %collective-permute-start) | collective-permute-done | bytes 40 | tf_op jit(solution)/shard_map/ppermute | solution.py:42
  11.6 0.8 collective-permute-done.1
  12.4 0.8 fusion
  13.2 3.4 %collective-permute-start.4 = (bf16[2,16,1024]{2,1,0:T(8,128)(2,1)S(1)}, bf16[2,16,1024]{2,1,0:T(8,128)(2,1)S(1)}, u32[]{:S(2)}, u32[]{:S(2)}) collective-permute-start(bf16[2,16,1024]{2,1,0:T(8,128)(2,1)S(1)} %get-tuple-element.40), channel_id=1, source_target_pairs={{0,192},{1,193},{2,194},{3,195},{4,196},{5,197},{6,198},{7,199},{8... | collective-permute-start | bytes 196616 | tf_op jit(solution)/shard_map/ppermute | solution.py:42
  16.6 0.0 collective-permute-start.3
  16.6 0.7 collective-permute-start.2
  17.3 0.0 collective-permute-done.7.l2
  17.3 0.6 collective-permute-done.6.l1
  17.9 1.6 %collective-permute-start.11 = (bf16[256,1024]{1,0:T(8,128)(2,1)}, bf16[256,1024]{1,0:T(8,128)(2,1)}, u32[]{:S(2)}, u32[]{:S(2)}) collective-permute-start(bf16[256,1024]{1,0:T(8,128)(2,1)} %bitcast.23), channel_id=1, source_target_pairs={{0,2},{1,3},{2,0},{3,1},{4,6},{5,7},{6,4},{7,5},{8,10},{9,11},{10,... | collective-permute-start | bytes 1572872 | tf_op jit(solution)/shard_map/ppermute | solution.py:42
  19.5 0.0 collective-permute-done.4
  19.5 2.3 %collective-permute-done.3 = bf16[2,16,1024]{2,1,0:T(8,128)(2,1)S(1)} collective-permute-done((bf16[2,16,1024]{2,1,0:T(8,128)(2,1)S(1)}, bf16[2,16,1024]{2,1,0:T(8,128)(2,1)S(1)}, u32[]{:S(2)}, u32[]{:S(2)}) %collective-permute-start.3) | collective-permute-done | bytes 65568 | tf_op jit(solution)/shard_map/ppermute | solution.py:42
  21.8 0.9 %collective-permute-done.2 = bf16[2,16,1024]{2,1,0:T(8,128)(2,1)S(1)} collective-permute-done((bf16[2,16,1024]{2,1,0:T(8,128)(2,1)S(1)}, bf16[2,16,1024]{2,1,0:T(8,128)(2,1)S(1)}, u32[]{:S(2)}, u32[]{:S(2)}) %collective-permute-start.2) | collective-permute-done | bytes 65568 | tf_op jit(solution)/shard_map/ppermute | solution.py:42
  22.7 0.0 copy-start.9
  22.7 0.6 collective-permute-start.10
  23.4 2.4 %collective-permute-start.9 = (bf16[4,2,16,1024]{3,2,1,0:T(8,128)(2,1)S(1)}, bf16[4,2,16,1024]{3,2,1,0:T(8,128)(2,1)S(1)}, u32[]{:S(2)}, u32[]{:S(2)}) collective-permute-start(bf16[4,2,16,1024]{3,2,1,0:T(8,128)(2,1)S(1)} %pad_maximum_fusion.x0), channel_id=1, source_target_pairs={{0,32},{1,33},{2,34},{3,35},{4,36},{5,37},{6,38},{7,39},{8,40},{9,... | collective-permute-start | bytes 786440 | tf_op jit(solution)/shard_map/ppermute | solution.py:42
  25.8 1.8 %collective-permute-start.8 = (bf16[4,2,16,1024]{3,2,1,0:T(8,128)(2,1)S(1)}, bf16[4,2,16,1024]{3,2,1,0:T(8,128)(2,1)}, u32[]{:S(2)}, u32[]{:S(2)}) collective-permute-start(bf16[4,2,16,1024]{3,2,1,0:T(8,128)(2,1)S(1)} %pad_maximum_fusion.x0), channel_id=1, source_target_pairs={{0,16},{1,17},{2,18},{3,19},{4,20},{5,21},{6,22},{7,23},{8,24},{9,... | collective-permute-start | bytes 786440 | tf_op jit(solution)/shard_map/ppermute | solution.py:42
  27.6 5.2 %collective-permute-start.5 = (bf16[256,1024]{1,0:T(8,128)(2,1)}, bf16[256,1024]{1,0:T(8,128)(2,1)}, u32[]{:S(2)}, u32[]{:S(2)}) collective-permute-start(bf16[256,1024]{1,0:T(8,128)(2,1)} %bitcast.24), channel_id=1, source_target_pairs={{0,4},{1,5},{2,6},{3,7},{4,0},{5,1},{6,2},{7,3},{8,12},{9,13},{10,... | collective-permute-start | bytes 1572872 | tf_op jit(solution)/shard_map/ppermute | solution.py:42
  32.8 0.0 collective-permute-done.10.x3
  32.8 2.8 %collective-permute-done.9.x2 = bf16[4,2,16,1024]{3,2,1,0:T(8,128)(2,1)S(1)} collective-permute-done((bf16[4,2,16,1024]{3,2,1,0:T(8,128)(2,1)S(1)}, bf16[4,2,16,1024]{3,2,1,0:T(8,128)(2,1)S(1)}, u32[]{:S(2)}, u32[]{:S(2)}) %collective-permute-start.9) | collective-permute-done | bytes 262176 | tf_op jit(solution)/shard_map/ppermute | solution.py:42
  35.5 0.0 copy-done.10
  35.5 0.7 copy-done.11
  36.2 0.3 collective-permute-done.8.x1
  36.5 0.0 copy-done.12
  36.5 0.0 copy-done.9
  36.5 2.1 %pick.1 = (bf16[2,2,16,1024]{3,2,1,0:T(8,128)(2,1)}, bf16[2,2,16,1024]{3,2,1,0:T(8,128)(2,1)}) custom-call(s32[1,2]{1,0:T(1,128)} %pair_ref.1, s32[1,2]{1,0:T(1,128)} %copy-done.12, bf16[4,2,16,1024]{3,2,1,0:T(8,128)(2,1)} %copy-done.9, bf16[4,2,16,1024]{3,2,1,0:T(8,128)(2,1)} %collective-permute-done.8.x1, bf16[4,2,16,1024]{3,2,1,0:T(8,128)(2,1)} %copy-done.11, ...), custom_call_target="tpu_custom_call" | custom-call | tf_op jit(solution)/shard_map/pick/pallas_call | solution.py:293
  38.6 0.0 collective-permute-start.12
  38.6 1.2 %slice.3 = s32[1]{0:T(128)} slice(s32[2]{0:T(128)} %time_ref.1), slice={[1:2]} | slice | bytes 8 | tf_op jit(solution)/shard_map/slice | solution.py:306
  40.5 0.0 collective-permute-done.11.l0
  40.5 0.0 collective-permute-done.12
  40.5 0.9 %add.3.p0 = bf16[2,2,16,1024]{3,2,1,0:T(8,128)(2,1)S(1)} add(bf16[2,2,16,1024]{3,2,1,0:T(8,128)(2,1)} %get-tuple-element.27, bf16[2,2,16,1024]{3,2,1,0:T(8,128)(2,1)S(1)} %collective-permute-done.12) | non-fusion elementwise | flops 65536 | bytes 393216 | tf_op jit(solution)/shard_map/add | solution.py:300
  41.5 3.3 %collective-permute-start.15 = (bf16[2,2,16,1024]{3,2,1,0:T(8,128)(2,1)S(1)}, bf16[2,2,16,1024]{3,2,1,0:T(8,128)(2,1)S(1)}, u32[]{:S(2)}, u32[]{:S(2)}) collective-permute-start(bf16[2,2,16,1024]{3,2,1,0:T(8,128)(2,1)S(1)} %add.3.p0), channel_id=1, source_target_pairs={{0,3},{1,0},{2,1},{3,2},{4,7},{5,4},{6,5},{7,6},{8,11},{9,8},{10,9... | collective-permute-start | bytes 393224 | tf_op jit(solution)/shard_map/ppermute | solution.py:42
  44.8 0.0 collective-permute-start.14
  44.8 1.0 %collective-permute-start.13 = (bf16[2,2,16,1024]{3,2,1,0:T(8,128)(2,1)S(1)}, bf16[2,2,16,1024]{3,2,1,0:T(8,128)(2,1)S(1)}, u32[]{:S(2)}, u32[]{:S(2)}) collective-permute-start(bf16[2,2,16,1024]{3,2,1,0:T(8,128)(2,1)S(1)} %add.3.p0), channel_id=1, source_target_pairs={{0,1},{1,2},{2,3},{3,0},{4,5},{5,6},{6,7},{7,4},{8,9},{9,10},{10,1... | collective-permute-start | bytes 393224 | tf_op jit(solution)/shard_map/ppermute | solution.py:42
  45.8 0.0 copy-done.2
  45.8 0.0 copy-done.6
  45.8 0.0 copy-done.5
  45.8 0.0 copy-done.4
  45.9 0.0 copy-start
  45.9 2.8 %copy-done = bf16[1024,3072]{1,0:T(8,128)(2,1)S(1)} copy-done((bf16[1024,3072]{1,0:T(8,128)(2,1)S(1)}, bf16[1024,3072]{1,0:T(8,128)(2,1)}, u32[]{:S(2)}) %copy-start) | copy-done | bytes 6291480
  48.6 1.2 %copy-done.3 = bf16[256,2048]{1,0:T(8,128)(2,1)S(1)} copy-done((bf16[256,2048]{1,0:T(8,128)(2,1)S(1)}, bf16[256,2048]{1,0:T(8,128)(2,1)}, u32[]{:S(2)}) %copy-start.3) | copy-done | bytes 1048600
  49.9 0.2 prelude.1
  50.1 4.0 %collective-permute-done.5.l1 = bf16[256,1024]{1,0:T(8,128)(2,1)} collective-permute-done((bf16[256,1024]{1,0:T(8,128)(2,1)}, bf16[256,1024]{1,0:T(8,128)(2,1)}, u32[]{:S(2)}, u32[]{:S(2)}) %collective-permute-start.5) | collective-permute-done | bytes 524320 | tf_op jit(solution)/shard_map/ppermute | solution.py:42
  54.1 3.2 %collective-permute-start.18 = (bf16[256,1024]{1,0:T(8,128)(2,1)}, bf16[256,1024]{1,0:T(8,128)(2,1)S(1)}, u32[]{:S(2)}, u32[]{:S(2)}) collective-permute-start(bf16[256,1024]{1,0:T(8,128)(2,1)} %collective-permute-done.5.l1), channel_id=1, source_target_pairs={{0,3},{1,0},{2,1},{3,2},{4,7},{5,4},{6,5},{7,6},{8,11},{9,8},{10,9... | collective-permute-start | bytes 1572872 | tf_op jit(solution)/shard_map/ppermute | solution.py:42
  57.3 0.0 collective-permute-start.17
  57.3 0.0 collective-permute-done.15.p3
  57.3 0.0 collective-permute-done.14.p2
  57.3 0.0 collective-permute-done.13.p1
  57.3 0.0 copy-done.1
  57.3 0.0 copy-done.7
  57.3 0.0 copy-done.8
  57.3 10.6 %first_keys.1 = (f32[16,256,128]{2,1,0:T(8,128)S(1)}, bf16[256,1024]{1,0:T(8,128)(2,1)S(1)}, f32[128,1024]{1,0:T(8,128)S(1)}, f32[128,1024]{1,0:T(8,128)S(1)}) custom-call(s32[2]{0:T(128)S(1)} %copy-done.8, bf16[256,1024]{1,0:T(8,128)(2,1)S(1)} %bitcast.25, bf16[256,1024]{1,0:T(8,128)(2,1)S(1)} %collective-permute-done.6.l1, ...), custom_call_target="tpu_custom_call" | custom-call | flops 4294967296 | bytes 8388608 | tf_op jit(solution)/shard_map/first_keys/pallas_call | solution.py:325
  68.0 1.8 %collective-permute-start.16 = (bf16[256,1024]{1,0:T(8,128)(2,1)}, bf16[256,1024]{1,0:T(8,128)(2,1)S(1)}, u32[]{:S(2)}, u32[]{:S(2)}) collective-permute-start(bf16[256,1024]{1,0:T(8,128)(2,1)} %collective-permute-done.5.l1), channel_id=1, source_target_pairs={{0,2},{1,3},{2,0},{3,1},{4,6},{5,7},{6,4},{7,5},{8,10},{9,11},{10,... | collective-permute-start | bytes 1572872 | tf_op jit(solution)/shard_map/ppermute | solution.py:42
  69.8 0.0 collective-permute-done.18.l3
  69.8 0.5 collective-permute-done.17.l2
  70.2 11.9 %middle_keys.1.acc_ref = f32[16,256,128]{2,1,0:T(8,128)S(1)} custom-call(bf16[256,1024]{1,0:T(8,128)(2,1)} %collective-permute-done.11.l0, bf16[256,1024]{1,0:T(8,128)(2,1)} %collective-permute-done.5.l1, bf16[256,1024]{1,0:T(8,128)(2,1)S(1)} %collective-permute-done.17.l2, bf16[256,1024]{1,0:T(8,128)(2,1)S(1)} %collective-permute-done.18.l3, ...), custom_call_target="tpu_custom_call" | custom-call | flops 4294967296 | bytes 8388608 | tf_op jit(solution)/shard_map/middle_keys/pallas_call | solution.py:339
  82.1 0.0 collective-permute-done.16.l0
  82.1 6.2 %last_keys.1 = bf16[256,1024]{1,0:T(8,128)(2,1)} custom-call(bf16[256,1024]{1,0:T(8,128)(2,1)S(1)} %bitcast.26, bf16[256,1024]{1,0:T(8,128)(2,1)S(1)} %collective-permute-done.16.l0, f32[128,1024]{1,0:T(8,128)S(1)} %get-tuple-element.35.first, f32[128,1024]{1,0:T(8,128)S(1)} %get-tuple-element.36.diff, f32[1,1024]{1,0:T(1,128)S(1)} %get-tuple-element.29.gain_ref, ...), custom_call_target="tpu_custom_call" | custom-call | flops 4294967296 | bytes 8388608 | tf_op jit(solution)/shard_map/last_keys/pallas_call | solution.py:351
  (11 shorter events, 0.1 us)
Async XLA Ops:
  0.0 45.8 %copy-start.2 = (bf16[1024,1024]{1,0:T(8,128)(2,1)S(1)}, bf16[1024,1024]{1,0:T(8,128)(2,1)}, u32[]{:S(2)}) copy-start(bf16[1024,1024]{1,0:T(8,128)(2,1)} %wo_ref.3) | copy-start | bytes 6291460
  0.0 45.8 %copy-start.6 = (f32[64]{0:T(128)S(1)}, f32[64]{0:T(128)}, u32[]{:S(2)}) copy-start(f32[64]{0:T(128)} %param.18) | copy-start | bytes 772
  0.0 45.8 %copy-start.5 = (f32[64]{0:T(128)S(1)}, f32[64]{0:T(128)}, u32[]{:S(2)}) copy-start(f32[64]{0:T(128)} %param.17) | copy-start | bytes 772
  0.0 45.8 %copy-start.4 = (f32[1024]{0:T(1024)S(1)}, f32[1024]{0:T(1024)}, u32[]{:S(2)}) copy-start(f32[1024]{0:T(1024)} %param.15) | copy-start | bytes 12292
  0.0 17.3 %collective-permute-start.7 = (bf16[256,1024]{1,0:T(8,128)(2,1)}, bf16[256,1024]{1,0:T(8,128)(2,1)S(1)}, u32[]{:S(2)}, u32[]{:S(2)}) collective-permute-start(bf16[256,1024]{1,0:T(8,128)(2,1)} %bitcast.21), channel_id=1, source_target_pairs={{0,3},{1,0},{2,1},{3,2},{4,7},{5,4},{6,5},{7,6},{8,11},{9,8},{10,9... | collective-permute-start | bytes 1572872 | tf_op jit(solution)/shard_map/ppermute | solution.py:42
  3.1 14.8 %collective-permute-start.6 = (bf16[256,1024]{1,0:T(8,128)(2,1)}, bf16[256,1024]{1,0:T(8,128)(2,1)S(1)}, u32[]{:S(2)}, u32[]{:S(2)}) collective-permute-start(bf16[256,1024]{1,0:T(8,128)(2,1)} %bitcast.22), channel_id=1, source_target_pairs={{0,1},{1,2},{2,3},{3,0},{4,5},{5,6},{6,7},{7,4},{8,9},{9,10},{10,1... | collective-permute-start | bytes 1572872 | tf_op jit(solution)/shard_map/ppermute | solution.py:42
  3.1 9.3 %collective-permute-start.1 = (bf16[16,1024]{1,0:T(8,128)(2,1)}, bf16[16,1024]{1,0:T(8,128)(2,1)S(1)}, u32[]{:S(2)}, u32[]{:S(2)}) collective-permute-start(bf16[16,1024]{1,0:T(8,128)(2,1)} %bitcast.30), channel_id=1, source_target_pairs={{0,4},{1,5},{2,6},{3,7},{4,0},{5,1},{6,2},{7,3},{8,12},{9,13},{10,... | collective-permute-start | bytes 98312 | tf_op jit(solution)/shard_map/ppermute | solution.py:42
  10.3 1.3 %collective-permute-start = (s32[1,2]{1,0:T(1,128)}, s32[1,2]{1,0:T(1,128)S(1)}, u32[]{:S(2)}, u32[]{:S(2)}) collective-permute-start(s32[1,2]{1,0:T(1,128)} %pair_ref.1), channel_id=1, source_target_pairs={{0,8},{1,9},{2,10},{3,11},{4,12},{5,13},{6,14},{7,15},{8,0},{9,1},... | collective-permute-start | bytes 32 | tf_op jit(solution)/shard_map/ppermute | solution.py:42
  11.6 25.0 %copy-start.12 = (s32[1,2]{1,0:T(1,128)}, s32[1,2]{1,0:T(1,128)S(1)}, u32[]{:S(2)}) copy-start(s32[1,2]{1,0:T(1,128)S(1)} %collective-permute-done.other_ref) | copy-start | bytes 28
  13.2 6.3 %collective-permute-start.4 = (bf16[2,16,1024]{2,1,0:T(8,128)(2,1)S(1)}, bf16[2,16,1024]{2,1,0:T(8,128)(2,1)S(1)}, u32[]{:S(2)}, u32[]{:S(2)}) collective-permute-start(bf16[2,16,1024]{2,1,0:T(8,128)(2,1)S(1)} %get-tuple-element.40), channel_id=1, source_target_pairs={{0,192},{1,193},{2,194},{3,195},{4,196},{5,197},{6,198},{7,199},{8... | collective-permute-start | bytes 196616 | tf_op jit(solution)/shard_map/ppermute | solution.py:42
  16.6 5.2 %collective-permute-start.3 = (bf16[2,16,1024]{2,1,0:T(8,128)(2,1)S(1)}, bf16[2,16,1024]{2,1,0:T(8,128)(2,1)S(1)}, u32[]{:S(2)}, u32[]{:S(2)}) collective-permute-start(bf16[2,16,1024]{2,1,0:T(8,128)(2,1)S(1)} %get-tuple-element.40), channel_id=1, source_target_pairs={{0,128},{1,129},{2,130},{3,131},{4,132},{5,133},{6,134},{7,135},{8... | collective-permute-start | bytes 196616 | tf_op jit(solution)/shard_map/ppermute | solution.py:42
  16.6 6.1 %collective-permute-start.2 = (bf16[2,16,1024]{2,1,0:T(8,128)(2,1)S(1)}, bf16[2,16,1024]{2,1,0:T(8,128)(2,1)S(1)}, u32[]{:S(2)}, u32[]{:S(2)}) collective-permute-start(bf16[2,16,1024]{2,1,0:T(8,128)(2,1)S(1)} %get-tuple-element.40), channel_id=1, source_target_pairs={{0,64},{1,65},{2,66},{3,67},{4,68},{5,69},{6,70},{7,71},{8,72},{9,... | collective-permute-start | bytes 196616 | tf_op jit(solution)/shard_map/ppermute | solution.py:42
  17.9 22.6 %collective-permute-start.11 = (bf16[256,1024]{1,0:T(8,128)(2,1)}, bf16[256,1024]{1,0:T(8,128)(2,1)}, u32[]{:S(2)}, u32[]{:S(2)}) collective-permute-start(bf16[256,1024]{1,0:T(8,128)(2,1)} %bitcast.23), channel_id=1, source_target_pairs={{0,2},{1,3},{2,0},{3,1},{4,6},{5,7},{6,4},{7,5},{8,10},{9,11},{10,... | collective-permute-start | bytes 1572872 | tf_op jit(solution)/shard_map/ppermute | solution.py:42
  22.7 13.8 %copy-start.9 = (bf16[4,2,16,1024]{3,2,1,0:T(8,128)(2,1)}, bf16[4,2,16,1024]{3,2,1,0:T(8,128)(2,1)S(1)}, u32[]{:S(2)}) copy-start(bf16[4,2,16,1024]{3,2,1,0:T(8,128)(2,1)S(1)} %pad_maximum_fusion.x0) | copy-start | bytes 786436
  22.7 10.0 %collective-permute-start.10 = (bf16[4,2,16,1024]{3,2,1,0:T(8,128)(2,1)S(1)}, bf16[4,2,16,1024]{3,2,1,0:T(8,128)(2,1)S(1)}, u32[]{:S(2)}, u32[]{:S(2)}) collective-permute-start(bf16[4,2,16,1024]{3,2,1,0:T(8,128)(2,1)S(1)} %pad_maximum_fusion.x0), channel_id=1, source_target_pairs={{0,48},{1,49},{2,50},{3,51},{4,52},{5,53},{6,54},{7,55},{8,56},{9,... | collective-permute-start | bytes 786440 | tf_op jit(solution)/shard_map/ppermute | solution.py:42
  23.4 12.2 %collective-permute-start.9 = (bf16[4,2,16,1024]{3,2,1,0:T(8,128)(2,1)S(1)}, bf16[4,2,16,1024]{3,2,1,0:T(8,128)(2,1)S(1)}, u32[]{:S(2)}, u32[]{:S(2)}) collective-permute-start(bf16[4,2,16,1024]{3,2,1,0:T(8,128)(2,1)S(1)} %pad_maximum_fusion.x0), channel_id=1, source_target_pairs={{0,32},{1,33},{2,34},{3,35},{4,36},{5,37},{6,38},{7,39},{8,40},{9,... | collective-permute-start | bytes 786440 | tf_op jit(solution)/shard_map/ppermute | solution.py:42
  25.8 10.8 %collective-permute-start.8 = (bf16[4,2,16,1024]{3,2,1,0:T(8,128)(2,1)S(1)}, bf16[4,2,16,1024]{3,2,1,0:T(8,128)(2,1)}, u32[]{:S(2)}, u32[]{:S(2)}) collective-permute-start(bf16[4,2,16,1024]{3,2,1,0:T(8,128)(2,1)S(1)} %pad_maximum_fusion.x0), channel_id=1, source_target_pairs={{0,16},{1,17},{2,18},{3,19},{4,20},{5,21},{6,22},{7,23},{8,24},{9,... | collective-permute-start | bytes 786440 | tf_op jit(solution)/shard_map/ppermute | solution.py:42
  27.6 26.6 %collective-permute-start.5 = (bf16[256,1024]{1,0:T(8,128)(2,1)}, bf16[256,1024]{1,0:T(8,128)(2,1)}, u32[]{:S(2)}, u32[]{:S(2)}) collective-permute-start(bf16[256,1024]{1,0:T(8,128)(2,1)} %bitcast.24), channel_id=1, source_target_pairs={{0,4},{1,5},{2,6},{3,7},{4,0},{5,1},{6,2},{7,3},{8,12},{9,13},{10,... | collective-permute-start | bytes 1572872 | tf_op jit(solution)/shard_map/ppermute | solution.py:42
  32.8 2.8 %copy-start.10 = (bf16[4,2,16,1024]{3,2,1,0:T(8,128)(2,1)}, bf16[4,2,16,1024]{3,2,1,0:T(8,128)(2,1)S(1)}, u32[]{:S(2)}) copy-start(bf16[4,2,16,1024]{3,2,1,0:T(8,128)(2,1)S(1)} %collective-permute-done.10.x3) | copy-start | bytes 786436
  35.5 0.7 copy-start.11
  38.6 1.9 %collective-permute-start.12 = (bf16[2,2,16,1024]{3,2,1,0:T(8,128)(2,1)}, bf16[2,2,16,1024]{3,2,1,0:T(8,128)(2,1)S(1)}, u32[]{:S(2)}, u32[]{:S(2)}) collective-permute-start(bf16[2,2,16,1024]{3,2,1,0:T(8,128)(2,1)} %get-tuple-element.28), channel_id=1, source_target_pairs={{0,8},{1,9},{2,10},{3,11},{4,12},{5,13},{6,14},{7,15},{8,0},{9,1},... | collective-permute-start | bytes 393224 | tf_op jit(solution)/shard_map/ppermute | solution.py:42
  41.5 15.8 %collective-permute-start.15 = (bf16[2,2,16,1024]{3,2,1,0:T(8,128)(2,1)S(1)}, bf16[2,2,16,1024]{3,2,1,0:T(8,128)(2,1)S(1)}, u32[]{:S(2)}, u32[]{:S(2)}) collective-permute-start(bf16[2,2,16,1024]{3,2,1,0:T(8,128)(2,1)S(1)} %add.3.p0), channel_id=1, source_target_pairs={{0,3},{1,0},{2,1},{3,2},{4,7},{5,4},{6,5},{7,6},{8,11},{9,8},{10,9... | collective-permute-start | bytes 393224 | tf_op jit(solution)/shard_map/ppermute | solution.py:42
  44.8 12.5 %collective-permute-start.14 = (bf16[2,2,16,1024]{3,2,1,0:T(8,128)(2,1)S(1)}, bf16[2,2,16,1024]{3,2,1,0:T(8,128)(2,1)S(1)}, u32[]{:S(2)}, u32[]{:S(2)}) collective-permute-start(bf16[2,2,16,1024]{3,2,1,0:T(8,128)(2,1)S(1)} %add.3.p0), channel_id=1, source_target_pairs={{0,2},{1,3},{2,0},{3,1},{4,6},{5,7},{6,4},{7,5},{8,10},{9,11},{10,... | collective-permute-start | bytes 393224 | tf_op jit(solution)/shard_map/ppermute | solution.py:42
  44.8 12.5 %collective-permute-start.13 = (bf16[2,2,16,1024]{3,2,1,0:T(8,128)(2,1)S(1)}, bf16[2,2,16,1024]{3,2,1,0:T(8,128)(2,1)S(1)}, u32[]{:S(2)}, u32[]{:S(2)}) collective-permute-start(bf16[2,2,16,1024]{3,2,1,0:T(8,128)(2,1)S(1)} %add.3.p0), channel_id=1, source_target_pairs={{0,1},{1,2},{2,3},{3,0},{4,5},{5,6},{6,7},{7,4},{8,9},{9,10},{10,1... | collective-permute-start | bytes 393224 | tf_op jit(solution)/shard_map/ppermute | solution.py:42
  45.9 2.8 %copy-start = (bf16[1024,3072]{1,0:T(8,128)(2,1)S(1)}, bf16[1024,3072]{1,0:T(8,128)(2,1)}, u32[]{:S(2)}) copy-start(bf16[1024,3072]{1,0:T(8,128)(2,1)} %w_ref.7) | copy-start | bytes 18874372
  48.6 1.2 %copy-start.3 = (bf16[256,2048]{1,0:T(8,128)(2,1)S(1)}, bf16[256,2048]{1,0:T(8,128)(2,1)}, u32[]{:S(2)}) copy-start(bf16[256,2048]{1,0:T(8,128)(2,1)} %mod_ref.1) | copy-start | bytes 3145732
  49.9 7.4 %copy-start.1 = (bf16[1024,3072]{1,0:T(8,128)(2,1)S(1)}, bf16[1024,3072]{1,0:T(8,128)(2,1)}, u32[]{:S(2)}) copy-start(bf16[1024,3072]{1,0:T(8,128)(2,1)} %w_ref.7) | copy-start | bytes 18874372
  49.9 7.5 %copy-start.7 = (bf16[1,2,128,1024]{3,2,1,0:T(8,128)(2,1)S(1)}, bf16[1,2,128,1024]{3,2,1,0:T(8,128)(2,1)}, u32[]{:S(2)}) copy-start(bf16[1,2,128,1024]{3,2,1,0:T(8,128)(2,1)} %param.10) | copy-start | bytes 1572868
  49.9 7.5 %copy-start.8 = (s32[2]{0:T(128)S(1)}, s32[2]{0:T(128)}, u32[]{:S(2)}) copy-start(s32[2]{0:T(128)} %time_ref.1) | copy-start | bytes 28
  54.1 15.6 %collective-permute-start.18 = (bf16[256,1024]{1,0:T(8,128)(2,1)}, bf16[256,1024]{1,0:T(8,128)(2,1)S(1)}, u32[]{:S(2)}, u32[]{:S(2)}) collective-permute-start(bf16[256,1024]{1,0:T(8,128)(2,1)} %collective-permute-done.5.l1), channel_id=1, source_target_pairs={{0,3},{1,0},{2,1},{3,2},{4,7},{5,4},{6,5},{7,6},{8,11},{9,8},{10,9... | collective-permute-start | bytes 1572872 | tf_op jit(solution)/shard_map/ppermute | solution.py:42
  57.3 12.9 %collective-permute-start.17 = (bf16[256,1024]{1,0:T(8,128)(2,1)}, bf16[256,1024]{1,0:T(8,128)(2,1)S(1)}, u32[]{:S(2)}, u32[]{:S(2)}) collective-permute-start(bf16[256,1024]{1,0:T(8,128)(2,1)} %collective-permute-done.5.l1), channel_id=1, source_target_pairs={{0,1},{1,2},{2,3},{3,0},{4,5},{5,6},{6,7},{7,4},{8,9},{9,10},{10,1... | collective-permute-start | bytes 1572872 | tf_op jit(solution)/shard_map/ppermute | solution.py:42
  68.0 14.1 %collective-permute-start.16 = (bf16[256,1024]{1,0:T(8,128)(2,1)}, bf16[256,1024]{1,0:T(8,128)(2,1)S(1)}, u32[]{:S(2)}, u32[]{:S(2)}) collective-permute-start(bf16[256,1024]{1,0:T(8,128)(2,1)} %collective-permute-done.5.l1), channel_id=1, source_target_pairs={{0,2},{1,3},{2,0},{3,1},{4,6},{5,7},{6,4},{7,5},{8,10},{9,11},{10,... | collective-permute-start | bytes 1572872 | tf_op jit(solution)/shard_map/ppermute | solution.py:42

commit v6 on v5

--- a/solution.py
+++ b/solution.py
@@ -236,24 +236,28 @@
     lax.fori_loop(0, D // 256, block, 0)
 
 
-def pick_kernel(pair_ref, other_ref, x0, x1, x2, x3, *out_refs):
+def pick_kernel(pair_ref, other_ref, x0, x1, x2, x3, held_ref, asked_ref, sems):
     zl, x, core = lax.axis_index("zl"), lax.axis_index("x"), lax.axis_index("core")
-    for wants, out_ref in zip((pair_ref, other_ref), out_refs):
+    slots = []
+    for i, (wants, out_ref) in enumerate(((pair_ref, held_ref), (other_ref, asked_ref))):
         for k in range(2):
             wanted = wants[0, k]
             back = (x + X - wanted // CORE % X) % X
             entry = (zl + ZL - wanted // (X * CORE)) % ZL
-            back = jnp.where(wanted % CORE == core, back, -1)
-
-            @pl.when(back < 0)
-            def _():
-                out_ref[k] = jnp.zeros_like(out_ref[k])
-
-            for t, held in enumerate((x0, x1, x2, x3)):
+            sem = sems.at[2 * i + k]
+            for t, source in enumerate((x0, x1, x2, x3)):
 
                 @pl.when(back == t)
                 def _():
-                    out_ref[k] = held[entry]
+                    pltpu.make_async_copy(source.at[entry], out_ref.at[k], sem).start()
+
+            slots.append((out_ref, k, sem, wanted % CORE == core))
+    for out_ref, k, sem, here in slots:
+        pltpu.make_async_copy(x0.at[0], out_ref.at[k], sem).wait()
+
+        @pl.when(jnp.logical_not(here))
+        def _():
+            out_ref[k] = jnp.zeros_like(out_ref[k])
 
 
 VMEM = pl.BlockSpec(memory_space=pltpu.VMEM)
@@ -293,8 +297,9 @@
     held, asked = pl.pallas_call(
         pick_kernel,
         out_shape=(picked, picked),
-        in_specs=[SMEM] * 2 + [VMEM] * 4,
+        in_specs=[SMEM] * 2 + [HBM] * 4,
         out_specs=(VMEM, VMEM),
+        scratch_shapes=[pltpu.SemaphoreType.DMA((4,))],
         name="pick",
     )(key_index, after(pair_other, (near_1, near_3)), *by_x)
     both = after(held, near_2) + send(asked, core=1)

time: 89.3 us -> 89.8 us (level)
  no operation moved by 1% of the time
where the time goes in v6:
time: 89.8 us; the launch traced here: 88.5 us
  starting transfers between devices  35.3 us (39%)
  Pallas kernels  31.3 us (35%)
  waiting for transfers between devices  13.1 us (15%)
  local copies, waits for them, and re-layouts  5.99 us (7%)
  other arithmetic  1.8 us (2%)
  between operations  1.05 us (1%)
    ppermute x19, starting transfers between devices, send(): return lax.ppermute(value, AXES, moves(**step))  35.3 us
    ppermute x19, waiting for transfers between devices, send(): return lax.ppermute(value, AXES, moves(**step))  13.1 us
    pallas_call x1, Pallas kernels, body(): pl.pallas_call(middle_kernel, out_shape=sums, in_specs=[HBM] * 4 + [VMEM]...  11.9 us
    pallas_call x1, Pallas kernels, body(): pl.pallas_call(first_kernel, out_shape=(sums, token, table, table), in_sp...  10.6 us
    pallas_call x1, Pallas kernels, body(): pl.pallas_call(last_kernel, out_shape=token, in_specs=[HBM] * 2 + [VMEM]...  6.18 us
    unnamed x26, local copies, waits for them, and re-layouts  4.75 us
    pallas_call x1, Pallas kernels, body(): pl.pallas_call(pick_kernel, out_shape=(picked, picked), in_specs=[SMEM] *...  2.38 us
  transfers between devices with their start and end apart: 19, of which 9 were waited for; matrix products, arithmetic and copies ran while one was open for 3% of the time, Pallas kernels for 28%

profile of v6, /device:TPU:2, one launch (start us, length us, event | category | flops | bytes accessed | tf_op | source)
XLA Modules:
  0.0 88.5 jit_solution(14130816795491682226)
XLA Ops:
  0.0 0.0 copy-start.2
  0.0 0.0 copy-start.6
  0.0 0.0 copy-start.4
  0.0 3.1 %collective-permute-start.7 = (bf16[256,1024]{1,0:T(8,128)(2,1)}, bf16[256,1024]{1,0:T(8,128)(2,1)S(1)}, u32[]{:S(2)}, u32[]{:S(2)}) collective-permute-start(bf16[256,1024]{1,0:T(8,128)(2,1)} %bitcast.21), channel_id=1, source_target_pairs={{0,3},{1,0},{2,1},{3,2},{4,7},{5,4},{6,5},{7,6},{8,11},{9,8},{10,9... | collective-permute-start | bytes 1572872 | tf_op jit(solution)/shard_map/ppermute | solution.py:42
  3.1 0.0 collective-permute-start.6
  3.1 7.2 %collective-permute-start.1 = (bf16[16,1024]{1,0:T(8,128)(2,1)}, bf16[16,1024]{1,0:T(8,128)(2,1)S(1)}, u32[]{:S(2)}, u32[]{:S(2)}) collective-permute-start(bf16[16,1024]{1,0:T(8,128)(2,1)} %bitcast.30), channel_id=1, source_target_pairs={{0,4},{1,5},{2,6},{3,7},{4,0},{5,1},{6,2},{7,3},{8,12},{9,13},{10,... | collective-permute-start | bytes 98312 | tf_op jit(solution)/shard_map/ppermute | solution.py:42
  10.3 0.0 collective-permute-start
  10.3 1.3 %collective-permute-done.other_ref = s32[1,2]{1,0:T(1,128)S(1)} collective-permute-done((s32[1,2]{1,0:T(1,128)}, s32[1,2]{1,0:T(1,128)S(1)}, u32[]{:S(2)}, u32[]{:S(2)}) %collective-permute-start) | collective-permute-done | bytes 40 | tf_op jit(solution)/shard_map/ppermute | solution.py:42
  11.6 0.8 collective-permute-done.1
  12.4 0.8 fusion
  13.2 3.4 %collective-permute-start.4 = (bf16[2,16,1024]{2,1,0:T(8,128)(2,1)S(1)}, bf16[2,16,1024]{2,1,0:T(8,128)(2,1)S(1)}, u32[]{:S(2)}, u32[]{:S(2)}) collective-permute-start(bf16[2,16,1024]{2,1,0:T(8,128)(2,1)S(1)} %get-tuple-element.40), channel_id=1, source_target_pairs={{0,192},{1,193},{2,194},{3,195},{4,196},{5,197},{6,198},{7,199},{8... | collective-permute-start | bytes 196616 | tf_op jit(solution)/shard_map/ppermute | solution.py:42
  16.6 0.0 collective-permute-start.3
  16.6 0.7 collective-permute-start.2
  17.3 0.0 collective-permute-done.7.l2
  17.3 0.6 collective-permute-done.6.l1
  17.9 1.6 %collective-permute-start.11 = (bf16[256,1024]{1,0:T(8,128)(2,1)}, bf16[256,1024]{1,0:T(8,128)(2,1)}, u32[]{:S(2)}, u32[]{:S(2)}) collective-permute-start(bf16[256,1024]{1,0:T(8,128)(2,1)} %bitcast.23), channel_id=1, source_target_pairs={{0,2},{1,3},{2,0},{3,1},{4,6},{5,7},{6,4},{7,5},{8,10},{9,11},{10,... | collective-permute-start | bytes 1572872 | tf_op jit(solution)/shard_map/ppermute | solution.py:42
  19.5 0.0 collective-permute-done.4
  19.5 2.3 %collective-permute-done.3 = bf16[2,16,1024]{2,1,0:T(8,128)(2,1)S(1)} collective-permute-done((bf16[2,16,1024]{2,1,0:T(8,128)(2,1)S(1)}, bf16[2,16,1024]{2,1,0:T(8,128)(2,1)S(1)}, u32[]{:S(2)}, u32[]{:S(2)}) %collective-permute-start.3) | collective-permute-done | bytes 65568 | tf_op jit(solution)/shard_map/ppermute | solution.py:42
  21.8 0.9 %collective-permute-done.2 = bf16[2,16,1024]{2,1,0:T(8,128)(2,1)S(1)} collective-permute-done((bf16[2,16,1024]{2,1,0:T(8,128)(2,1)S(1)}, bf16[2,16,1024]{2,1,0:T(8,128)(2,1)S(1)}, u32[]{:S(2)}, u32[]{:S(2)}) %collective-permute-start.2) | collective-permute-done | bytes 65568 | tf_op jit(solution)/shard_map/ppermute | solution.py:42
  22.7 0.0 copy-start.9
  22.7 0.6 collective-permute-start.10
  23.4 2.4 %collective-permute-start.9 = (bf16[4,2,16,1024]{3,2,1,0:T(8,128)(2,1)S(1)}, bf16[4,2,16,1024]{3,2,1,0:T(8,128)(2,1)S(1)}, u32[]{:S(2)}, u32[]{:S(2)}) collective-permute-start(bf16[4,2,16,1024]{3,2,1,0:T(8,128)(2,1)S(1)} %pad_maximum_fusion.x0), channel_id=1, source_target_pairs={{0,32},{1,33},{2,34},{3,35},{4,36},{5,37},{6,38},{7,39},{8,40},{9,... | collective-permute-start | bytes 786440 | tf_op jit(solution)/shard_map/ppermute | solution.py:42
  25.8 1.8 %collective-permute-start.8 = (bf16[4,2,16,1024]{3,2,1,0:T(8,128)(2,1)S(1)}, bf16[4,2,16,1024]{3,2,1,0:T(8,128)(2,1)}, u32[]{:S(2)}, u32[]{:S(2)}) collective-permute-start(bf16[4,2,16,1024]{3,2,1,0:T(8,128)(2,1)S(1)} %pad_maximum_fusion.x0), channel_id=1, source_target_pairs={{0,16},{1,17},{2,18},{3,19},{4,20},{5,21},{6,22},{7,23},{8,24},{9,... | collective-permute-start | bytes 786440 | tf_op jit(solution)/shard_map/ppermute | solution.py:42
  27.6 5.2 %collective-permute-start.5 = (bf16[256,1024]{1,0:T(8,128)(2,1)}, bf16[256,1024]{1,0:T(8,128)(2,1)}, u32[]{:S(2)}, u32[]{:S(2)}) collective-permute-start(bf16[256,1024]{1,0:T(8,128)(2,1)} %bitcast.24), channel_id=1, source_target_pairs={{0,4},{1,5},{2,6},{3,7},{4,0},{5,1},{6,2},{7,3},{8,12},{9,13},{10,... | collective-permute-start | bytes 1572872 | tf_op jit(solution)/shard_map/ppermute | solution.py:42
  32.8 0.0 collective-permute-done.10.x3
  32.8 2.8 %collective-permute-done.9.x2 = bf16[4,2,16,1024]{3,2,1,0:T(8,128)(2,1)S(1)} collective-permute-done((bf16[4,2,16,1024]{3,2,1,0:T(8,128)(2,1)S(1)}, bf16[4,2,16,1024]{3,2,1,0:T(8,128)(2,1)S(1)}, u32[]{:S(2)}, u32[]{:S(2)}) %collective-permute-start.9) | collective-permute-done | bytes 262176 | tf_op jit(solution)/shard_map/ppermute | solution.py:42
  35.5 0.0 copy-done.10
  35.5 0.7 copy-done.11
  36.2 0.3 collective-permute-done.8.x1
  36.5 0.0 copy-done.12
  36.5 0.0 copy-done.9
  36.5 2.4 %pick.1 = (bf16[2,2,16,1024]{3,2,1,0:T(8,128)(2,1)}, bf16[2,2,16,1024]{3,2,1,0:T(8,128)(2,1)}) custom-call(s32[1,2]{1,0:T(1,128)} %pair_ref.1, s32[1,2]{1,0:T(1,128)} %copy-done.12, bf16[4,2,16,1024]{3,2,1,0:T(8,128)(2,1)} %copy-done.9, bf16[4,2,16,1024]{3,2,1,0:T(8,128)(2,1)} %collective-permute-done.8.x1, bf16[4,2,16,1024]{3,2,1,0:T(8,128)(2,1)} %copy-done.11, ...), custom_call_target="tpu_custom_call" | custom-call | tf_op jit(solution)/shard_map/pick/pallas_call | solution.py:297
  38.9 0.1 collective-permute-start.12
  39.0 1.2 %slice.3 = s32[1]{0:T(128)} slice(s32[2]{0:T(128)} %time_ref.1), slice={[1:2]} | slice | bytes 8 | tf_op jit(solution)/shard_map/slice | solution.py:311
  40.9 0.0 collective-permute-done.11.l0
  40.9 0.0 collective-permute-done.12
  40.9 0.9 %add.3.p0 = bf16[2,2,16,1024]{3,2,1,0:T(8,128)(2,1)S(1)} add(bf16[2,2,16,1024]{3,2,1,0:T(8,128)(2,1)} %get-tuple-element.27, bf16[2,2,16,1024]{3,2,1,0:T(8,128)(2,1)S(1)} %collective-permute-done.12) | non-fusion elementwise | flops 65536 | bytes 393216 | tf_op jit(solution)/shard_map/add | solution.py:305
  41.9 3.3 %collective-permute-start.15 = (bf16[2,2,16,1024]{3,2,1,0:T(8,128)(2,1)S(1)}, bf16[2,2,16,1024]{3,2,1,0:T(8,128)(2,1)S(1)}, u32[]{:S(2)}, u32[]{:S(2)}) collective-permute-start(bf16[2,2,16,1024]{3,2,1,0:T(8,128)(2,1)S(1)} %add.3.p0), channel_id=1, source_target_pairs={{0,3},{1,0},{2,1},{3,2},{4,7},{5,4},{6,5},{7,6},{8,11},{9,8},{10,9... | collective-permute-start | bytes 393224 | tf_op jit(solution)/shard_map/ppermute | solution.py:42
  45.2 0.0 collective-permute-start.14
  45.2 1.0 %collective-permute-start.13 = (bf16[2,2,16,1024]{3,2,1,0:T(8,128)(2,1)S(1)}, bf16[2,2,16,1024]{3,2,1,0:T(8,128)(2,1)S(1)}, u32[]{:S(2)}, u32[]{:S(2)}) collective-permute-start(bf16[2,2,16,1024]{3,2,1,0:T(8,128)(2,1)S(1)} %add.3.p0), channel_id=1, source_target_pairs={{0,1},{1,2},{2,3},{3,0},{4,5},{5,6},{6,7},{7,4},{8,9},{9,10},{10,1... | collective-permute-start | bytes 393224 | tf_op jit(solution)/shard_map/ppermute | solution.py:42
  46.2 0.0 copy-done.2
  46.2 0.0 copy-done.6
  46.2 0.0 copy-done.5
  46.2 0.0 copy-done.4
  46.3 0.0 copy-start
  46.3 2.8 %copy-done = bf16[1024,3072]{1,0:T(8,128)(2,1)S(1)} copy-done((bf16[1024,3072]{1,0:T(8,128)(2,1)S(1)}, bf16[1024,3072]{1,0:T(8,128)(2,1)}, u32[]{:S(2)}) %copy-start) | copy-done | bytes 6291480
  49.0 1.2 %copy-done.3 = bf16[256,2048]{1,0:T(8,128)(2,1)S(1)} copy-done((bf16[256,2048]{1,0:T(8,128)(2,1)S(1)}, bf16[256,2048]{1,0:T(8,128)(2,1)}, u32[]{:S(2)}) %copy-start.3) | copy-done | bytes 1048600
  50.3 0.2 prelude.1
  50.5 3.6 %collective-permute-done.5.l1 = bf16[256,1024]{1,0:T(8,128)(2,1)} collective-permute-done((bf16[256,1024]{1,0:T(8,128)(2,1)}, bf16[256,1024]{1,0:T(8,128)(2,1)}, u32[]{:S(2)}, u32[]{:S(2)}) %collective-permute-start.5) | collective-permute-done | bytes 524320 | tf_op jit(solution)/shard_map/ppermute | solution.py:42
  54.1 3.2 %collective-permute-start.18 = (bf16[256,1024]{1,0:T(8,128)(2,1)}, bf16[256,1024]{1,0:T(8,128)(2,1)S(1)}, u32[]{:S(2)}, u32[]{:S(2)}) collective-permute-start(bf16[256,1024]{1,0:T(8,128)(2,1)} %collective-permute-done.5.l1), channel_id=1, source_target_pairs={{0,3},{1,0},{2,1},{3,2},{4,7},{5,4},{6,5},{7,6},{8,11},{9,8},{10,9... | collective-permute-start | bytes 1572872 | tf_op jit(solution)/shard_map/ppermute | solution.py:42
  57.3 0.0 collective-permute-start.17
  57.3 0.0 collective-permute-done.15.p3
  57.3 0.0 collective-permute-done.14.p2
  57.3 0.0 collective-permute-done.13.p1
  57.3 0.0 copy-done.1
  57.3 0.0 copy-done.7
  57.3 0.0 copy-done.8
  57.3 10.6 %first_keys.1 = (f32[16,256,128]{2,1,0:T(8,128)S(1)}, bf16[256,1024]{1,0:T(8,128)(2,1)S(1)}, f32[128,1024]{1,0:T(8,128)S(1)}, f32[128,1024]{1,0:T(8,128)S(1)}) custom-call(s32[2]{0:T(128)S(1)} %copy-done.8, bf16[256,1024]{1,0:T(8,128)(2,1)S(1)} %bitcast.25, bf16[256,1024]{1,0:T(8,128)(2,1)S(1)} %collective-permute-done.6.l1, ...), custom_call_target="tpu_custom_call" | custom-call | flops 4294967296 | bytes 8388608 | tf_op jit(solution)/shard_map/first_keys/pallas_call | solution.py:330
  68.0 1.8 %collective-permute-start.16 = (bf16[256,1024]{1,0:T(8,128)(2,1)}, bf16[256,1024]{1,0:T(8,128)(2,1)S(1)}, u32[]{:S(2)}, u32[]{:S(2)}) collective-permute-start(bf16[256,1024]{1,0:T(8,128)(2,1)} %collective-permute-done.5.l1), channel_id=1, source_target_pairs={{0,2},{1,3},{2,0},{3,1},{4,6},{5,7},{6,4},{7,5},{8,10},{9,11},{10,... | collective-permute-start | bytes 1572872 | tf_op jit(solution)/shard_map/ppermute | solution.py:42
  69.8 0.0 collective-permute-done.18.l3
  69.8 0.5 collective-permute-done.17.l2
  70.2 11.9 %middle_keys.1.acc_ref = f32[16,256,128]{2,1,0:T(8,128)S(1)} custom-call(bf16[256,1024]{1,0:T(8,128)(2,1)} %collective-permute-done.11.l0, bf16[256,1024]{1,0:T(8,128)(2,1)} %collective-permute-done.5.l1, bf16[256,1024]{1,0:T(8,128)(2,1)S(1)} %collective-permute-done.17.l2, bf16[256,1024]{1,0:T(8,128)(2,1)S(1)} %collective-permute-done.18.l3, ...), custom_call_target="tpu_custom_call" | custom-call | flops 4294967296 | bytes 8388608 | tf_op jit(solution)/shard_map/middle_keys/pallas_call | solution.py:344
  82.1 0.0 collective-permute-done.16.l0
  82.1 6.2 %last_keys.1 = bf16[256,1024]{1,0:T(8,128)(2,1)} custom-call(bf16[256,1024]{1,0:T(8,128)(2,1)S(1)} %bitcast.26, bf16[256,1024]{1,0:T(8,128)(2,1)S(1)} %collective-permute-done.16.l0, f32[128,1024]{1,0:T(8,128)S(1)} %get-tuple-element.35.first, f32[128,1024]{1,0:T(8,128)S(1)} %get-tuple-element.36.diff, f32[1,1024]{1,0:T(1,128)S(1)} %get-tuple-element.29.gain_ref, ...), custom_call_target="tpu_custom_call" | custom-call | flops 4294967296 | bytes 8388608 | tf_op jit(solution)/shard_map/last_keys/pallas_call | solution.py:356
  (11 shorter events, 0.1 us)
Async XLA Ops:
  0.0 46.2 %copy-start.2 = (bf16[1024,1024]{1,0:T(8,128)(2,1)S(1)}, bf16[1024,1024]{1,0:T(8,128)(2,1)}, u32[]{:S(2)}) copy-start(bf16[1024,1024]{1,0:T(8,128)(2,1)} %wo_ref.3) | copy-start | bytes 6291460
  0.0 46.2 %copy-start.6 = (f32[64]{0:T(128)S(1)}, f32[64]{0:T(128)}, u32[]{:S(2)}) copy-start(f32[64]{0:T(128)} %param.18) | copy-start | bytes 772
  0.0 46.2 %copy-start.5 = (f32[64]{0:T(128)S(1)}, f32[64]{0:T(128)}, u32[]{:S(2)}) copy-start(f32[64]{0:T(128)} %param.17) | copy-start | bytes 772
  0.0 46.2 %copy-start.4 = (f32[1024]{0:T(1024)S(1)}, f32[1024]{0:T(1024)}, u32[]{:S(2)}) copy-start(f32[1024]{0:T(1024)} %param.15) | copy-start | bytes 12292
  0.0 17.3 %collective-permute-start.7 = (bf16[256,1024]{1,0:T(8,128)(2,1)}, bf16[256,1024]{1,0:T(8,128)(2,1)S(1)}, u32[]{:S(2)}, u32[]{:S(2)}) collective-permute-start(bf16[256,1024]{1,0:T(8,128)(2,1)} %bitcast.21), channel_id=1, source_target_pairs={{0,3},{1,0},{2,1},{3,2},{4,7},{5,4},{6,5},{7,6},{8,11},{9,8},{10,9... | collective-permute-start | bytes 1572872 | tf_op jit(solution)/shard_map/ppermute | solution.py:42
  3.1 14.8 %collective-permute-start.6 = (bf16[256,1024]{1,0:T(8,128)(2,1)}, bf16[256,1024]{1,0:T(8,128)(2,1)S(1)}, u32[]{:S(2)}, u32[]{:S(2)}) collective-permute-start(bf16[256,1024]{1,0:T(8,128)(2,1)} %bitcast.22), channel_id=1, source_target_pairs={{0,1},{1,2},{2,3},{3,0},{4,5},{5,6},{6,7},{7,4},{8,9},{9,10},{10,1... | collective-permute-start | bytes 1572872 | tf_op jit(solution)/shard_map/ppermute | solution.py:42
  3.1 9.3 %collective-permute-start.1 = (bf16[16,1024]{1,0:T(8,128)(2,1)}, bf16[16,1024]{1,0:T(8,128)(2,1)S(1)}, u32[]{:S(2)}, u32[]{:S(2)}) collective-permute-start(bf16[16,1024]{1,0:T(8,128)(2,1)} %bitcast.30), channel_id=1, source_target_pairs={{0,4},{1,5},{2,6},{3,7},{4,0},{5,1},{6,2},{7,3},{8,12},{9,13},{10,... | collective-permute-start | bytes 98312 | tf_op jit(solution)/shard_map/ppermute | solution.py:42
  10.3 1.3 %collective-permute-start = (s32[1,2]{1,0:T(1,128)}, s32[1,2]{1,0:T(1,128)S(1)}, u32[]{:S(2)}, u32[]{:S(2)}) collective-permute-start(s32[1,2]{1,0:T(1,128)} %pair_ref.1), channel_id=1, source_target_pairs={{0,8},{1,9},{2,10},{3,11},{4,12},{5,13},{6,14},{7,15},{8,0},{9,1},... | collective-permute-start | bytes 32 | tf_op jit(solution)/shard_map/ppermute | solution.py:42
  11.6 25.0 %copy-start.12 = (s32[1,2]{1,0:T(1,128)}, s32[1,2]{1,0:T(1,128)S(1)}, u32[]{:S(2)}) copy-start(s32[1,2]{1,0:T(1,128)S(1)} %collective-permute-done.other_ref) | copy-start | bytes 28
  13.2 6.3 %collective-permute-start.4 = (bf16[2,16,1024]{2,1,0:T(8,128)(2,1)S(1)}, bf16[2,16,1024]{2,1,0:T(8,128)(2,1)S(1)}, u32[]{:S(2)}, u32[]{:S(2)}) collective-permute-start(bf16[2,16,1024]{2,1,0:T(8,128)(2,1)S(1)} %get-tuple-element.40), channel_id=1, source_target_pairs={{0,192},{1,193},{2,194},{3,195},{4,196},{5,197},{6,198},{7,199},{8... | collective-permute-start | bytes 196616 | tf_op jit(solution)/shard_map/ppermute | solution.py:42
  16.6 5.2 %collective-permute-start.3 = (bf16[2,16,1024]{2,1,0:T(8,128)(2,1)S(1)}, bf16[2,16,1024]{2,1,0:T(8,128)(2,1)S(1)}, u32[]{:S(2)}, u32[]{:S(2)}) collective-permute-start(bf16[2,16,1024]{2,1,0:T(8,128)(2,1)S(1)} %get-tuple-element.40), channel_id=1, source_target_pairs={{0,128},{1,129},{2,130},{3,131},{4,132},{5,133},{6,134},{7,135},{8... | collective-permute-start | bytes 196616 | tf_op jit(solution)/shard_map/ppermute | solution.py:42
  16.6 6.1 %collective-permute-start.2 = (bf16[2,16,1024]{2,1,0:T(8,128)(2,1)S(1)}, bf16[2,16,1024]{2,1,0:T(8,128)(2,1)S(1)}, u32[]{:S(2)}, u32[]{:S(2)}) collective-permute-start(bf16[2,16,1024]{2,1,0:T(8,128)(2,1)S(1)} %get-tuple-element.40), channel_id=1, source_target_pairs={{0,64},{1,65},{2,66},{3,67},{4,68},{5,69},{6,70},{7,71},{8,72},{9,... | collective-permute-start | bytes 196616 | tf_op jit(solution)/shard_map/ppermute | solution.py:42
  17.9 23.0 %collective-permute-start.11 = (bf16[256,1024]{1,0:T(8,128)(2,1)}, bf16[256,1024]{1,0:T(8,128)(2,1)}, u32[]{:S(2)}, u32[]{:S(2)}) collective-permute-start(bf16[256,1024]{1,0:T(8,128)(2,1)} %bitcast.23), channel_id=1, source_target_pairs={{0,2},{1,3},{2,0},{3,1},{4,6},{5,7},{6,4},{7,5},{8,10},{9,11},{10,... | collective-permute-start | bytes 1572872 | tf_op jit(solution)/shard_map/ppermute | solution.py:42
  22.7 13.8 %copy-start.9 = (bf16[4,2,16,1024]{3,2,1,0:T(8,128)(2,1)}, bf16[4,2,16,1024]{3,2,1,0:T(8,128)(2,1)S(1)}, u32[]{:S(2)}) copy-start(bf16[4,2,16,1024]{3,2,1,0:T(8,128)(2,1)S(1)} %pad_maximum_fusion.x0) | copy-start | bytes 786436
  22.7 10.0 %collective-permute-start.10 = (bf16[4,2,16,1024]{3,2,1,0:T(8,128)(2,1)S(1)}, bf16[4,2,16,1024]{3,2,1,0:T(8,128)(2,1)S(1)}, u32[]{:S(2)}, u32[]{:S(2)}) collective-permute-start(bf16[4,2,16,1024]{3,2,1,0:T(8,128)(2,1)S(1)} %pad_maximum_fusion.x0), channel_id=1, source_target_pairs={{0,48},{1,49},{2,50},{3,51},{4,52},{5,53},{6,54},{7,55},{8,56},{9,... | collective-permute-start | bytes 786440 | tf_op jit(solution)/shard_map/ppermute | solution.py:42
  23.4 12.2 %collective-permute-start.9 = (bf16[4,2,16,1024]{3,2,1,0:T(8,128)(2,1)S(1)}, bf16[4,2,16,1024]{3,2,1,0:T(8,128)(2,1)S(1)}, u32[]{:S(2)}, u32[]{:S(2)}) collective-permute-start(bf16[4,2,16,1024]{3,2,1,0:T(8,128)(2,1)S(1)} %pad_maximum_fusion.x0), channel_id=1, source_target_pairs={{0,32},{1,33},{2,34},{3,35},{4,36},{5,37},{6,38},{7,39},{8,40},{9,... | collective-permute-start | bytes 786440 | tf_op jit(solution)/shard_map/ppermute | solution.py:42
  25.8 10.8 %collective-permute-start.8 = (bf16[4,2,16,1024]{3,2,1,0:T(8,128)(2,1)S(1)}, bf16[4,2,16,1024]{3,2,1,0:T(8,128)(2,1)}, u32[]{:S(2)}, u32[]{:S(2)}) collective-permute-start(bf16[4,2,16,1024]{3,2,1,0:T(8,128)(2,1)S(1)} %pad_maximum_fusion.x0), channel_id=1, source_target_pairs={{0,16},{1,17},{2,18},{3,19},{4,20},{5,21},{6,22},{7,23},{8,24},{9,... | collective-permute-start | bytes 786440 | tf_op jit(solution)/shard_map/ppermute | solution.py:42
  27.6 26.6 %collective-permute-start.5 = (bf16[256,1024]{1,0:T(8,128)(2,1)}, bf16[256,1024]{1,0:T(8,128)(2,1)}, u32[]{:S(2)}, u32[]{:S(2)}) collective-permute-start(bf16[256,1024]{1,0:T(8,128)(2,1)} %bitcast.24), channel_id=1, source_target_pairs={{0,4},{1,5},{2,6},{3,7},{4,0},{5,1},{6,2},{7,3},{8,12},{9,13},{10,... | collective-permute-start | bytes 1572872 | tf_op jit(solution)/shard_map/ppermute | solution.py:42
  32.8 2.8 %copy-start.10 = (bf16[4,2,16,1024]{3,2,1,0:T(8,128)(2,1)}, bf16[4,2,16,1024]{3,2,1,0:T(8,128)(2,1)S(1)}, u32[]{:S(2)}) copy-start(bf16[4,2,16,1024]{3,2,1,0:T(8,128)(2,1)S(1)} %collective-permute-done.10.x3) | copy-start | bytes 786436
  35.5 0.7 copy-start.11
  38.9 2.0 %collective-permute-start.12 = (bf16[2,2,16,1024]{3,2,1,0:T(8,128)(2,1)}, bf16[2,2,16,1024]{3,2,1,0:T(8,128)(2,1)S(1)}, u32[]{:S(2)}, u32[]{:S(2)}) collective-permute-start(bf16[2,2,16,1024]{3,2,1,0:T(8,128)(2,1)} %get-tuple-element.28), channel_id=1, source_target_pairs={{0,8},{1,9},{2,10},{3,11},{4,12},{5,13},{6,14},{7,15},{8,0},{9,1},... | collective-permute-start | bytes 393224 | tf_op jit(solution)/shard_map/ppermute | solution.py:42
  41.9 15.4 %collective-permute-start.15 = (bf16[2,2,16,1024]{3,2,1,0:T(8,128)(2,1)S(1)}, bf16[2,2,16,1024]{3,2,1,0:T(8,128)(2,1)S(1)}, u32[]{:S(2)}, u32[]{:S(2)}) collective-permute-start(bf16[2,2,16,1024]{3,2,1,0:T(8,128)(2,1)S(1)} %add.3.p0), channel_id=1, source_target_pairs={{0,3},{1,0},{2,1},{3,2},{4,7},{5,4},{6,5},{7,6},{8,11},{9,8},{10,9... | collective-permute-start | bytes 393224 | tf_op jit(solution)/shard_map/ppermute | solution.py:42
  45.2 12.1 %collective-permute-start.14 = (bf16[2,2,16,1024]{3,2,1,0:T(8,128)(2,1)S(1)}, bf16[2,2,16,1024]{3,2,1,0:T(8,128)(2,1)S(1)}, u32[]{:S(2)}, u32[]{:S(2)}) collective-permute-start(bf16[2,2,16,1024]{3,2,1,0:T(8,128)(2,1)S(1)} %add.3.p0), channel_id=1, source_target_pairs={{0,2},{1,3},{2,0},{3,1},{4,6},{5,7},{6,4},{7,5},{8,10},{9,11},{10,... | collective-permute-start | bytes 393224 | tf_op jit(solution)/shard_map/ppermute | solution.py:42
  45.2 12.1 %collective-permute-start.13 = (bf16[2,2,16,1024]{3,2,1,0:T(8,128)(2,1)S(1)}, bf16[2,2,16,1024]{3,2,1,0:T(8,128)(2,1)S(1)}, u32[]{:S(2)}, u32[]{:S(2)}) collective-permute-start(bf16[2,2,16,1024]{3,2,1,0:T(8,128)(2,1)S(1)} %add.3.p0), channel_id=1, source_target_pairs={{0,1},{1,2},{2,3},{3,0},{4,5},{5,6},{6,7},{7,4},{8,9},{9,10},{10,1... | collective-permute-start | bytes 393224 | tf_op jit(solution)/shard_map/ppermute | solution.py:42
  46.3 2.8 %copy-start = (bf16[1024,3072]{1,0:T(8,128)(2,1)S(1)}, bf16[1024,3072]{1,0:T(8,128)(2,1)}, u32[]{:S(2)}) copy-start(bf16[1024,3072]{1,0:T(8,128)(2,1)} %w_ref.7) | copy-start | bytes 18874372
  49.0 1.2 %copy-start.3 = (bf16[256,2048]{1,0:T(8,128)(2,1)S(1)}, bf16[256,2048]{1,0:T(8,128)(2,1)}, u32[]{:S(2)}) copy-start(bf16[256,2048]{1,0:T(8,128)(2,1)} %mod_ref.1) | copy-start | bytes 3145732
  50.3 7.0 %copy-start.1 = (bf16[1024,3072]{1,0:T(8,128)(2,1)S(1)}, bf16[1024,3072]{1,0:T(8,128)(2,1)}, u32[]{:S(2)}) copy-start(bf16[1024,3072]{1,0:T(8,128)(2,1)} %w_ref.7) | copy-start | bytes 18874372
  50.3 7.1 %copy-start.7 = (bf16[1,2,128,1024]{3,2,1,0:T(8,128)(2,1)S(1)}, bf16[1,2,128,1024]{3,2,1,0:T(8,128)(2,1)}, u32[]{:S(2)}) copy-start(bf16[1,2,128,1024]{3,2,1,0:T(8,128)(2,1)} %param.10) | copy-start | bytes 1572868
  50.3 7.1 %copy-start.8 = (s32[2]{0:T(128)S(1)}, s32[2]{0:T(128)}, u32[]{:S(2)}) copy-start(s32[2]{0:T(128)} %time_ref.1) | copy-start | bytes 28
  54.1 15.6 %collective-permute-start.18 = (bf16[256,1024]{1,0:T(8,128)(2,1)}, bf16[256,1024]{1,0:T(8,128)(2,1)S(1)}, u32[]{:S(2)}, u32[]{:S(2)}) collective-permute-start(bf16[256,1024]{1,0:T(8,128)(2,1)} %collective-permute-done.5.l1), channel_id=1, source_target_pairs={{0,3},{1,0},{2,1},{3,2},{4,7},{5,4},{6,5},{7,6},{8,11},{9,8},{10,9... | collective-permute-start | bytes 1572872 | tf_op jit(solution)/shard_map/ppermute | solution.py:42
  57.3 12.9 %collective-permute-start.17 = (bf16[256,1024]{1,0:T(8,128)(2,1)}, bf16[256,1024]{1,0:T(8,128)(2,1)S(1)}, u32[]{:S(2)}, u32[]{:S(2)}) collective-permute-start(bf16[256,1024]{1,0:T(8,128)(2,1)} %collective-permute-done.5.l1), channel_id=1, source_target_pairs={{0,1},{1,2},{2,3},{3,0},{4,5},{5,6},{6,7},{7,4},{8,9},{9,10},{10,1... | collective-permute-start | bytes 1572872 | tf_op jit(solution)/shard_map/ppermute | solution.py:42
  68.0 14.1 %collective-permute-start.16 = (bf16[256,1024]{1,0:T(8,128)(2,1)}, bf16[256,1024]{1,0:T(8,128)(2,1)S(1)}, u32[]{:S(2)}, u32[]{:S(2)}) collective-permute-start(bf16[256,1024]{1,0:T(8,128)(2,1)} %collective-permute-done.5.l1), channel_id=1, source_target_pairs={{0,2},{1,3},{2,0},{3,1},{4,6},{5,7},{6,4},{7,5},{8,10},{9,11},{10,... | collective-permute-start | bytes 1572872 | tf_op jit(solution)/shard_map/ppermute | solution.py:42
